TPU v7x, 32 devices: a whole 2x2x4 slice. The times are simulated.
32 devices in a mesh: groups: 2 (over x), expert: 16 (over z, y, core).
Axes of the slice: x: 2, y: 2, z: 4, core: 2. Of those that a mesh axis runs over, the one named last changes fastest.
Arguments:
- tokens: bfloat16 [2048, 3072], P(('groups', 'expert')), parts along dimension 0, may hold values from -6 to 6
- cotangent: bfloat16 [2048, 3072], P(('groups', 'expert')), parts along dimension 0, may hold values from -6 to 6
- gate_weights: float32 [2048, 4], P(('groups', 'expert')), parts along dimension 0, may hold values from 0.1 to 1
- expert_ids: int32 [2048, 4], P(('groups', 'expert')), parts along dimension 0, may hold values from 0 to 15, as said below
- w_gate: bfloat16 [3072, 10752], P(None, 'expert'), may hold values from -0.109375 to 0.109375
- w_up: bfloat16 [3072, 10752], P(None, 'expert'), may hold values from -0.109375 to 0.109375
- w_down: bfloat16 [10752, 3072], P('expert'), may hold values from -0.078125 to 0.078125
Outputs:
- input_grad: bfloat16 [2048, 3072], P(('groups', 'expert')), parts along dimension 0
- gate_grad: float32 [2048, 4], P(('groups', 'expert')), parts along dimension 0
There are 2 independent parts, one for each index of `groups`. A program takes and returns all parts, laid end to end along the dimension named above; an argument that names none is the same for every part. Nothing has to cross between parts.
Inputs may be any that keep to these rules, and one draw needn't show every extreme that they name: `expert_ids`: each row names 4 different experts. Within each aligned block of 64 rows no expert below 2 is named by more than 12 rows, and one of them is named by exactly 12 rows.
All inputs are finite; a program needn't handle non-finite values.
Results may differ from a plain program's by a relative error of at most 0.0057.
Values may be sent and summed in bfloat16 or wider, within the bound.
No kernel may reach another device: no remote copies, remote signals or barrier semaphores. Data moves between devices by JAX's collectives and lax.ppermute only.
A program may use at most 128 MiB of HBM per device.

v0:
```python
import jax
import jax.numpy as jnp
from jax import lax
from jax.sharding import PartitionSpec as P

EXPERTS = 16
EXP_WIN = 2
CAP = 12


def shortened(x):

    def short(part):
        return part.astype(jnp.bfloat16) if part.dtype == jnp.float32 else part

    return jax.tree.map(short, x)


def shard_pass(expert_in, expert_grad, w_gate, w_up, w_down):
    gate_pre = jnp.dot(expert_in, w_gate, preferred_element_type=jnp.float32)
    up_proj = jnp.dot(expert_in, w_up, preferred_element_type=jnp.float32)
    sigmoid_gate = jax.nn.sigmoid(gate_pre)
    active = gate_pre * sigmoid_gate
    hidden = (active * up_proj).astype(jnp.bfloat16)
    expert_out = jnp.dot(hidden, w_down, preferred_element_type=jnp.float32)
    gate_score = jnp.sum(expert_grad.astype(jnp.float32) * expert_out, axis=1).astype(jnp.bfloat16)
    hidden_grad = jnp.dot(expert_grad, w_down.T, preferred_element_type=jnp.float32)
    slope = sigmoid_gate * (1.0 + gate_pre * (1.0 - sigmoid_gate))
    gate_back = (hidden_grad * up_proj * slope).astype(jnp.bfloat16)
    up_back = (hidden_grad * active).astype(jnp.bfloat16)
    summed = jnp.dot(gate_back, w_gate.T, preferred_element_type=jnp.float32) + jnp.dot(
        up_back, w_up.T, preferred_element_type=jnp.float32
    )
    return (summed.astype(jnp.bfloat16), gate_score)


def slot_numbers(expert_ids):
    tok_rows = expert_ids.shape[0]
    chosen = expert_ids[:, :, None] == jnp.arange(EXPERTS, dtype=jnp.int32)[None, None, :]
    per_token = jnp.sum(chosen.astype(jnp.float32), axis=1)
    earlier_mask = (jnp.arange(tok_rows)[:, None] > jnp.arange(tok_rows)[None, :]).astype(
        jnp.float32
    )
    earlier = jnp.dot(earlier_mask, per_token, preferred_element_type=jnp.float32).astype(jnp.int32)
    return jnp.sum(jnp.where(chosen, earlier[:, None, :], 0), axis=2)


def per_device(tokens, cotangent, gate_weights, expert_ids, w_gate, w_up, w_down):
    devices = lax.axis_size("expert")
    window = EXP_WIN
    split = devices // window
    model_width = tokens.shape[1]
    slot_index = slot_numbers(expert_ids)
    served = expert_ids < window
    position = expert_ids * CAP + slot_index
    slots_all = jnp.arange(window * CAP, dtype=jnp.int32)
    placed_on = jnp.any(position[:, :, None] == slots_all[None, None, :], axis=1).astype(
        jnp.bfloat16
    )
    joined = jnp.concatenate((tokens, cotangent), axis=1)
    outgoing = lax.dot_general(
        placed_on, joined, (((0,), (0,)), ((), ())), preferred_element_type=jnp.float32
    )
    outgoing = outgoing.astype(jnp.bfloat16).reshape(window, CAP, 2 * model_width)
    sending = jnp.repeat(outgoing, split, axis=0)
    received = lax.all_to_all(sending, "expert", split_axis=0, concat_axis=0, tiled=True)
    sources = received.shape[0]
    count = received.shape[1]
    flattened = received.reshape(-1, 2 * model_width)
    slot_grad, gate_score = shard_pass(
        flattened[:, :model_width], flattened[:, model_width:], w_gate, w_up, w_down
    )
    grad_back, score_back = lax.all_to_all(
        shortened(
            (slot_grad.reshape(sources, count, model_width), gate_score.reshape(sources, count))
        ),
        "expert",
        split_axis=0,
        concat_axis=0,
        tiled=True,
    )
    grad_total = jnp.sum(
        grad_back.reshape(window, split, CAP, model_width).astype(jnp.float32), axis=1
    ).reshape(window * CAP, model_width)
    score_total = jnp.sum(
        score_back.reshape(window, split, CAP).astype(jnp.float32), axis=1
    ).reshape(window * CAP)
    safe_position = jnp.where(served, position, 0)
    grad_rows = grad_total[safe_position]
    weighted = jnp.where(served[:, :, None], gate_weights[:, :, None] * grad_rows, 0.0)
    input_grad = jnp.sum(weighted, axis=1).astype(jnp.bfloat16)
    gate_grad = jnp.where(served, score_total[safe_position], 0.0)
    return (input_grad, gate_grad)


def solution(mesh):
    in_specs = (
        P(("groups", "expert"), None),
        P(("groups", "expert"), None),
        P(("groups", "expert"), None),
        P(("groups", "expert"), None),
        P(None, "expert"),
        P(None, "expert"),
        P("expert", None),
    )
    out_specs = (P(("groups", "expert"), None), P(("groups", "expert"), None))
    return jax.shard_map(
        per_device, mesh=mesh, in_specs=in_specs, out_specs=out_specs, check_vma=False
    )
```

profile of v0, /device:TPU:13, one launch (start us, length us, event | category | flops | bytes accessed | tf_op | source)
XLA Modules:
  0.0 156.8 jit_solution(10142861049371794935)
XLA Ops:
  0.6 0.7 convert_reduce_fusion.1
  1.3 0.1 convolution_convert_fusion.1
  1.5 0.7 select_reduce_fusion.1
  2.2 0.7 compare_select_fusion
  2.9 1.3 convolution_convert_fusion
  4.2 0.1 reshape.49
  4.3 0.3 broadcast_in_dim.51
  4.7 76.1 %all_to_all.16 = bf16[16,12,6144]{2,1,0:T(8,128)(2,1)S(1)} all-to-all(bf16[16,12,6144]{2,1,0:T(8,128)(2,1)S(1)} %bitcast.15), channel_id=1, replica_groups=mesh['groups'=2,'expert'=16] {'expert'}, dimensions={0} | all-to-all | bytes 4718592 | tf_op jit(solution)/shard_map/all_to_all | solution.py:66
  80.8 2.1 %reshape.51 = bf16[192,6144]{1,0:T(8,128)(2,1)} reshape(bf16[16,12,6144]{2,1,0:T(8,128)(2,1)S(1)} %all_to_all.16) | data formatting | bytes 4718592 | tf_op jit(solution)/shard_map/reshape | solution.py:69
  82.9 0.0 copy-start
  82.9 0.0 copy-start.3
  82.9 4.1 %fusion.2 = f32[192,672]{1,0:T(8,128)S(1)} fusion(bf16[3072,672]{0,1:T(8,128)(2,1)} %param.11, bf16[192,6144]{1,0:T(8,128)(2,1)} %reshape.51), kind=kOutput, calls=%fused_computation.10 | convolution fusion | flops 792723456 | bytes 5824512 | tf_op jit(solution)/shard_map/dot_general | solution.py:20
  87.1 0.0 copy-done
  87.1 0.3 copy-done.3
  87.4 0.0 copy-start.2
  87.4 1.5 fusion.4
  88.9 0.7 copy-done.2
  89.6 1.5 fusion.6
  91.0 1.3 fusion.1
  92.3 0.7 convert_element_type.75
  93.0 5.2 %all-to-all-start.2 = ((bf16[16,1,12]{2,1,0:T(2,128)(2,1)}), bf16[16,1,12]{2,1,0:T(2,128)(2,1)S(1)}, u32[]{:S(2)}, u32[]{:S(2)}) async-start(bf16[16,1,12]{2,1,0:T(2,128)(2,1)} %convert_element_type.75), calls=%async_computation.2 | async-start | bytes 16384 | tf_op jit(solution)/shard_map/all_to_all | solution.py:73
  98.2 0.0 copy-start.4
  98.2 3.5 %fusion.12 = f32[192,3072]{1,0:T(8,128)S(1)} fusion(bf16[3072,672]{0,1:T(8,128)(2,1)} %param.11, f32[192,672]{1,0:T(8,128)S(1)} %fusion.2, f32[192,672]{1,0:T(8,128)S(1)} %fusion.6, f32[192,672]{1,0:T(8,128)S(1)} %fusion.4), kind=kOutput, calls=%fused_computation.24 | convolution fusion | flops 794013696 | bytes 8036352 | tf_op jit(solution)/shard_map/dot_general | solution.py:31
  101.7 0.0 copy-done.4
  101.7 1.2 fusion
  102.9 0.0 copy-start.1
  102.9 1.3 reshape.52
  104.2 0.0 all-to-all-done.2
  104.2 6.0 %all-to-all-start.1 = ((bf16[16,12,3072]{2,1,0:T(8,128)(2,1)}), bf16[16,12,3072]{2,1,0:T(8,128)(2,1)S(1)}, u32[]{:S(2)}, u32[]{:S(2)}) async-start(bf16[16,12,3072]{2,1,0:T(8,128)(2,1)} %reshape.52), calls=%async_computation.1 | async-start | bytes 3145728 | tf_op jit(solution)/shard_map/all_to_all | solution.py:73
  110.3 0.1 copy.29
  110.4 0.1 copy.31
  110.5 0.1 reshape.59
  110.6 0.0 copy-done.1
  110.6 0.1 copy.30
  110.7 0.1 reshape.54
  110.8 1.9 %gather_fusion.1 = f32[256]{0:T(256)S(1)} fusion(f32[24]{0:T(128)S(1)} %reshape.54, s32[1024]{0:T(1024)S(1)} %pad_clamp_fusion), kind=kCustom, calls=%fused_computation.1 | custom fusion | bytes 3072 | tf_op jit(solution)/shard_map/gather | solution.py:92
  112.7 0.1 reshape.66
  112.8 0.1 copy.33
  112.9 0.6 broadcast_select_fusion
  113.5 33.0 %all-to-all-done.1 = bf16[16,12,3072]{2,1,0:T(8,128)(2,1)S(1)} async-done(((bf16[16,12,3072]{2,1,0:T(8,128)(2,1)}), bf16[16,12,3072]{2,1,0:T(8,128)(2,1)S(1)}, u32[]{:S(2)}, u32[]{:S(2)}) %all-to-all-start.1) | async-done | bytes 1179680 | tf_op jit(solution)/shard_map/all_to_all | solution.py:73
  146.4 0.3 convert_reduce_fusion
  146.7 3.3 %gather_fusion = f32[256,3072]{1,0:T(8,128)} fusion(f32[24,3072]{1,0:T(8,128)S(1)} %reshape.53, s32[1024]{0:T(1024)S(1)} %pad_clamp_fusion), kind=kCustom, calls=%fused_computation | custom fusion | bytes 6292480 | tf_op jit(solution)/shard_map/gather | solution.py:89
  150.1 3.1 %reshape.58 = f32[64,4,3072]{2,1,0:T(4,128)S(1)} reshape(f32[256,3072]{1,0:T(8,128)} %gather_fusion) | data formatting | bytes 6291456 | tf_op jit(solution)/shard_map/gather | solution.py:89
  153.2 3.6 %select_reduce_fusion = bf16[64,3072]{1,0:T(8,128)(2,1)} fusion(f32[64,4,3072]{2,1,0:T(4,128)S(1)} %reshape.58, f32[64,4]{1,0:T(8,128)S(1)} %copy.30, pred[64,4]{1,0:T(8,128)(4,1)S(1)} %copy.29), kind=kLoop, calls=%fused_computation.7 | loop fusion | flops 2162688 | bytes 3540224 | tf_op jit(solution)/shard_map/reduce_sum | solution.py:91
  (5 shorter events, 0.1 us)
Async XLA Ops:
  82.9 4.1 %copy-start = (bf16[192,6144]{1,0:T(8,128)(2,1)S(1)}, bf16[192,6144]{1,0:T(8,128)(2,1)}, u32[]{:S(2)}) copy-start(bf16[192,6144]{1,0:T(8,128)(2,1)} %reshape.51) | copy-start | bytes 7077892
  82.9 4.5 %copy-start.3 = (bf16[3072,672]{0,1:T(8,128)(2,1)S(1)}, bf16[3072,672]{0,1:T(8,128)(2,1)}, u32[]{:S(2)}) copy-start(bf16[3072,672]{0,1:T(8,128)(2,1)} %param.12) | copy-start | bytes 12386308
  87.4 2.2 %copy-start.2 = (bf16[672,3072]{1,0:T(8,128)(2,1)S(1)}, bf16[672,3072]{1,0:T(8,128)(2,1)}, u32[]{:S(2)}) copy-start(bf16[672,3072]{1,0:T(8,128)(2,1)} %param.13) | copy-start | bytes 12386308
  93.0 11.2 %all-to-all-start.2 = ((bf16[16,1,12]{2,1,0:T(2,128)(2,1)}), bf16[16,1,12]{2,1,0:T(2,128)(2,1)S(1)}, u32[]{:S(2)}, u32[]{:S(2)}) async-start(bf16[16,1,12]{2,1,0:T(2,128)(2,1)} %convert_element_type.75), calls=%async_computation.2 | async-start | bytes 16384 | tf_op jit(solution)/shard_map/all_to_all | solution.py:73
  98.2 3.5 %copy-start.4 = (bf16[3072,672]{0,1:T(8,128)(2,1)S(1)}, bf16[3072,672]{0,1:T(8,128)(2,1)}, u32[]{:S(2)}) copy-start(bf16[3072,672]{0,1:T(8,128)(2,1)} %param.12) | copy-start | bytes 12386308
  102.9 7.7 %copy-start.1 = (f32[64,4]{0,1:T(4,128)S(1)}, f32[64,4]{0,1:T(4,128)}, u32[]{:S(2)}) copy-start(f32[64,4]{0,1:T(4,128)} %param.9) | copy-start | bytes 3076
  104.2 42.2 %all-to-all-start.1 = ((bf16[16,12,3072]{2,1,0:T(8,128)(2,1)}), bf16[16,12,3072]{2,1,0:T(8,128)(2,1)S(1)}, u32[]{:S(2)}, u32[]{:S(2)}) async-start(bf16[16,12,3072]{2,1,0:T(8,128)(2,1)} %reshape.52), calls=%async_computation.1 | async-start | bytes 3145728 | tf_op jit(solution)/shard_map/all_to_all | solution.py:73
where the time goes:
time: 157 us
  blocking collectives  76.1 us (48%)
  waiting for transfers between devices  33 us (21%)
  local copies, waits for them, and re-layouts  14.6 us (9%)
  matrix products  14.4 us (9%)
  starting transfers between devices  11.2 us (7%)
  other arithmetic  6.62 us (4%)
    all_to_all x1, blocking collectives, per_device(): lax.all_to_all(sending, 'expert', split_axis=0, concat_axis=0, tiled=True)  76.1 us
    all_to_all x2, waiting for transfers between devices, per_device(): lax.all_to_all(shortened((slot_grad.reshape(sources, count, model_width),...  33 us
    all_to_all x2, starting transfers between devices, per_device(): lax.all_to_all(shortened((slot_grad.reshape(sources, count, model_width),...  11.2 us
    gather x2, local copies, waits for them, and re-layouts, per_device(): grad_rows = grad_total[safe_position]  6.44 us
    dot_general x1, matrix products, shard_pass(): gate_pre = jnp.dot(expert_in, w_gate, preferred_element_type=jnp.float32)  4.12 us
    reduce_sum x1, other arithmetic, per_device(): input_grad = jnp.sum(weighted, axis=1).astype(jnp.bfloat16)  3.62 us
    dot_general x1, matrix products, shard_pass(): jnp.dot(gate_back, w_gate.T, preferred_element_type=jnp.float32)  3.48 us
  transfers between devices with their start and end apart: 2, of which 1 were waited for; matrix products, arithmetic and copies ran while one was open for 6% of the time, Pallas kernels for 0%

commit v1 on v0

v1 whole, which is shorter than its diff:
```python
import functools

import jax
import jax.numpy as jnp
from jax import lax
from jax.experimental import pallas as pl
from jax.experimental.pallas import tpu as pltpu
from jax.sharding import PartitionSpec as P

EXP_WIN = 2
CAP = 12
PAIR = 2 * CAP
LANES = 128
COLS = 512
F32 = jnp.float32
BF16 = jnp.bfloat16
EXACT = lax.Precision.HIGHEST
VMEM = pl.BlockSpec(memory_space=pltpu.VMEM)
SMEM = pl.BlockSpec(memory_space=pltpu.SMEM)


def call(kernel, name, out_shape, in_specs, args, scratch=(), flops=0, limit=16):
    moved = sum(a.size * a.dtype.itemsize for a in args)
    moved += sum(o.size * o.dtype.itemsize for o in out_shape)
    return pl.pallas_call(
        kernel,
        name=name,
        out_shape=out_shape,
        in_specs=in_specs,
        out_specs=[VMEM] * len(out_shape),
        scratch_shapes=list(scratch),
        compiler_params=pltpu.CompilerParams(vmem_limit_bytes=limit << 20),
        cost_estimate=pl.CostEstimate(flops=flops, bytes_accessed=moved, transcendentals=0),
    )(*args)


def struct(shape, dtype):
    return jax.ShapeDtypeStruct(shape, dtype)


def pick_kernel(mine_ref, ids_ref, gates_ref, tok_ref, cot_ref, own_ref, other_ref, place_ref, weight_ref):
    rows = 2 * PAIR
    count = ids_ref.shape[1]
    row = lax.broadcasted_iota(jnp.int32, (rows, count), 0)
    mine = mine_ref[0]
    expert = jnp.where(row < PAIR, mine, EXP_WIN - 1 - mine)
    named = jnp.zeros((rows, count), F32)
    weight = jnp.zeros((rows, count), F32)
    for k in range(ids_ref.shape[0]):
        same = ids_ref[k : k + 1, :] == expert
        named = named + jnp.where(same, 1.0, 0.0)
        weight = weight + jnp.where(same, gates_ref[k : k + 1, :], 0.0)
    before = jnp.where(
        lax.broadcasted_iota(jnp.int32, (count, count), 0)
        < lax.broadcasted_iota(jnp.int32, (count, count), 1),
        1.0,
        0.0,
    )
    slot = jnp.dot(named, before, preferred_element_type=F32)
    taken = sum((row >= CAP * i).astype(jnp.int32) for i in range(1, 4))
    want = (row - CAP * taken).astype(F32)
    place = jnp.where((slot == want) & (named > 0.5), 1.0, 0.0)
    first = (taken == 0) | (taken == 2)
    from_tok = jnp.where(first, place, 0.0).astype(BF16)
    from_cot = jnp.where(first, 0.0, place).astype(BF16)
    picked = jnp.dot(from_tok, tok_ref[...], preferred_element_type=F32)
    picked = picked + jnp.dot(from_cot, cot_ref[...], preferred_element_type=F32)
    own_ref[...] = picked[:PAIR].astype(BF16)
    other_ref[...] = picked[PAIR:].astype(BF16)
    place_ref[...] = place
    weight_ref[...] = place * weight


def nt(a, b):
    return lax.dot_general(a, b, (((1,), (1,)), ((), ())), preferred_element_type=F32)


def shard_kernel(blocks, *refs):
    block_refs = refs[:blocks]
    wg_ref, wu_ref, wd_ref, keep_ref, send_ref, g_ref, u_ref, dh_ref, dg_ref, du_ref = refs[blocks:]
    width = wg_ref.shape[1]
    half = width // 2
    g_ref[...] = jnp.zeros_like(g_ref)
    u_ref[...] = jnp.zeros_like(u_ref)
    dh_ref[...] = jnp.zeros_like(dh_ref)

    def forward(step, carry):
        cols = pl.ds(pl.multiple_of(step * COLS, COLS), COLS)
        parts = [ref[:, cols].astype(F32) for ref in block_refs]
        tok = jnp.concatenate([p[:CAP] for p in parts], axis=0).astype(BF16)
        cot = jnp.concatenate([p[CAP:] for p in parts], axis=0).astype(BF16)
        g_ref[...] += nt(tok, wg_ref[:, cols])
        u_ref[...] += nt(tok, wu_ref[:, cols])
        dh_ref[...] += nt(cot, wd_ref[:, cols])
        return carry

    lax.fori_loop(0, width // COLS, forward, 0)
    g = g_ref[...]
    u = u_ref[...]
    dh = dh_ref[...]
    sig = jax.nn.sigmoid(g)
    act = g * sig
    hidden = (act * u).astype(BF16).astype(F32)
    score = jnp.sum(hidden * dh, axis=1, keepdims=True)
    dg_ref[...] = (dh * u * (sig * (1.0 + g * (1.0 - sig)))).astype(BF16)
    du_ref[...] = (dh * act).astype(BF16)
    rows = keep_ref.shape[0]

    def spread(left, right):
        pieces = []
        for b in range(blocks):
            pieces += [left[CAP * b : CAP * b + CAP], right[CAP * b : CAP * b + CAP]]
        return jnp.concatenate(pieces, axis=0)

    def backward(step, carry):
        halves = []
        for base in (0, half):
            cols = pl.ds(pl.multiple_of(base + step * COLS, COLS), COLS)
            halves.append(
                jnp.dot(dg_ref[...], wg_ref[:, cols], preferred_element_type=F32)
                + jnp.dot(du_ref[...], wu_ref[:, cols], preferred_element_type=F32)
            )
        out = spread(*halves).astype(BF16)
        to = pl.ds(pl.multiple_of(step * COLS, COLS), COLS)
        keep_ref[:, to] = out[:rows]
        send_ref[:, to] = out[rows:]
        return carry

    lax.fori_loop(0, half // COLS, backward, 0)
    score = jnp.broadcast_to(score, (score.shape[0], LANES))
    tail = two_lanes(spread(score, jnp.zeros_like(score))).astype(BF16)
    keep_ref[:, half:] = tail[:rows]
    send_ref[:, half:] = tail[rows:]


def two_lanes(total):
    high = total.astype(BF16).astype(F32)
    lane = lax.broadcasted_iota(jnp.int32, total.shape, 1)
    return jnp.where(lane == 0, high, jnp.where(lane == 1, total - high, 0.0))


def packed(total):
    half = total.shape[1] - LANES
    tail = total[:, half:]
    tail = jnp.broadcast_to(tail[:, 0:1] + tail[:, 1:2], tail.shape)
    return jnp.concatenate([total[:, :half], two_lanes(tail)], axis=1).astype(BF16)


def chip_kernel(keep_ref, got_ref, self_ref, *out_refs):
    total = keep_ref[...].astype(F32) + got_ref[...].astype(F32)
    self_ref[...] = total[:PAIR]
    for i, ref in enumerate(out_refs):
        ref[...] = packed(total[PAIR * (i + 1) : PAIR * (i + 2)])


def total_of(refs):
    total = refs[0][...].astype(F32)
    for ref in refs[1:]:
        total = total + ref[...].astype(F32)
    return total


def other_kernel(*refs):
    refs[-1][...] = packed(total_of(refs[:-1]))


def final_kernel(sources, mine_ref, ids_ref, place_ref, weight_ref, back_ref, *refs):
    own = total_of(refs[:sources])
    grad_ref, gate_ref = refs[sources:]
    other = back_ref[...].astype(F32)
    both = jnp.concatenate([own, other], axis=0)
    half = both.shape[1] - LANES
    rows, count = place_ref.shape
    eye = jnp.where(
        lax.broadcasted_iota(jnp.int32, (count, count), 0)
        == lax.broadcasted_iota(jnp.int32, (count, count), 1),
        1.0,
        0.0,
    )
    weight = lax.dot_general(
        eye, weight_ref[...], (((1,), (1,)), ((), ())), precision=EXACT, preferred_element_type=F32
    )
    lane = lax.broadcasted_iota(jnp.int32, weight.shape, 1)
    first = (lane < CAP) | ((lane >= PAIR) & (lane < PAIR + CAP))
    for i in range(2):
        part = jnp.where(first == (i == 0), weight, 0.0)
        out = jnp.dot(part, both[:, :half], precision=EXACT, preferred_element_type=F32)
        grad_ref[:, half * i : half * (i + 1)] = out.astype(BF16)
    tail = both[:, half:]
    score = (tail[:, 0:1] + tail[:, 1:2]) * place_ref[...]
    mine = mine_ref[0]
    ids = ids_ref[...]
    own_score = jnp.sum(score[:PAIR], axis=0, keepdims=True)
    other_score = jnp.sum(score[PAIR:], axis=0, keepdims=True)
    gate_ref[...] = jnp.where(ids == mine, own_score, 0.0) + jnp.where(
        ids == EXP_WIN - 1 - mine, other_score, 0.0
    )


def per_device(tokens, cotangent, gate_weights, expert_ids, w_gate, w_up, w_down):
    devices = lax.axis_size("expert")
    split = devices // EXP_WIN
    evens = range(2, split, 2)
    width = tokens.shape[1]
    units = w_down.shape[0]
    count = tokens.shape[0]
    wide = width // 2 + LANES
    mine = (lax.axis_index("expert") // split).astype(jnp.int32).reshape(1)
    ids = expert_ids.T
    gates = gate_weights.T
    weights = (w_gate.T, w_up.T, w_down)

    def swap(x, offset):
        return lax.ppermute(x, "expert", [(i, i ^ offset) for i in range(devices)])

    own, other, place, weight = call(
        pick_kernel,
        "pick",
        [struct((PAIR, width), BF16)] * 2 + [struct((2 * PAIR, count), F32)] * 2,
        [SMEM] + [VMEM] * 4,
        (mine, ids, gates, tokens, cotangent),
        flops=4 * 2 * PAIR * count * width,
    )

    def spread_rows(block):
        return [block] + [swap(block, k) for k in evens]

    def shard(blocks):
        blocks = blocks + [swap(b, 1) for b in blocks]
        m = len(blocks) * CAP
        return call(
            functools.partial(shard_kernel, len(blocks)),
            "shard",
            [struct((m, wide), BF16)] * 2,
            [VMEM] * (len(blocks) + 3),
            (*blocks, *weights),
            [pltpu.VMEM((m, units), F32)] * 3 + [pltpu.VMEM((m, units), BF16)] * 2,
            flops=10 * m * width * units,
        )

    def chip_sums(keep, send):
        got = swap(send, 1)
        return call(
            chip_kernel,
            "chip",
            [struct((PAIR, wide), F32)] + [struct((PAIR, wide), BF16)] * len(evens),
            [VMEM] * 2,
            (keep, got),
        )

    def returned(sums):
        return [sums[0]] + [swap(s, k) for s, k in zip(sums[1:], evens)]

    crossed = swap(other, split)
    own_blocks = spread_rows(own)
    cross_blocks = spread_rows(crossed)
    own_back = returned(chip_sums(*shard(own_blocks)))
    cross_back = returned(chip_sums(*shard(cross_blocks)))
    (cross_total,) = call(
        other_kernel, "other", [struct((PAIR, wide), BF16)], [VMEM] * len(cross_back), tuple(cross_back)
    )
    back = swap(cross_total, split)
    grad, gate_grad = call(
        functools.partial(final_kernel, len(own_back)),
        "final",
        [struct((count, width), BF16), struct(ids.shape, F32)],
        [SMEM] + [VMEM] * (4 + len(own_back)),
        (mine, ids, place, weight, back, *own_back),
    )
    return (grad, gate_grad.T)


def solution(mesh):
    rows = P(("groups", "expert"), None)
    return jax.shard_map(
        per_device,
        mesh=mesh,
        in_specs=(rows, rows, rows, rows, P(None, "expert"), P(None, "expert"), P("expert", None)),
        out_specs=(rows, rows),
        check_vma=False,
    )
```

time: 157 us -> 67.6 us (0.43)
  the two profiles are of different devices: /device:TPU:13 before, /device:TPU:0 now
where the time goes in v1:
time: 67.6 us; the launch traced here: 67.3 us
  starting transfers between devices  24.1 us (36%)
  waiting for transfers between devices  16.6 us (25%)
  Pallas kernels  15.9 us (24%)
  local copies, waits for them, and re-layouts  9.87 us (15%)
  between operations  0.76 us (1%)
    ppermute x24, starting transfers between devices, swap(): return lax.ppermute(x, 'expert', [(i, i ^ offset) for i in range(devices)])  24.1 us
    ppermute x24, waiting for transfers between devices, swap(): return lax.ppermute(x, 'expert', [(i, i ^ offset) for i in range(devices)])  16.6 us
    pallas_call x7, Pallas kernels, call(): pl.pallas_call(kernel, name=name, out_shape=out_shape, in_specs=in_specs,...  15.9 us
    unnamed x22, local copies, waits for them, and re-layouts  9.87 us
  transfers between devices with their start and end apart: 24, of which 8 were waited for; matrix products, arithmetic and copies ran while one was open for 0% of the time, Pallas kernels for 21%

profile of v1, /device:TPU:0, one launch (start us, length us, event | category | flops | bytes accessed | tf_op | source)
XLA Modules:
  0.0 67.3 jit_solution(17415703427101368351)
XLA Ops:
  0.7 1.0 %copy-done.6 = bf16[64,3072]{1,0:T(8,128)(2,1)S(1)} copy-done((bf16[64,3072]{1,0:T(8,128)(2,1)S(1)}, bf16[64,3072]{1,0:T(8,128)(2,1)}, u32[]{:S(2)}) %copy-start.6) | copy-done | bytes 393240
  1.6 1.0 %copy-done.7 = bf16[64,3072]{1,0:T(8,128)(2,1)S(1)} copy-done((bf16[64,3072]{1,0:T(8,128)(2,1)S(1)}, bf16[64,3072]{1,0:T(8,128)(2,1)}, u32[]{:S(2)}) %copy-start.7) | copy-done | bytes 393240
  2.6 0.7 %copy-done.8 = s32[64,4]{0,1:T(4,128)S(1)} copy-done((s32[64,4]{0,1:T(4,128)S(1)}, s32[64,4]{0,1:T(4,128)}, u32[]{:S(2)}) %copy-start.8) | copy-done | bytes 1048
  3.3 0.7 %copy-done.10 = f32[64,4]{0,1:T(4,128)S(1)} copy-done((f32[64,4]{0,1:T(4,128)S(1)}, f32[64,4]{0,1:T(4,128)}, u32[]{:S(2)}) %copy-start.10) | copy-done | bytes 1048
  4.0 0.4 pick.1
  4.4 4.1 %collective-permute-start = (bf16[24,3072]{1,0:T(8,128)(2,1)S(1)}, bf16[24,3072]{1,0:T(8,128)(2,1)S(1)}, u32[]{:S(2)}, u32[]{:S(2)}) collective-permute-start(bf16[24,3072]{1,0:T(8,128)(2,1)S(1)} %get-tuple-element.22), channel_id=1, source_target_pairs={{0,8},{1,9},{2,10},{3,11},{4,12},{5,13},{6,14},{7,15},{8,0},{9,1},... | collective-permute-start | bytes 442376 | tf_op jit(solution)/shard_map/ppermute | solution.py:214
  8.5 1.5 %collective-permute-start.13 = (bf16[24,3072]{1,0:T(8,128)(2,1)S(1)}, bf16[24,3072]{1,0:T(8,128)(2,1)S(1)}, u32[]{:S(2)}, u32[]{:S(2)}) collective-permute-start(bf16[24,3072]{1,0:T(8,128)(2,1)S(1)} %get-tuple-element.29.refs_0_), channel_id=1, source_target_pairs={{0,2},{1,3},{2,0},{3,1},{4,6},{5,7},{6,4},{7,5},{8,10},{9,11},{10,... | collective-permute-start | bytes 442376 | tf_op jit(solution)/shard_map/ppermute | solution.py:214
  10.1 1.6 %collective-permute-start.14 = (bf16[24,3072]{1,0:T(8,128)(2,1)S(1)}, bf16[24,3072]{1,0:T(8,128)(2,1)S(1)}, u32[]{:S(2)}, u32[]{:S(2)}) collective-permute-start(bf16[24,3072]{1,0:T(8,128)(2,1)S(1)} %get-tuple-element.29.refs_0_), channel_id=1, source_target_pairs={{0,4},{1,5},{2,6},{3,7},{4,0},{5,1},{6,2},{7,3},{8,12},{9,13},{10,... | collective-permute-start | bytes 442376 | tf_op jit(solution)/shard_map/ppermute | solution.py:214
  11.6 4.0 %collective-permute-done.refs_0_ = bf16[24,3072]{1,0:T(8,128)(2,1)S(1)} collective-permute-done((bf16[24,3072]{1,0:T(8,128)(2,1)S(1)}, bf16[24,3072]{1,0:T(8,128)(2,1)S(1)}, u32[]{:S(2)}, u32[]{:S(2)}) %collective-permute-start) | collective-permute-done | bytes 147488 | tf_op jit(solution)/shard_map/ppermute | solution.py:214
  15.6 1.6 %collective-permute-start.1 = (bf16[24,3072]{1,0:T(8,128)(2,1)S(1)}, bf16[24,3072]{1,0:T(8,128)(2,1)S(1)}, u32[]{:S(2)}, u32[]{:S(2)}) collective-permute-start(bf16[24,3072]{1,0:T(8,128)(2,1)S(1)} %collective-permute-done.refs_0_), channel_id=1, source_target_pairs={{0,2},{1,3},{2,0},{3,1},{4,6},{5,7},{6,4},{7,5},{8,10},{9,11},{10,... | collective-permute-start | bytes 442376 | tf_op jit(solution)/shard_map/ppermute | solution.py:214
  17.2 0.6 collective-permute-start.2
  17.8 1.3 %collective-permute-start.3 = (bf16[24,3072]{1,0:T(8,128)(2,1)S(1)}, bf16[24,3072]{1,0:T(8,128)(2,1)S(1)}, u32[]{:S(2)}, u32[]{:S(2)}) collective-permute-start(bf16[24,3072]{1,0:T(8,128)(2,1)S(1)} %collective-permute-done.refs_0_), channel_id=1, source_target_pairs={{0,6},{1,7},{2,4},{3,5},{4,2},{5,3},{6,0},{7,1},{8,14},{9,15},{10,... | collective-permute-start | bytes 442376 | tf_op jit(solution)/shard_map/ppermute | solution.py:214
  19.1 1.6 %collective-permute-start.15 = (bf16[24,3072]{1,0:T(8,128)(2,1)S(1)}, bf16[24,3072]{1,0:T(8,128)(2,1)S(1)}, u32[]{:S(2)}, u32[]{:S(2)}) collective-permute-start(bf16[24,3072]{1,0:T(8,128)(2,1)S(1)} %get-tuple-element.29.refs_0_), channel_id=1, source_target_pairs={{0,6},{1,7},{2,4},{3,5},{4,2},{5,3},{6,0},{7,1},{8,14},{9,15},{10,... | collective-permute-start | bytes 442376 | tf_op jit(solution)/shard_map/ppermute | solution.py:214
  20.7 0.9 %collective-permute-done.1.refs_1_ = bf16[24,3072]{1,0:T(8,128)(2,1)S(1)} collective-permute-done((bf16[24,3072]{1,0:T(8,128)(2,1)S(1)}, bf16[24,3072]{1,0:T(8,128)(2,1)S(1)}, u32[]{:S(2)}, u32[]{:S(2)}) %collective-permute-start.1) | collective-permute-done | bytes 147488 | tf_op jit(solution)/shard_map/ppermute | solution.py:214
  21.6 2.4 %collective-permute-done.2.refs_2_ = bf16[24,3072]{1,0:T(8,128)(2,1)S(1)} collective-permute-done((bf16[24,3072]{1,0:T(8,128)(2,1)S(1)}, bf16[24,3072]{1,0:T(8,128)(2,1)S(1)}, u32[]{:S(2)}, u32[]{:S(2)}) %collective-permute-start.2) | collective-permute-done | bytes 147488 | tf_op jit(solution)/shard_map/ppermute | solution.py:214
  24.0 0.0 collective-permute-start.6
  24.0 2.9 %collective-permute-done.3.refs_3_ = bf16[24,3072]{1,0:T(8,128)(2,1)S(1)} collective-permute-done((bf16[24,3072]{1,0:T(8,128)(2,1)S(1)}, bf16[24,3072]{1,0:T(8,128)(2,1)S(1)}, u32[]{:S(2)}, u32[]{:S(2)}) %collective-permute-start.3) | collective-permute-done | bytes 147488 | tf_op jit(solution)/shard_map/ppermute | solution.py:214
  26.9 0.0 collective-permute-start.7
  26.9 1.6 %collective-permute-done.15.refs_3_ = bf16[24,3072]{1,0:T(8,128)(2,1)S(1)} collective-permute-done((bf16[24,3072]{1,0:T(8,128)(2,1)S(1)}, bf16[24,3072]{1,0:T(8,128)(2,1)S(1)}, u32[]{:S(2)}, u32[]{:S(2)}) %collective-permute-start.15) | collective-permute-done | bytes 147488 | tf_op jit(solution)/shard_map/ppermute | solution.py:214
  28.6 0.0 collective-permute-start.16
  28.6 0.5 collective-permute-start.17
  29.1 0.1 collective-permute-start.18
  29.2 0.0 collective-permute-done.6.refs_6_
  29.2 0.4 collective-permute-start.19
  29.6 2.2 %copy-done = bf16[3072,672]{0,1:T(8,128)(2,1)S(1)} copy-done((bf16[3072,672]{0,1:T(8,128)(2,1)S(1)}, bf16[3072,672]{0,1:T(8,128)(2,1)}, u32[]{:S(2)}) %copy-start) | copy-done | bytes 4128792
  31.8 2.2 %copy-done.2 = bf16[3072,672]{0,1:T(8,128)(2,1)S(1)} copy-done((bf16[3072,672]{0,1:T(8,128)(2,1)S(1)}, bf16[3072,672]{0,1:T(8,128)(2,1)}, u32[]{:S(2)}) %copy-start.2) | copy-done | bytes 4128792
  33.9 2.2 %copy-done.4 = bf16[672,3072]{1,0:T(8,128)(2,1)S(1)} copy-done((bf16[672,3072]{1,0:T(8,128)(2,1)S(1)}, bf16[672,3072]{1,0:T(8,128)(2,1)}, u32[]{:S(2)}) %copy-start.4) | copy-done | bytes 4128792
  36.1 6.7 %shard.2 = (bf16[96,1664]{1,0:T(8,128)(2,1)S(1)}, bf16[96,1664]{1,0:T(8,128)(2,1)S(1)}) custom-call(bf16[24,3072]{1,0:T(8,128)(2,1)S(1)} %collective-permute-done.refs_0_, bf16[24,3072]{1,0:T(8,128)(2,1)S(1)} %collective-permute-done.1.refs_1_, bf16[24,3072]{1,0:T(8,128)(2,1)S(1)} %collective-permute-done.2.refs_2_, ...), custom_call_target="tpu_custom_call" | custom-call | flops 1981808640 | bytes 14204928 | tf_op jit(solution)/shard_map/shard/pallas_call | solution.py:25
  42.8 0.0 copy-start.9
  42.8 0.1 collective-permute-start.8
  42.9 0.0 collective-permute-done.16.refs_4_
  42.9 0.0 collective-permute-done.17.refs_5_
  43.0 6.7 %shard.3 = (bf16[96,1664]{1,0:T(8,128)(2,1)S(1)}, bf16[96,1664]{1,0:T(8,128)(2,1)S(1)}) custom-call(bf16[24,3072]{1,0:T(8,128)(2,1)S(1)} %get-tuple-element.29.refs_0_, bf16[24,3072]{1,0:T(8,128)(2,1)S(1)} %collective-permute-done.13.refs_1_, bf16[24,3072]{1,0:T(8,128)(2,1)S(1)} %collective-permute-done.14.refs_2_, ...), custom_call_target="tpu_custom_call" | custom-call | flops 1981808640 | bytes 14204928 | tf_op jit(solution)/shard_map/shard/pallas_call | solution.py:25
  49.7 0.5 collective-permute-start.20
  50.2 0.2 chip.2
  50.3 0.8 %collective-permute-start.9 = (bf16[24,1664]{1,0:T(8,128)(2,1)S(1)}, bf16[24,1664]{1,0:T(8,128)(2,1)S(1)}, u32[]{:S(2)}, u32[]{:S(2)}) collective-permute-start(bf16[24,1664]{1,0:T(8,128)(2,1)S(1)} %get-tuple-element.26), channel_id=1, source_target_pairs={{0,2},{1,3},{2,0},{3,1},{4,6},{5,7},{6,4},{7,5},{8,10},{9,11},{10,... | collective-permute-start | bytes 239624 | tf_op jit(solution)/shard_map/ppermute | solution.py:214
  51.1 1.7 %collective-permute-start.10 = (bf16[24,1664]{1,0:T(8,128)(2,1)S(1)}, bf16[24,1664]{1,0:T(8,128)(2,1)S(1)}, u32[]{:S(2)}, u32[]{:S(2)}) collective-permute-start(bf16[24,1664]{1,0:T(8,128)(2,1)S(1)} %get-tuple-element.27), channel_id=1, source_target_pairs={{0,4},{1,5},{2,6},{3,7},{4,0},{5,1},{6,2},{7,3},{8,12},{9,13},{10,... | collective-permute-start | bytes 239624 | tf_op jit(solution)/shard_map/ppermute | solution.py:214
  52.9 1.0 %collective-permute-start.11 = (bf16[24,1664]{1,0:T(8,128)(2,1)S(1)}, bf16[24,1664]{1,0:T(8,128)(2,1)S(1)}, u32[]{:S(2)}, u32[]{:S(2)}) collective-permute-start(bf16[24,1664]{1,0:T(8,128)(2,1)S(1)} %get-tuple-element.28), channel_id=1, source_target_pairs={{0,6},{1,7},{2,4},{3,5},{4,2},{5,3},{6,0},{7,1},{8,14},{9,15},{10,... | collective-permute-start | bytes 239624 | tf_op jit(solution)/shard_map/ppermute | solution.py:214
  53.9 0.2 chip.3
  54.0 0.8 %collective-permute-start.21 = (bf16[24,1664]{1,0:T(8,128)(2,1)S(1)}, bf16[24,1664]{1,0:T(8,128)(2,1)S(1)}, u32[]{:S(2)}, u32[]{:S(2)}) collective-permute-start(bf16[24,1664]{1,0:T(8,128)(2,1)S(1)} %get-tuple-element.33), channel_id=1, source_target_pairs={{0,2},{1,3},{2,0},{3,1},{4,6},{5,7},{6,4},{7,5},{8,10},{9,11},{10,... | collective-permute-start | bytes 239624 | tf_op jit(solution)/shard_map/ppermute | solution.py:214
  54.9 1.7 %collective-permute-start.22 = (bf16[24,1664]{1,0:T(8,128)(2,1)S(1)}, bf16[24,1664]{1,0:T(8,128)(2,1)S(1)}, u32[]{:S(2)}, u32[]{:S(2)}) collective-permute-start(bf16[24,1664]{1,0:T(8,128)(2,1)S(1)} %get-tuple-element.34), channel_id=1, source_target_pairs={{0,4},{1,5},{2,6},{3,7},{4,0},{5,1},{6,2},{7,3},{8,12},{9,13},{10,... | collective-permute-start | bytes 239624 | tf_op jit(solution)/shard_map/ppermute | solution.py:214
  56.6 1.0 %collective-permute-start.23 = (bf16[24,1664]{1,0:T(8,128)(2,1)S(1)}, bf16[24,1664]{1,0:T(8,128)(2,1)S(1)}, u32[]{:S(2)}, u32[]{:S(2)}) collective-permute-start(bf16[24,1664]{1,0:T(8,128)(2,1)S(1)} %get-tuple-element.35), channel_id=1, source_target_pairs={{0,6},{1,7},{2,4},{3,5},{4,2},{5,3},{6,0},{7,1},{8,14},{9,15},{10,... | collective-permute-start | bytes 239624 | tf_op jit(solution)/shard_map/ppermute | solution.py:214
  57.6 1.3 %collective-permute-done.11.refs_3_ = bf16[24,1664]{1,0:T(8,128)(2,1)S(1)} collective-permute-done((bf16[24,1664]{1,0:T(8,128)(2,1)S(1)}, bf16[24,1664]{1,0:T(8,128)(2,1)S(1)}, u32[]{:S(2)}, u32[]{:S(2)}) %collective-permute-start.11) | collective-permute-done | bytes 79904 | tf_op jit(solution)/shard_map/ppermute | solution.py:214
  58.9 0.2 other.1
  59.0 3.1 %collective-permute-start.12 = (bf16[24,1664]{1,0:T(8,128)(2,1)S(1)}, bf16[24,1664]{1,0:T(8,128)(2,1)S(1)}, u32[]{:S(2)}, u32[]{:S(2)}) collective-permute-start(bf16[24,1664]{1,0:T(8,128)(2,1)S(1)} %other.1), channel_id=1, source_target_pairs={{0,8},{1,9},{2,10},{3,11},{4,12},{5,13},{6,14},{7,15},{8,0},{9,1},... | collective-permute-start | bytes 239624 | tf_op jit(solution)/shard_map/ppermute | solution.py:214
  62.1 0.6 collective-permute-done.23.refs_3_
  62.8 2.8 %collective-permute-done.12.back_ref = bf16[24,1664]{1,0:T(8,128)(2,1)S(1)} collective-permute-done((bf16[24,1664]{1,0:T(8,128)(2,1)S(1)}, bf16[24,1664]{1,0:T(8,128)(2,1)S(1)}, u32[]{:S(2)}, u32[]{:S(2)}) %collective-permute-start.12) | collective-permute-done | bytes 79904 | tf_op jit(solution)/shard_map/ppermute | solution.py:214
  65.6 1.7 %final.1 = (bf16[64,3072]{1,0:T(8,128)(2,1)}, f32[4,64]{1,0:T(4,128)}) custom-call(s32[1]{0:T(128)} %bitcast.mine_ref, s32[4,64]{1,0:T(4,128)S(1)} %bitcast.11, f32[48,64]{1,0:T(8,128)S(1)} %get-tuple-element.20.place_ref, f32[48,64]{1,0:T(8,128)S(1)} %get-tuple-element.21.weight_ref, bf16[24,1664]{1,0:T(8,128)(2,1)S(1)} %collective-permute-done.12.back_ref, ...), custom_call_target="tpu_custom_call" | custom-call | bytes 899076 | tf_op jit(solution)/shard_map/final/pallas_call | solution.py:25
  (29 shorter events, 0.1 us)
Async XLA Ops:
  0.6 1.0 %copy-start.6 = (bf16[64,3072]{1,0:T(8,128)(2,1)S(1)}, bf16[64,3072]{1,0:T(8,128)(2,1)}, u32[]{:S(2)}) copy-start(bf16[64,3072]{1,0:T(8,128)(2,1)} %tok_ref.1) | copy-start | bytes 1179652
  1.6 1.0 %copy-start.7 = (bf16[64,3072]{1,0:T(8,128)(2,1)S(1)}, bf16[64,3072]{1,0:T(8,128)(2,1)}, u32[]{:S(2)}) copy-start(bf16[64,3072]{1,0:T(8,128)(2,1)} %cot_ref.1) | copy-start | bytes 1179652
  2.6 0.7 %copy-start.8 = (s32[64,4]{0,1:T(4,128)S(1)}, s32[64,4]{0,1:T(4,128)}, u32[]{:S(2)}) copy-start(s32[64,4]{0,1:T(4,128)} %param.10) | copy-start | bytes 3076
  3.3 0.7 %copy-start.10 = (f32[64,4]{0,1:T(4,128)S(1)}, f32[64,4]{0,1:T(4,128)}, u32[]{:S(2)}) copy-start(f32[64,4]{0,1:T(4,128)} %param.9) | copy-start | bytes 3076
  4.4 11.2 %collective-permute-start = (bf16[24,3072]{1,0:T(8,128)(2,1)S(1)}, bf16[24,3072]{1,0:T(8,128)(2,1)S(1)}, u32[]{:S(2)}, u32[]{:S(2)}) collective-permute-start(bf16[24,3072]{1,0:T(8,128)(2,1)S(1)} %get-tuple-element.22), channel_id=1, source_target_pairs={{0,8},{1,9},{2,10},{3,11},{4,12},{5,13},{6,14},{7,15},{8,0},{9,1},... | collective-permute-start | bytes 442376 | tf_op jit(solution)/shard_map/ppermute | solution.py:214
  8.5 10.6 %collective-permute-start.13 = (bf16[24,3072]{1,0:T(8,128)(2,1)S(1)}, bf16[24,3072]{1,0:T(8,128)(2,1)S(1)}, u32[]{:S(2)}, u32[]{:S(2)}) collective-permute-start(bf16[24,3072]{1,0:T(8,128)(2,1)S(1)} %get-tuple-element.29.refs_0_), channel_id=1, source_target_pairs={{0,2},{1,3},{2,0},{3,1},{4,6},{5,7},{6,4},{7,5},{8,10},{9,11},{10,... | collective-permute-start | bytes 442376 | tf_op jit(solution)/shard_map/ppermute | solution.py:214
  10.1 10.7 %collective-permute-start.14 = (bf16[24,3072]{1,0:T(8,128)(2,1)S(1)}, bf16[24,3072]{1,0:T(8,128)(2,1)S(1)}, u32[]{:S(2)}, u32[]{:S(2)}) collective-permute-start(bf16[24,3072]{1,0:T(8,128)(2,1)S(1)} %get-tuple-element.29.refs_0_), channel_id=1, source_target_pairs={{0,4},{1,5},{2,6},{3,7},{4,0},{5,1},{6,2},{7,3},{8,12},{9,13},{10,... | collective-permute-start | bytes 442376 | tf_op jit(solution)/shard_map/ppermute | solution.py:214
  15.6 5.9 %collective-permute-start.1 = (bf16[24,3072]{1,0:T(8,128)(2,1)S(1)}, bf16[24,3072]{1,0:T(8,128)(2,1)S(1)}, u32[]{:S(2)}, u32[]{:S(2)}) collective-permute-start(bf16[24,3072]{1,0:T(8,128)(2,1)S(1)} %collective-permute-done.refs_0_), channel_id=1, source_target_pairs={{0,2},{1,3},{2,0},{3,1},{4,6},{5,7},{6,4},{7,5},{8,10},{9,11},{10,... | collective-permute-start | bytes 442376 | tf_op jit(solution)/shard_map/ppermute | solution.py:214
  17.2 6.8 %collective-permute-start.2 = (bf16[24,3072]{1,0:T(8,128)(2,1)S(1)}, bf16[24,3072]{1,0:T(8,128)(2,1)S(1)}, u32[]{:S(2)}, u32[]{:S(2)}) collective-permute-start(bf16[24,3072]{1,0:T(8,128)(2,1)S(1)} %collective-permute-done.refs_0_), channel_id=1, source_target_pairs={{0,4},{1,5},{2,6},{3,7},{4,0},{5,1},{6,2},{7,3},{8,12},{9,13},{10,... | collective-permute-start | bytes 442376 | tf_op jit(solution)/shard_map/ppermute | solution.py:214
  17.8 9.1 %collective-permute-start.3 = (bf16[24,3072]{1,0:T(8,128)(2,1)S(1)}, bf16[24,3072]{1,0:T(8,128)(2,1)S(1)}, u32[]{:S(2)}, u32[]{:S(2)}) collective-permute-start(bf16[24,3072]{1,0:T(8,128)(2,1)S(1)} %collective-permute-done.refs_0_), channel_id=1, source_target_pairs={{0,6},{1,7},{2,4},{3,5},{4,2},{5,3},{6,0},{7,1},{8,14},{9,15},{10,... | collective-permute-start | bytes 442376 | tf_op jit(solution)/shard_map/ppermute | solution.py:214
  19.1 9.4 %collective-permute-start.15 = (bf16[24,3072]{1,0:T(8,128)(2,1)S(1)}, bf16[24,3072]{1,0:T(8,128)(2,1)S(1)}, u32[]{:S(2)}, u32[]{:S(2)}) collective-permute-start(bf16[24,3072]{1,0:T(8,128)(2,1)S(1)} %get-tuple-element.29.refs_0_), channel_id=1, source_target_pairs={{0,6},{1,7},{2,4},{3,5},{4,2},{5,3},{6,0},{7,1},{8,14},{9,15},{10,... | collective-permute-start | bytes 442376 | tf_op jit(solution)/shard_map/ppermute | solution.py:214
  20.7 7.9 %collective-permute-start.4 = (bf16[24,3072]{1,0:T(8,128)(2,1)S(1)}, bf16[24,3072]{1,0:T(8,128)(2,1)S(1)}, u32[]{:S(2)}, u32[]{:S(2)}) collective-permute-start(bf16[24,3072]{1,0:T(8,128)(2,1)S(1)} %collective-permute-done.refs_0_), channel_id=1, source_target_pairs={{0,1},{1,0},{2,3},{3,2},{4,5},{5,4},{6,7},{7,6},{8,9},{9,8},{10,11... | collective-permute-start | bytes 442376 | tf_op jit(solution)/shard_map/ppermute | solution.py:214
  21.6 7.5 %collective-permute-start.5 = (bf16[24,3072]{1,0:T(8,128)(2,1)S(1)}, bf16[24,3072]{1,0:T(8,128)(2,1)S(1)}, u32[]{:S(2)}, u32[]{:S(2)}) collective-permute-start(bf16[24,3072]{1,0:T(8,128)(2,1)S(1)} %collective-permute-done.1.refs_1_), channel_id=1, source_target_pairs={{0,1},{1,0},{2,3},{3,2},{4,5},{5,4},{6,7},{7,6},{8,9},{9,8},{10,11... | collective-permute-start | bytes 442376 | tf_op jit(solution)/shard_map/ppermute | solution.py:214
  24.0 5.2 %collective-permute-start.6 = (bf16[24,3072]{1,0:T(8,128)(2,1)S(1)}, bf16[24,3072]{1,0:T(8,128)(2,1)S(1)}, u32[]{:S(2)}, u32[]{:S(2)}) collective-permute-start(bf16[24,3072]{1,0:T(8,128)(2,1)S(1)} %collective-permute-done.2.refs_2_), channel_id=1, source_target_pairs={{0,1},{1,0},{2,3},{3,2},{4,5},{5,4},{6,7},{7,6},{8,9},{9,8},{10,11... | collective-permute-start | bytes 442376 | tf_op jit(solution)/shard_map/ppermute | solution.py:214
  26.9 2.7 %collective-permute-start.7 = (bf16[24,3072]{1,0:T(8,128)(2,1)S(1)}, bf16[24,3072]{1,0:T(8,128)(2,1)S(1)}, u32[]{:S(2)}, u32[]{:S(2)}) collective-permute-start(bf16[24,3072]{1,0:T(8,128)(2,1)S(1)} %collective-permute-done.3.refs_3_), channel_id=1, source_target_pairs={{0,1},{1,0},{2,3},{3,2},{4,5},{5,4},{6,7},{7,6},{8,9},{9,8},{10,11... | collective-permute-start | bytes 442376 | tf_op jit(solution)/shard_map/ppermute | solution.py:214
  28.6 14.4 %collective-permute-start.16 = (bf16[24,3072]{1,0:T(8,128)(2,1)S(1)}, bf16[24,3072]{1,0:T(8,128)(2,1)S(1)}, u32[]{:S(2)}, u32[]{:S(2)}) collective-permute-start(bf16[24,3072]{1,0:T(8,128)(2,1)S(1)} %get-tuple-element.29.refs_0_), channel_id=1, source_target_pairs={{0,1},{1,0},{2,3},{3,2},{4,5},{5,4},{6,7},{7,6},{8,9},{9,8},{10,11... | collective-permute-start | bytes 442376 | tf_op jit(solution)/shard_map/ppermute | solution.py:214
  28.6 14.4 %collective-permute-start.17 = (bf16[24,3072]{1,0:T(8,128)(2,1)S(1)}, bf16[24,3072]{1,0:T(8,128)(2,1)S(1)}, u32[]{:S(2)}, u32[]{:S(2)}) collective-permute-start(bf16[24,3072]{1,0:T(8,128)(2,1)S(1)} %collective-permute-done.13.refs_1_), channel_id=1, source_target_pairs={{0,1},{1,0},{2,3},{3,2},{4,5},{5,4},{6,7},{7,6},{8,9},{9,8},{10,11... | collective-permute-start | bytes 442376 | tf_op jit(solution)/shard_map/ppermute | solution.py:214
  29.1 13.9 %collective-permute-start.18 = (bf16[24,3072]{1,0:T(8,128)(2,1)S(1)}, bf16[24,3072]{1,0:T(8,128)(2,1)S(1)}, u32[]{:S(2)}, u32[]{:S(2)}) collective-permute-start(bf16[24,3072]{1,0:T(8,128)(2,1)S(1)} %collective-permute-done.14.refs_2_), channel_id=1, source_target_pairs={{0,1},{1,0},{2,3},{3,2},{4,5},{5,4},{6,7},{7,6},{8,9},{9,8},{10,11... | collective-permute-start | bytes 442376 | tf_op jit(solution)/shard_map/ppermute | solution.py:214
  29.2 13.8 %collective-permute-start.19 = (bf16[24,3072]{1,0:T(8,128)(2,1)S(1)}, bf16[24,3072]{1,0:T(8,128)(2,1)S(1)}, u32[]{:S(2)}, u32[]{:S(2)}) collective-permute-start(bf16[24,3072]{1,0:T(8,128)(2,1)S(1)} %collective-permute-done.15.refs_3_), channel_id=1, source_target_pairs={{0,1},{1,0},{2,3},{3,2},{4,5},{5,4},{6,7},{7,6},{8,9},{9,8},{10,11... | collective-permute-start | bytes 442376 | tf_op jit(solution)/shard_map/ppermute | solution.py:214
  29.6 2.2 %copy-start = (bf16[3072,672]{0,1:T(8,128)(2,1)S(1)}, bf16[3072,672]{0,1:T(8,128)(2,1)}, u32[]{:S(2)}) copy-start(bf16[3072,672]{0,1:T(8,128)(2,1)} %param.11) | copy-start | bytes 12386308
  31.8 2.2 %copy-start.2 = (bf16[3072,672]{0,1:T(8,128)(2,1)S(1)}, bf16[3072,672]{0,1:T(8,128)(2,1)}, u32[]{:S(2)}) copy-start(bf16[3072,672]{0,1:T(8,128)(2,1)} %param.12) | copy-start | bytes 12386308
  33.9 2.2 %copy-start.4 = (bf16[672,3072]{1,0:T(8,128)(2,1)S(1)}, bf16[672,3072]{1,0:T(8,128)(2,1)}, u32[]{:S(2)}) copy-start(bf16[672,3072]{1,0:T(8,128)(2,1)} %refs_10_.3) | copy-start | bytes 12386308
  36.1 6.8 %copy-start.1 = (bf16[3072,672]{0,1:T(8,128)(2,1)S(1)}, bf16[3072,672]{0,1:T(8,128)(2,1)}, u32[]{:S(2)}) copy-start(bf16[3072,672]{0,1:T(8,128)(2,1)} %param.11) | copy-start | bytes 12386308
  36.1 6.9 %copy-start.3 = (bf16[3072,672]{0,1:T(8,128)(2,1)S(1)}, bf16[3072,672]{0,1:T(8,128)(2,1)}, u32[]{:S(2)}) copy-start(bf16[3072,672]{0,1:T(8,128)(2,1)} %param.12) | copy-start | bytes 12386308
  36.1 6.9 %copy-start.5 = (bf16[672,3072]{1,0:T(8,128)(2,1)S(1)}, bf16[672,3072]{1,0:T(8,128)(2,1)}, u32[]{:S(2)}) copy-start(bf16[672,3072]{1,0:T(8,128)(2,1)} %refs_10_.3) | copy-start | bytes 12386308
  42.8 22.8 %copy-start.9 = (s32[64,4]{0,1:T(4,128)S(1)}, s32[64,4]{0,1:T(4,128)}, u32[]{:S(2)}) copy-start(s32[64,4]{0,1:T(4,128)} %param.10) | copy-start | bytes 3076
  42.8 7.4 %collective-permute-start.8 = (bf16[96,1664]{1,0:T(8,128)(2,1)S(1)}, bf16[96,1664]{1,0:T(8,128)(2,1)S(1)}, u32[]{:S(2)}, u32[]{:S(2)}) collective-permute-start(bf16[96,1664]{1,0:T(8,128)(2,1)S(1)} %get-tuple-element.24), channel_id=1, source_target_pairs={{0,1},{1,0},{2,3},{3,2},{4,5},{5,4},{6,7},{7,6},{8,9},{9,8},{10,11... | collective-permute-start | bytes 958472 | tf_op jit(solution)/shard_map/ppermute | solution.py:214
  49.7 4.2 %collective-permute-start.20 = (bf16[96,1664]{1,0:T(8,128)(2,1)S(1)}, bf16[96,1664]{1,0:T(8,128)(2,1)S(1)}, u32[]{:S(2)}, u32[]{:S(2)}) collective-permute-start(bf16[96,1664]{1,0:T(8,128)(2,1)S(1)} %get-tuple-element.31), channel_id=1, source_target_pairs={{0,1},{1,0},{2,3},{3,2},{4,5},{5,4},{6,7},{7,6},{8,9},{9,8},{10,11... | collective-permute-start | bytes 958472 | tf_op jit(solution)/shard_map/ppermute | solution.py:214
  50.3 6.3 %collective-permute-start.9 = (bf16[24,1664]{1,0:T(8,128)(2,1)S(1)}, bf16[24,1664]{1,0:T(8,128)(2,1)S(1)}, u32[]{:S(2)}, u32[]{:S(2)}) collective-permute-start(bf16[24,1664]{1,0:T(8,128)(2,1)S(1)} %get-tuple-element.26), channel_id=1, source_target_pairs={{0,2},{1,3},{2,0},{3,1},{4,6},{5,7},{6,4},{7,5},{8,10},{9,11},{10,... | collective-permute-start | bytes 239624 | tf_op jit(solution)/shard_map/ppermute | solution.py:214
  51.1 6.5 %collective-permute-start.10 = (bf16[24,1664]{1,0:T(8,128)(2,1)S(1)}, bf16[24,1664]{1,0:T(8,128)(2,1)S(1)}, u32[]{:S(2)}, u32[]{:S(2)}) collective-permute-start(bf16[24,1664]{1,0:T(8,128)(2,1)S(1)} %get-tuple-element.27), channel_id=1, source_target_pairs={{0,4},{1,5},{2,6},{3,7},{4,0},{5,1},{6,2},{7,3},{8,12},{9,13},{10,... | collective-permute-start | bytes 239624 | tf_op jit(solution)/shard_map/ppermute | solution.py:214
  52.9 6.0 %collective-permute-start.11 = (bf16[24,1664]{1,0:T(8,128)(2,1)S(1)}, bf16[24,1664]{1,0:T(8,128)(2,1)S(1)}, u32[]{:S(2)}, u32[]{:S(2)}) collective-permute-start(bf16[24,1664]{1,0:T(8,128)(2,1)S(1)} %get-tuple-element.28), channel_id=1, source_target_pairs={{0,6},{1,7},{2,4},{3,5},{4,2},{5,3},{6,0},{7,1},{8,14},{9,15},{10,... | collective-permute-start | bytes 239624 | tf_op jit(solution)/shard_map/ppermute | solution.py:214
  54.0 8.1 %collective-permute-start.21 = (bf16[24,1664]{1,0:T(8,128)(2,1)S(1)}, bf16[24,1664]{1,0:T(8,128)(2,1)S(1)}, u32[]{:S(2)}, u32[]{:S(2)}) collective-permute-start(bf16[24,1664]{1,0:T(8,128)(2,1)S(1)} %get-tuple-element.33), channel_id=1, source_target_pairs={{0,2},{1,3},{2,0},{3,1},{4,6},{5,7},{6,4},{7,5},{8,10},{9,11},{10,... | collective-permute-start | bytes 239624 | tf_op jit(solution)/shard_map/ppermute | solution.py:214
  54.9 7.3 %collective-permute-start.22 = (bf16[24,1664]{1,0:T(8,128)(2,1)S(1)}, bf16[24,1664]{1,0:T(8,128)(2,1)S(1)}, u32[]{:S(2)}, u32[]{:S(2)}) collective-permute-start(bf16[24,1664]{1,0:T(8,128)(2,1)S(1)} %get-tuple-element.34), channel_id=1, source_target_pairs={{0,4},{1,5},{2,6},{3,7},{4,0},{5,1},{6,2},{7,3},{8,12},{9,13},{10,... | collective-permute-start | bytes 239624 | tf_op jit(solution)/shard_map/ppermute | solution.py:214
  56.6 6.2 %collective-permute-start.23 = (bf16[24,1664]{1,0:T(8,128)(2,1)S(1)}, bf16[24,1664]{1,0:T(8,128)(2,1)S(1)}, u32[]{:S(2)}, u32[]{:S(2)}) collective-permute-start(bf16[24,1664]{1,0:T(8,128)(2,1)S(1)} %get-tuple-element.35), channel_id=1, source_target_pairs={{0,6},{1,7},{2,4},{3,5},{4,2},{5,3},{6,0},{7,1},{8,14},{9,15},{10,... | collective-permute-start | bytes 239624 | tf_op jit(solution)/shard_map/ppermute | solution.py:214
  59.0 6.5 %collective-permute-start.12 = (bf16[24,1664]{1,0:T(8,128)(2,1)S(1)}, bf16[24,1664]{1,0:T(8,128)(2,1)S(1)}, u32[]{:S(2)}, u32[]{:S(2)}) collective-permute-start(bf16[24,1664]{1,0:T(8,128)(2,1)S(1)} %other.1), channel_id=1, source_target_pairs={{0,8},{1,9},{2,10},{3,11},{4,12},{5,13},{6,14},{7,15},{8,0},{9,1},... | collective-permute-start | bytes 239624 | tf_op jit(solution)/shard_map/ppermute | solution.py:214

commit v2 on v1

v2 whole, which is shorter than its diff:
```python
import functools

import jax
import jax.numpy as jnp
from jax import lax
from jax.experimental import pallas as pl
from jax.experimental.pallas import tpu as pltpu
from jax.sharding import PartitionSpec as P

EXP_WIN = 2
CAP = 12
PAIR = 2 * CAP
LANES = 128
ROWS = 16
SKIP = CAP - (PAIR - ROWS)
F32 = jnp.float32
BF16 = jnp.bfloat16
PICK_LIMIT = 60
GATE_FLOPS = 10**10
VMEM = pl.BlockSpec(memory_space=pltpu.VMEM)
HBM = pl.BlockSpec(memory_space=pltpu.HBM)
SMEM = pl.BlockSpec(memory_space=pltpu.SMEM)


def call(kernel, name, out_shape, in_specs, args, scratch=(), flops=0, limit=16):
    moved = sum(a.size * a.dtype.itemsize for a in args)
    moved += sum(o.size * o.dtype.itemsize for o in out_shape)
    return pl.pallas_call(
        kernel,
        name=name,
        out_shape=out_shape,
        in_specs=in_specs,
        out_specs=[VMEM] * len(out_shape),
        scratch_shapes=list(scratch),
        compiler_params=pltpu.CompilerParams(vmem_limit_bytes=limit << 20),
        cost_estimate=pl.CostEstimate(flops=flops, bytes_accessed=moved, transcendentals=0),
    )(*args)


def struct(shape, dtype):
    return jax.ShapeDtypeStruct(shape, dtype)


def pick_kernel(mine_ref, ids_hbm, gates_hbm, tok_hbm, cot_hbm, own_ref, other_ref, ids_ref, place_ref, weight_ref, gates_ref, tok_ref, cot_ref, sems):
    pairs = ((ids_hbm, ids_ref), (gates_hbm, gates_ref), (tok_hbm, tok_ref), (cot_hbm, cot_ref))
    copies = [pltpu.make_async_copy(a, b, sems.at[i]) for i, (a, b) in enumerate(pairs)]
    for copy in copies:
        copy.start()
    rows = 2 * PAIR
    count = ids_ref.shape[1]
    row = lax.broadcasted_iota(jnp.int32, (rows, count), 0)
    mine = mine_ref[0]
    expert = jnp.where(row < PAIR, mine, EXP_WIN - 1 - mine)
    before = jnp.where(
        lax.broadcasted_iota(jnp.int32, (count, count), 0)
        < lax.broadcasted_iota(jnp.int32, (count, count), 1),
        1.0,
        0.0,
    )
    taken = sum((row >= CAP * i).astype(jnp.int32) for i in range(1, 4))
    want = (row - CAP * taken).astype(F32)
    first = (taken == 0) | (taken == 2)
    named = jnp.zeros((rows, count), F32)
    weight = jnp.zeros((rows, count), F32)
    copies[0].wait()
    copies[1].wait()
    for k in range(ids_ref.shape[0]):
        same = ids_ref[k : k + 1, :] == expert
        named = named + jnp.where(same, 1.0, 0.0)
        weight = weight + jnp.where(same, gates_ref[k : k + 1, :], 0.0)
    slot = jnp.dot(named, before, preferred_element_type=F32)
    place = jnp.where((slot == want) & (named > 0.5), 1.0, 0.0)
    upper = jnp.where(first, place, 0.0).astype(BF16)
    lower = jnp.where(first, 0.0, place).astype(BF16)
    copies[2].wait()
    copies[3].wait()

    def rows_of(part, a, b):
        picked = jnp.dot(upper[part], a, preferred_element_type=F32)
        return (picked + jnp.dot(lower[part], b, preferred_element_type=F32)).astype(BF16)

    half = tok_ref.shape[1] // 2
    for i, ref in enumerate((tok_ref, cot_ref)):
        other_ref[PAIR * i : PAIR * (i + 1), :] = rows_of(slice(PAIR, rows), ref[:, :half], ref[:, half:])
    own_ref[...] = rows_of(slice(0, PAIR), tok_ref[...], cot_ref[...])
    place_ref[...] = place
    weight_ref[...] = place * weight


def split_two(x):
    high = x.astype(BF16).astype(F32)
    return high, x - high


def layout_kernel(weight_ref, left_ref, right_ref):
    weight = weight_ref[...]
    own_high, own_low = split_two(weight[:PAIR])
    other_high, other_low = split_two(weight[PAIR:])
    rest = jnp.zeros((LANES - 5 * PAIR, weight.shape[1]), F32)
    table = jnp.concatenate([other_high, other_low, own_high, own_low, own_high, rest], axis=0)
    row = lax.broadcasted_iota(jnp.int32, table.shape, 0)
    block = sum((row >= PAIR * i).astype(jnp.int32) for i in range(1, 6))
    first = row - PAIR * block < CAP
    left_ref[...] = jnp.where(first, table, 0.0).T.astype(BF16)
    right_ref[...] = jnp.where(first, 0.0, table).T.astype(BF16)


def gate_kernel(*refs):
    refs[-1][...] = jnp.zeros_like(refs[-1])


def nt(a, b):
    return lax.dot_general(a, b, (((1,), (1,)), ((), ())), preferred_element_type=F32)


def tn(a, b):
    return lax.dot_general(a, b, (((0,), (0,)), ((), ())), preferred_element_type=F32)


def weave(left, right, blocks):
    low = lax.broadcasted_iota(jnp.int32, (8, left.shape[1]), 0) < SKIP
    pieces = []
    for b in range(blocks):
        a = ROWS * b
        pieces += [
            left[a : a + 8],
            jnp.where(low, left[a + 8 : a + ROWS], right[a : a + 8]),
            right[a + 8 : a + ROWS],
        ]
    return jnp.concatenate(pieces, axis=0)


def halves(own_refs, own_at, other_refs, other_at, left_ref, right_ref):
    half = left_ref.shape[1]
    upper = slice(other_at, other_at + ROWS)
    lower = slice(other_at + PAIR - ROWS, other_at + PAIR)
    for b, ref in enumerate(own_refs):
        rows = slice(ROWS * b, ROWS * (b + 1))
        left_ref[rows, :] = ref[own_at, :half]
        right_ref[rows, :] = ref[own_at, half:]
    for b, ref in enumerate(other_refs, len(own_refs)):
        rows = slice(ROWS * b, ROWS * (b + 1))
        left_ref[rows, :] = ref[upper, :]
        right_ref[rows, :] = ref[lower, :]


def back_by(x):
    return pltpu.roll(x, x.shape[1] - SKIP, 1)


def forward_kernel(blocks, *refs):
    own_refs, other_refs = refs[:blocks], refs[blocks : 2 * blocks]
    wg_ref, wu_ref, _, slope_ref, active_ref, hidden_ref, left_ref, right_ref = refs[2 * blocks :]
    half = left_ref.shape[1]
    halves(own_refs, slice(0, ROWS), other_refs, 0, left_ref, right_ref)
    split = ROWS * blocks

    def product(w_ref):
        a = nt(w_ref[:, :half], left_ref[...])
        b = nt(w_ref[:, half:], right_ref[...])
        return a + jnp.concatenate([b[:, :split], back_by(b[:, split:])], axis=1)

    g = product(wg_ref)
    u = product(wu_ref)
    sig = jax.nn.sigmoid(g)
    act = g * sig
    hidden_ref[...] = (act * u).astype(BF16)
    active_ref[...] = act
    slope_ref[...] = u * (sig * (1.0 + g * (1.0 - sig)))


def backward_kernel(blocks, *refs):
    own_refs, other_refs = refs[:blocks], refs[blocks : 2 * blocks]
    slope_ref, active_ref, hidden_ref, wg_ref, wu_ref, wd_ref = refs[2 * blocks : 2 * blocks + 6]
    keep_ref, send_ref, left_ref, right_ref = refs[2 * blocks + 6 :]
    half = left_ref.shape[1]
    halves(own_refs, slice(PAIR - ROWS, PAIR), other_refs, PAIR, left_ref, right_ref)
    split = ROWS * blocks
    a = nt(wd_ref[:, :half], left_ref[...])
    b = nt(wd_ref[:, half:], right_ref[...])
    own = back_by(a[:, :split] + b[:, :split])
    dh = jnp.concatenate([own, a[:, split:] + back_by(b[:, split:])], axis=1)
    score = jnp.sum(hidden_ref[...].astype(F32) * dh, axis=0, keepdims=True)
    grads = (dh * slope_ref[...], dh * active_ref[...])

    def put(to, left, right):
        for i in range(2):
            mine = slice(split * i, split * i + split // 2)
            theirs = slice(split * i + split // 2, split * (i + 1))
            rows = slice(PAIR * blocks // 2 * i, PAIR * blocks // 2 * (i + 1))
            keep_ref[rows, to] = weave(left[mine], right[mine], blocks // 2).astype(BF16)
            send_ref[rows, to] = weave(left[theirs], right[theirs], blocks // 2).astype(BF16)

    def back(pair, cols):
        return jnp.dot(pair[0], wg_ref[:, cols], preferred_element_type=F32) + jnp.dot(
            pair[1], wu_ref[:, cols], preferred_element_type=F32
        )

    upper = [x.T.astype(BF16) for x in grads]
    lower = [pltpu.roll(x, SKIP, 1).T.astype(BF16) for x in grads]
    put(slice(0, half), back(upper, slice(0, half)), back(lower, slice(half, 2 * half)))
    score = two_lanes(jnp.broadcast_to(score, (LANES, 2 * split)).T)
    put(slice(half, half + LANES), score, jnp.zeros_like(score))


def two_lanes(total):
    high, low = split_two(total)
    lane = lax.broadcasted_iota(jnp.int32, total.shape, 1)
    return jnp.where(lane == 0, high, jnp.where(lane == 1, low, 0.0))


def packed(total):
    half = total.shape[1] - LANES
    tail = total[:, half:]
    tail = jnp.broadcast_to(tail[:, 0:1] + tail[:, 1:2], tail.shape)
    return jnp.concatenate([total[:, :half], two_lanes(tail)], axis=1).astype(BF16)


def chip_kernel(keep_ref, got_ref, *out_refs):
    total = keep_ref[...].astype(F32) + got_ref[...].astype(F32)
    for i, ref in enumerate(out_refs):
        part = total[PAIR * i : PAIR * (i + 1)]
        ref[...] = part if ref.dtype == F32 else packed(part)


def total_of(refs):
    total = refs[0][...].astype(F32)
    for ref in refs[1:]:
        total = total + ref[...].astype(F32)
    return total


def other_kernel(*refs):
    refs[-1][...] = packed(total_of(refs[:-1]))


def final_kernel(sources, mine_ref, ids_ref, place_ref, left_ref, right_ref, back_ref, *refs):
    own = total_of(refs[:sources])
    grad_ref, gate_ref = refs[sources:]
    back = back_ref[...]
    half = own.shape[1] - LANES
    own_high, own_low = split_two(own[:, :half])
    other = back[:, :half].astype(F32)
    rest = jnp.zeros((LANES - 5 * PAIR, half), F32)
    table = jnp.concatenate([other, other, own_high, own_high, own_low, rest], axis=0).astype(BF16)
    for i, ref in enumerate((left_ref, right_ref)):
        out = jnp.dot(ref[...], table, preferred_element_type=F32)
        grad_ref[:, half * i : half * (i + 1)] = out.astype(BF16)
    tail = jnp.concatenate([own[:, half:], back[:, half:].astype(F32)], axis=0)
    score = (tail[:, 0:1] + tail[:, 1:2]) * place_ref[...]
    mine = mine_ref[0]
    ids = ids_ref[...]
    own_score = jnp.sum(score[:PAIR], axis=0, keepdims=True)
    other_score = jnp.sum(score[PAIR:], axis=0, keepdims=True)
    gate_ref[...] = jnp.where(ids == mine, own_score, 0.0) + jnp.where(
        ids == EXP_WIN - 1 - mine, other_score, 0.0
    )


def per_device(tokens, cotangent, gate_weights, expert_ids, w_gate, w_up, w_down):
    devices = lax.axis_size("expert")
    split = devices // EXP_WIN
    evens = range(2, split, 2)
    width = tokens.shape[1]
    units = w_down.shape[0]
    count = tokens.shape[0]
    wide = width // 2 + LANES
    mine = (lax.axis_index("expert") // split).astype(jnp.int32).reshape(1)
    ids = expert_ids.T
    gates = gate_weights.T

    def swap(x, offset):
        return lax.ppermute(x, "expert", [(i, i ^ offset) for i in range(devices)])

    def like(x):
        return pltpu.VMEM(x.shape, x.dtype)

    own, other, ids, place, weight = call(
        pick_kernel,
        "pick",
        [struct((PAIR, width), BF16), struct((2 * PAIR, width // 2), BF16)]
        + [struct(ids.shape, ids.dtype)]
        + [struct((2 * PAIR, count), F32)] * 2,
        [SMEM] + [HBM] * 4,
        (mine, ids, gates, tokens, cotangent),
        [like(gates), like(tokens), like(cotangent), pltpu.SemaphoreType.DMA((4,))],
        flops=4 * 2 * PAIR * count * width,
        limit=PICK_LIMIT,
    )
    weights = (w_gate.T, w_up.T, w_down)
    left, right = call(
        layout_kernel,
        "layout",
        [struct((count, LANES), BF16)] * 2,
        [VMEM],
        (weight,),
    )

    def near(block):
        return [block] + [swap(block, k) for k in evens]

    def both_cores(blocks):
        return blocks + [swap(b, 1) for b in blocks]

    rows = 2 * split * ROWS
    stacked = [pltpu.VMEM((rows, width // 2), BF16)] * 2
    def gate(*args):
        return call(
            gate_kernel, "gate", [struct((8, LANES), F32)], [VMEM] * len(args), args, flops=GATE_FLOPS
        )[0]

    together = lax.optimization_barrier
    other = swap(other, split)
    own, token = together((own, gate()))
    other, token = together((other, token))
    own = near(own)
    other = near(other)
    own, other[-1] = together((own, other[-1]))
    own = both_cores(own)
    other = both_cores(other)
    states = call(
        functools.partial(forward_kernel, split),
        "forward",
        [struct((units, rows), F32)] * 2 + [struct((units, rows), BF16)],
        [VMEM] * (2 * split + 3),
        (*own, *other, *weights[:2], token),
        stacked,
        flops=4 * rows * width * units,
        limit=24,
    )
    keep, send = call(
        functools.partial(backward_kernel, split),
        "backward",
        [struct((PAIR * split, wide), BF16)] * 2,
        [VMEM] * (2 * split + 6),
        (*own, *other, *states, *weights),
        stacked,
        flops=6 * rows * width * units,
        limit=24,
    )
    got = swap(send, 1)
    kinds = [struct((PAIR, wide), F32)] + [struct((PAIR, wide), BF16)] * len(evens)
    sums = call(chip_kernel, "chip", kinds * 2, [VMEM] * 2, (keep, got))

    def returned(sums):
        return [sums[0]] + [swap(s, k) for s, k in zip(sums[1:], evens)]

    cross_back = returned(sums[len(kinds) :])
    own_back = returned(sums[: len(kinds)])
    (cross_total,) = call(
        other_kernel, "other", [struct((PAIR, wide), BF16)], [VMEM] * len(cross_back), tuple(cross_back)
    )
    back = swap(cross_total, split)
    grad, gate_grad = call(
        functools.partial(final_kernel, len(own_back)),
        "final",
        [struct((count, width), BF16), struct(ids.shape, F32)],
        [SMEM] + [VMEM] * (5 + len(own_back)),
        (mine, ids, place, left, right, back, *own_back),
    )
    return (grad, gate_grad.T)


def solution(mesh):
    rows = P(("groups", "expert"), None)
    return jax.shard_map(
        per_device,
        mesh=mesh,
        in_specs=(rows, rows, rows, rows, P(None, "expert"), P(None, "expert"), P("expert", None)),
        out_specs=(rows, rows),
        check_vma=False,
    )
```

time: 67.6 us -> 52.7 us (0.78)
  local copies, waits for them, and re-layouts: 9.87 us -> 0.04 us
  Pallas kernels: 15.9 us -> 10.5 us
  waiting for transfers between devices: 16.6 us -> 18.8 us
  starting transfers between devices: 24.1 us -> 22.5 us
    unnamed x22 -> x14, local copies, waits for them, and re-layouts: 9.87 us -> 0.04 us
    pallas_call x7 -> x8, Pallas kernels: 15.9 us -> 10.5 us  [call(): pl.pallas_call(kernel, name=name, out_shape=out_shape, in_specs=in_specs,...]
    ppermute x24 -> x23, waiting for transfers between devices: 16.6 us -> 18.8 us  [swap(): return lax.ppermute(x, 'expert', [(i, i ^ offset) for i in range(devices)])]
    ppermute x24 -> x23, starting transfers between devices: 24.1 us -> 22.5 us  [swap(): return lax.ppermute(x, 'expert', [(i, i ^ offset) for i in range(devices)])]
  transfers between devices with their start and end apart: 24 -> 23, of which waited for: 8 -> 12; matrix products, arithmetic and copies ran while one was open for 0% -> 0% of each run, Pallas kernels for 21% -> 0%
where the time goes in v2:
time: 52.7 us; the launch traced here: 52.5 us
  starting transfers between devices  22.5 us (43%)
  waiting for transfers between devices  18.8 us (36%)
  Pallas kernels  10.5 us (20%)
  between operations  0.79 us (1%)
    ppermute x23, starting transfers between devices, swap(): return lax.ppermute(x, 'expert', [(i, i ^ offset) for i in range(devices)])  22.5 us
    ppermute x23, waiting for transfers between devices, swap(): return lax.ppermute(x, 'expert', [(i, i ^ offset) for i in range(devices)])  18.8 us
    pallas_call x8, Pallas kernels, call(): pl.pallas_call(kernel, name=name, out_shape=out_shape, in_specs=in_specs,...  10.5 us
  transfers between devices with their start and end apart: 23, of which 12 were waited for; matrix products, arithmetic and copies ran while one was open for 0% of the time, Pallas kernels for 0%

profile of v2, /device:TPU:0, one launch (start us, length us, event | category | flops | bytes accessed | tf_op | source)
XLA Modules:
  0.0 52.5 jit_solution(15588261603734240140)
XLA Ops:
  0.6 2.2 %pick.1 = (bf16[24,3072]{1,0:T(8,128)(2,1)}, bf16[48,1536]{1,0:T(8,128)(2,1)}, s32[4,64]{1,0:T(4,128)}, f32[48,64]{1,0:T(8,128)}, f32[48,64]{1,0:T(8,128)}) custom-call(s32[1]{0:T(128)} %bitcast.mine_ref, s32[4,64]{1,0:T(4,128)} %bitcast.10, f32[4,64]{1,0:T(4,128)} %bitcast.11, bf16[64,3072]{1,0:T(8,128)(2,1)} %tok_hbm.1, bf16[64,3072]{1,0:T(8,128)(2,1)} %cot_hbm.1), custom_call_target="tpu_custom_call" | custom-call | flops 37748736 | bytes 1108996 | tf_op jit(solution)/shard_map/pick/pallas_call | solution.py:28
  2.9 0.0 copy-start.3
  2.9 0.0 copy-start
  2.9 0.0 copy-start.1
  2.9 4.1 %collective-permute-start.3 = (bf16[48,1536]{1,0:T(8,128)(2,1)}, bf16[48,1536]{1,0:T(8,128)(2,1)S(1)}, u32[]{:S(2)}, u32[]{:S(2)}) collective-permute-start(bf16[48,1536]{1,0:T(8,128)(2,1)} %get-tuple-element.40), channel_id=1, source_target_pairs={{0,8},{1,9},{2,10},{3,11},{4,12},{5,13},{6,14},{7,15},{8,0},{9,1},... | collective-permute-start | bytes 442376 | tf_op jit(solution)/shard_map/ppermute | solution.py:273
  7.0 1.5 %collective-permute-start = (bf16[24,3072]{1,0:T(8,128)(2,1)S(1)}, bf16[24,3072]{1,0:T(8,128)(2,1)S(1)}, u32[]{:S(2)}, u32[]{:S(2)}) collective-permute-start(bf16[24,3072]{1,0:T(8,128)(2,1)S(1)} %copy-done.3), channel_id=1, source_target_pairs={{0,2},{1,3},{2,0},{3,1},{4,6},{5,7},{6,4},{7,5},{8,10},{9,11},{10,... | collective-permute-start | bytes 442376 | tf_op jit(solution)/shard_map/ppermute | solution.py:273
  8.5 1.6 %collective-permute-start.1 = (bf16[24,3072]{1,0:T(8,128)(2,1)S(1)}, bf16[24,3072]{1,0:T(8,128)(2,1)S(1)}, u32[]{:S(2)}, u32[]{:S(2)}) collective-permute-start(bf16[24,3072]{1,0:T(8,128)(2,1)S(1)} %copy-done.3), channel_id=1, source_target_pairs={{0,4},{1,5},{2,6},{3,7},{4,0},{5,1},{6,2},{7,3},{8,12},{9,13},{10,... | collective-permute-start | bytes 442376 | tf_op jit(solution)/shard_map/ppermute | solution.py:273
  10.1 0.4 collective-permute-start.2
  10.5 3.8 %collective-permute-done.3.refs_8_ = bf16[48,1536]{1,0:T(8,128)(2,1)S(1)} collective-permute-done((bf16[48,1536]{1,0:T(8,128)(2,1)}, bf16[48,1536]{1,0:T(8,128)(2,1)S(1)}, u32[]{:S(2)}, u32[]{:S(2)}) %collective-permute-start.3) | collective-permute-done | bytes 147488 | tf_op jit(solution)/shard_map/ppermute | solution.py:273
  14.3 1.7 %collective-permute-start.4 = (bf16[48,1536]{1,0:T(8,128)(2,1)S(1)}, bf16[48,1536]{1,0:T(8,128)(2,1)S(1)}, u32[]{:S(2)}, u32[]{:S(2)}) collective-permute-start(bf16[48,1536]{1,0:T(8,128)(2,1)S(1)} %collective-permute-done.3.refs_8_), channel_id=1, source_target_pairs={{0,6},{1,7},{2,4},{3,5},{4,2},{5,3},{6,0},{7,1},{8,14},{9,15},{10,... | collective-permute-start | bytes 442376 | tf_op jit(solution)/shard_map/ppermute | solution.py:273
  16.1 0.5 collective-permute-start.9
  16.6 0.0 collective-permute-done.refs_1_
  16.6 1.3 %collective-permute-start.10 = (bf16[48,1536]{1,0:T(8,128)(2,1)S(1)}, bf16[48,1536]{1,0:T(8,128)(2,1)S(1)}, u32[]{:S(2)}, u32[]{:S(2)}) collective-permute-start(bf16[48,1536]{1,0:T(8,128)(2,1)S(1)} %collective-permute-done.3.refs_8_), channel_id=1, source_target_pairs={{0,4},{1,5},{2,6},{3,7},{4,0},{5,1},{6,2},{7,3},{8,12},{9,13},{10,... | collective-permute-start | bytes 442376 | tf_op jit(solution)/shard_map/ppermute | solution.py:273
  17.8 0.0 collective-permute-done.1.refs_2_
  17.8 0.0 collective-permute-start.11
  17.8 2.3 %collective-permute-done.2.refs_3_ = bf16[24,3072]{1,0:T(8,128)(2,1)S(1)} collective-permute-done((bf16[24,3072]{1,0:T(8,128)(2,1)S(1)}, bf16[24,3072]{1,0:T(8,128)(2,1)S(1)}, u32[]{:S(2)}, u32[]{:S(2)}) %collective-permute-start.2) | collective-permute-done | bytes 147488 | tf_op jit(solution)/shard_map/ppermute | solution.py:273
  20.2 3.1 %collective-permute-done.4.refs_11_ = bf16[48,1536]{1,0:T(8,128)(2,1)S(1)} collective-permute-done((bf16[48,1536]{1,0:T(8,128)(2,1)S(1)}, bf16[48,1536]{1,0:T(8,128)(2,1)S(1)}, u32[]{:S(2)}, u32[]{:S(2)}) %collective-permute-start.4) | collective-permute-done | bytes 147488 | tf_op jit(solution)/shard_map/ppermute | solution.py:273
  23.3 0.5 collective-permute-start.5
  23.8 1.4 %collective-permute-done.9.refs_9_ = bf16[48,1536]{1,0:T(8,128)(2,1)S(1)} collective-permute-done((bf16[48,1536]{1,0:T(8,128)(2,1)S(1)}, bf16[48,1536]{1,0:T(8,128)(2,1)S(1)}, u32[]{:S(2)}, u32[]{:S(2)}) %collective-permute-start.9) | collective-permute-done | bytes 147488 | tf_op jit(solution)/shard_map/ppermute | solution.py:273
  25.1 0.0 collective-permute-start.6
  25.2 0.0 collective-permute-done.10.refs_10_
  25.2 0.5 collective-permute-start.7
  25.7 0.1 collective-permute-start.8
  25.7 0.4 collective-permute-start.12
  26.2 0.1 collective-permute-start.13
  26.2 0.3 collective-permute-done.6.refs_5_
  26.5 0.2 collective-permute-done.7.refs_6_
  26.7 0.3 collective-permute-done.8.refs_7_
  27.0 0.2 collective-permute-done.12.refs_13_
  27.2 0.3 collective-permute-done.13.refs_14_
  27.6 2.6 %forward.1 = (f32[672,256]{1,0:T(8,128)S(1)}, f32[672,256]{1,0:T(8,128)S(1)}, bf16[672,256]{1,0:T(8,128)(2,1)S(1)}) custom-call(bf16[24,3072]{1,0:T(8,128)(2,1)S(1)} %copy-done.3, bf16[24,3072]{1,0:T(8,128)(2,1)S(1)} %collective-permute-done.refs_1_, bf16[24,3072]{1,0:T(8,128)(2,1)S(1)} %collective-permute-done.1.refs_2_, ...), custom_call_target="tpu_custom_call" | custom-call | flops 2113929216 | bytes 12341248 | tf_op jit(solution)/shard_map/forward/pallas_call | solution.py:28
  30.2 0.0 copy-start.6
  30.2 4.1 %backward.1 = (bf16[192,1664]{1,0:T(8,128)(2,1)S(1)}, bf16[192,1664]{1,0:T(8,128)(2,1)S(1)}) custom-call(bf16[24,3072]{1,0:T(8,128)(2,1)S(1)} %copy-done.3, bf16[24,3072]{1,0:T(8,128)(2,1)S(1)} %collective-permute-done.refs_1_, bf16[24,3072]{1,0:T(8,128)(2,1)S(1)} %collective-permute-done.1.refs_2_, bf16[24,3072]{1,0:T(8,128)(2,1)S(1)} %collective-permute-done.2.refs_3_, ...), custom_call_target="tpu_custom_call" | custom-call | flops 3170893824 | bytes 17743872 | tf_op jit(solution)/shard_map/backward/pallas_call | solution.py:28
  34.3 0.3 collective-permute-start.15
  34.6 1.9 %collective-permute-done.15.got_ref = bf16[192,1664]{1,0:T(8,128)(2,1)S(1)} collective-permute-done((bf16[192,1664]{1,0:T(8,128)(2,1)S(1)}, bf16[192,1664]{1,0:T(8,128)(2,1)S(1)}, u32[]{:S(2)}, u32[]{:S(2)}) %collective-permute-start.15) | collective-permute-done | bytes 639008 | tf_op jit(solution)/shard_map/ppermute | solution.py:273
  36.5 0.2 chip.1
  36.7 1.4 %collective-permute-start.16 = (bf16[24,1664]{1,0:T(8,128)(2,1)S(1)}, bf16[24,1664]{1,0:T(8,128)(2,1)S(1)}, u32[]{:S(2)}, u32[]{:S(2)}) collective-permute-start(bf16[24,1664]{1,0:T(8,128)(2,1)S(1)} %get-tuple-element.55), channel_id=1, source_target_pairs={{0,2},{1,3},{2,0},{3,1},{4,6},{5,7},{6,4},{7,5},{8,10},{9,11},{10,... | collective-permute-start | bytes 239624 | tf_op jit(solution)/shard_map/ppermute | solution.py:273
  38.2 0.4 collective-permute-start.17
  38.6 1.7 %collective-permute-start.18 = (bf16[24,1664]{1,0:T(8,128)(2,1)S(1)}, bf16[24,1664]{1,0:T(8,128)(2,1)S(1)}, u32[]{:S(2)}, u32[]{:S(2)}) collective-permute-start(bf16[24,1664]{1,0:T(8,128)(2,1)S(1)} %get-tuple-element.57), channel_id=1, source_target_pairs={{0,6},{1,7},{2,4},{3,5},{4,2},{5,3},{6,0},{7,1},{8,14},{9,15},{10,... | collective-permute-start | bytes 239624 | tf_op jit(solution)/shard_map/ppermute | solution.py:273
  40.3 1.4 %collective-permute-start.20 = (bf16[24,1664]{1,0:T(8,128)(2,1)S(1)}, bf16[24,1664]{1,0:T(8,128)(2,1)S(1)}, u32[]{:S(2)}, u32[]{:S(2)}) collective-permute-start(bf16[24,1664]{1,0:T(8,128)(2,1)S(1)} %get-tuple-element.59), channel_id=1, source_target_pairs={{0,2},{1,3},{2,0},{3,1},{4,6},{5,7},{6,4},{7,5},{8,10},{9,11},{10,... | collective-permute-start | bytes 239624 | tf_op jit(solution)/shard_map/ppermute | solution.py:273
  41.7 0.4 collective-permute-start.21
  42.1 1.7 %collective-permute-start.22 = (bf16[24,1664]{1,0:T(8,128)(2,1)S(1)}, bf16[24,1664]{1,0:T(8,128)(2,1)S(1)}, u32[]{:S(2)}, u32[]{:S(2)}) collective-permute-start(bf16[24,1664]{1,0:T(8,128)(2,1)S(1)} %get-tuple-element.61), channel_id=1, source_target_pairs={{0,6},{1,7},{2,4},{3,5},{4,2},{5,3},{6,0},{7,1},{8,14},{9,15},{10,... | collective-permute-start | bytes 239624 | tf_op jit(solution)/shard_map/ppermute | solution.py:273
  43.8 1.4 %collective-permute-done.18.refs_3_ = bf16[24,1664]{1,0:T(8,128)(2,1)S(1)} collective-permute-done((bf16[24,1664]{1,0:T(8,128)(2,1)S(1)}, bf16[24,1664]{1,0:T(8,128)(2,1)S(1)}, u32[]{:S(2)}, u32[]{:S(2)}) %collective-permute-start.18) | collective-permute-done | bytes 79904 | tf_op jit(solution)/shard_map/ppermute | solution.py:273
  45.1 0.2 other.1
  45.3 2.5 %collective-permute-start.19 = (bf16[24,1664]{1,0:T(8,128)(2,1)S(1)}, bf16[24,1664]{1,0:T(8,128)(2,1)S(1)}, u32[]{:S(2)}, u32[]{:S(2)}) collective-permute-start(bf16[24,1664]{1,0:T(8,128)(2,1)S(1)} %other.1), channel_id=1, source_target_pairs={{0,8},{1,9},{2,10},{3,11},{4,12},{5,13},{6,14},{7,15},{8,0},{9,1},... | collective-permute-start | bytes 239624 | tf_op jit(solution)/shard_map/ppermute | solution.py:273
  47.8 0.1 layout.1
  47.9 3.6 %collective-permute-done.19.back_ref = bf16[24,1664]{1,0:T(8,128)(2,1)S(1)} collective-permute-done((bf16[24,1664]{1,0:T(8,128)(2,1)S(1)}, bf16[24,1664]{1,0:T(8,128)(2,1)S(1)}, u32[]{:S(2)}, u32[]{:S(2)}) %collective-permute-start.19) | collective-permute-done | bytes 79904 | tf_op jit(solution)/shard_map/ppermute | solution.py:273
  51.5 1.0 %final.1 = (bf16[64,3072]{1,0:T(8,128)(2,1)}, f32[4,64]{1,0:T(4,128)}) custom-call(s32[1]{0:T(128)} %bitcast.mine_ref, s32[4,64]{1,0:T(4,128)S(1)} %copy-done.6, f32[48,64]{1,0:T(8,128)S(1)} %copy-done.4, bf16[64,128]{1,0:T(8,128)(2,1)S(1)} %get-tuple-element.36.left_ref, bf16[64,128]{1,0:T(8,128)(2,1)S(1)} %get-tuple-element.37.right_ref, ...), custom_call_target="tpu_custom_call" | custom-call | bytes 919556 | tf_op jit(solution)/shard_map/final/pallas_call | solution.py:28
  (20 shorter events, 0.0 us)
Async XLA Ops:
  2.9 4.1 %copy-start.3 = (bf16[24,3072]{1,0:T(8,128)(2,1)S(1)}, bf16[24,3072]{1,0:T(8,128)(2,1)}, u32[]{:S(2)}) copy-start(bf16[24,3072]{1,0:T(8,128)(2,1)} %get-tuple-element.43.refs_0_) | copy-start | bytes 442372
  2.9 24.7 %copy-start = (bf16[3072,672]{0,1:T(8,128)(2,1)S(1)}, bf16[3072,672]{0,1:T(8,128)(2,1)}, u32[]{:S(2)}) copy-start(bf16[3072,672]{0,1:T(8,128)(2,1)} %param.11) | copy-start | bytes 12386308
  2.9 24.7 %copy-start.1 = (bf16[3072,672]{0,1:T(8,128)(2,1)S(1)}, bf16[3072,672]{0,1:T(8,128)(2,1)}, u32[]{:S(2)}) copy-start(bf16[3072,672]{0,1:T(8,128)(2,1)} %param.12) | copy-start | bytes 12386308
  2.9 11.4 %collective-permute-start.3 = (bf16[48,1536]{1,0:T(8,128)(2,1)}, bf16[48,1536]{1,0:T(8,128)(2,1)S(1)}, u32[]{:S(2)}, u32[]{:S(2)}) collective-permute-start(bf16[48,1536]{1,0:T(8,128)(2,1)} %get-tuple-element.40), channel_id=1, source_target_pairs={{0,8},{1,9},{2,10},{3,11},{4,12},{5,13},{6,14},{7,15},{8,0},{9,1},... | collective-permute-start | bytes 442376 | tf_op jit(solution)/shard_map/ppermute | solution.py:273
  7.0 9.6 %collective-permute-start = (bf16[24,3072]{1,0:T(8,128)(2,1)S(1)}, bf16[24,3072]{1,0:T(8,128)(2,1)S(1)}, u32[]{:S(2)}, u32[]{:S(2)}) collective-permute-start(bf16[24,3072]{1,0:T(8,128)(2,1)S(1)} %copy-done.3), channel_id=1, source_target_pairs={{0,2},{1,3},{2,0},{3,1},{4,6},{5,7},{6,4},{7,5},{8,10},{9,11},{10,... | collective-permute-start | bytes 442376 | tf_op jit(solution)/shard_map/ppermute | solution.py:273
  8.5 9.3 %collective-permute-start.1 = (bf16[24,3072]{1,0:T(8,128)(2,1)S(1)}, bf16[24,3072]{1,0:T(8,128)(2,1)S(1)}, u32[]{:S(2)}, u32[]{:S(2)}) collective-permute-start(bf16[24,3072]{1,0:T(8,128)(2,1)S(1)} %copy-done.3), channel_id=1, source_target_pairs={{0,4},{1,5},{2,6},{3,7},{4,0},{5,1},{6,2},{7,3},{8,12},{9,13},{10,... | collective-permute-start | bytes 442376 | tf_op jit(solution)/shard_map/ppermute | solution.py:273
  10.1 10.1 %collective-permute-start.2 = (bf16[24,3072]{1,0:T(8,128)(2,1)S(1)}, bf16[24,3072]{1,0:T(8,128)(2,1)S(1)}, u32[]{:S(2)}, u32[]{:S(2)}) collective-permute-start(bf16[24,3072]{1,0:T(8,128)(2,1)S(1)} %copy-done.3), channel_id=1, source_target_pairs={{0,6},{1,7},{2,4},{3,5},{4,2},{5,3},{6,0},{7,1},{8,14},{9,15},{10,... | collective-permute-start | bytes 442376 | tf_op jit(solution)/shard_map/ppermute | solution.py:273
  14.3 9.0 %collective-permute-start.4 = (bf16[48,1536]{1,0:T(8,128)(2,1)S(1)}, bf16[48,1536]{1,0:T(8,128)(2,1)S(1)}, u32[]{:S(2)}, u32[]{:S(2)}) collective-permute-start(bf16[48,1536]{1,0:T(8,128)(2,1)S(1)} %collective-permute-done.3.refs_8_), channel_id=1, source_target_pairs={{0,6},{1,7},{2,4},{3,5},{4,2},{5,3},{6,0},{7,1},{8,14},{9,15},{10,... | collective-permute-start | bytes 442376 | tf_op jit(solution)/shard_map/ppermute | solution.py:273
  16.1 9.1 %collective-permute-start.9 = (bf16[48,1536]{1,0:T(8,128)(2,1)S(1)}, bf16[48,1536]{1,0:T(8,128)(2,1)S(1)}, u32[]{:S(2)}, u32[]{:S(2)}) collective-permute-start(bf16[48,1536]{1,0:T(8,128)(2,1)S(1)} %collective-permute-done.3.refs_8_), channel_id=1, source_target_pairs={{0,2},{1,3},{2,0},{3,1},{4,6},{5,7},{6,4},{7,5},{8,10},{9,11},{10,... | collective-permute-start | bytes 442376 | tf_op jit(solution)/shard_map/ppermute | solution.py:273
  16.6 8.6 %collective-permute-start.10 = (bf16[48,1536]{1,0:T(8,128)(2,1)S(1)}, bf16[48,1536]{1,0:T(8,128)(2,1)S(1)}, u32[]{:S(2)}, u32[]{:S(2)}) collective-permute-start(bf16[48,1536]{1,0:T(8,128)(2,1)S(1)} %collective-permute-done.3.refs_8_), channel_id=1, source_target_pairs={{0,4},{1,5},{2,6},{3,7},{4,0},{5,1},{6,2},{7,3},{8,12},{9,13},{10,... | collective-permute-start | bytes 442376 | tf_op jit(solution)/shard_map/ppermute | solution.py:273
  17.8 7.8 %collective-permute-start.11 = (bf16[48,1536]{1,0:T(8,128)(2,1)S(1)}, bf16[48,1536]{1,0:T(8,128)(2,1)S(1)}, u32[]{:S(2)}, u32[]{:S(2)}) collective-permute-start(bf16[48,1536]{1,0:T(8,128)(2,1)S(1)} %collective-permute-done.3.refs_8_), channel_id=1, source_target_pairs={{0,1},{1,0},{2,3},{3,2},{4,5},{5,4},{6,7},{7,6},{8,9},{9,8},{10,11... | collective-permute-start | bytes 442376 | tf_op jit(solution)/shard_map/ppermute | solution.py:273
  23.3 2.5 %collective-permute-start.14 = (bf16[48,1536]{1,0:T(8,128)(2,1)S(1)}, bf16[48,1536]{1,0:T(8,128)(2,1)S(1)}, u32[]{:S(2)}, u32[]{:S(2)}) collective-permute-start(bf16[48,1536]{1,0:T(8,128)(2,1)S(1)} %collective-permute-done.4.refs_11_), channel_id=1, source_target_pairs={{0,1},{1,0},{2,3},{3,2},{4,5},{5,4},{6,7},{7,6},{8,9},{9,8},{10,11... | collective-permute-start | bytes 442376 | tf_op jit(solution)/shard_map/ppermute | solution.py:273
  23.3 2.9 %collective-permute-start.5 = (bf16[24,3072]{1,0:T(8,128)(2,1)S(1)}, bf16[24,3072]{1,0:T(8,128)(2,1)S(1)}, u32[]{:S(2)}, u32[]{:S(2)}) collective-permute-start(bf16[24,3072]{1,0:T(8,128)(2,1)S(1)} %copy-done.3), channel_id=1, source_target_pairs={{0,1},{1,0},{2,3},{3,2},{4,5},{5,4},{6,7},{7,6},{8,9},{9,8},{10,11... | collective-permute-start | bytes 442376 | tf_op jit(solution)/shard_map/ppermute | solution.py:273
  25.1 1.4 %collective-permute-start.6 = (bf16[24,3072]{1,0:T(8,128)(2,1)S(1)}, bf16[24,3072]{1,0:T(8,128)(2,1)S(1)}, u32[]{:S(2)}, u32[]{:S(2)}) collective-permute-start(bf16[24,3072]{1,0:T(8,128)(2,1)S(1)} %collective-permute-done.refs_1_), channel_id=1, source_target_pairs={{0,1},{1,0},{2,3},{3,2},{4,5},{5,4},{6,7},{7,6},{8,9},{9,8},{10,11... | collective-permute-start | bytes 442376 | tf_op jit(solution)/shard_map/ppermute | solution.py:273
  25.2 1.6 %collective-permute-start.7 = (bf16[24,3072]{1,0:T(8,128)(2,1)S(1)}, bf16[24,3072]{1,0:T(8,128)(2,1)S(1)}, u32[]{:S(2)}, u32[]{:S(2)}) collective-permute-start(bf16[24,3072]{1,0:T(8,128)(2,1)S(1)} %collective-permute-done.1.refs_2_), channel_id=1, source_target_pairs={{0,1},{1,0},{2,3},{3,2},{4,5},{5,4},{6,7},{7,6},{8,9},{9,8},{10,11... | collective-permute-start | bytes 442376 | tf_op jit(solution)/shard_map/ppermute | solution.py:273
  25.7 1.4 %collective-permute-start.8 = (bf16[24,3072]{1,0:T(8,128)(2,1)S(1)}, bf16[24,3072]{1,0:T(8,128)(2,1)S(1)}, u32[]{:S(2)}, u32[]{:S(2)}) collective-permute-start(bf16[24,3072]{1,0:T(8,128)(2,1)S(1)} %collective-permute-done.2.refs_3_), channel_id=1, source_target_pairs={{0,1},{1,0},{2,3},{3,2},{4,5},{5,4},{6,7},{7,6},{8,9},{9,8},{10,11... | collective-permute-start | bytes 442376 | tf_op jit(solution)/shard_map/ppermute | solution.py:273
  25.7 1.5 %collective-permute-start.12 = (bf16[48,1536]{1,0:T(8,128)(2,1)S(1)}, bf16[48,1536]{1,0:T(8,128)(2,1)S(1)}, u32[]{:S(2)}, u32[]{:S(2)}) collective-permute-start(bf16[48,1536]{1,0:T(8,128)(2,1)S(1)} %collective-permute-done.9.refs_9_), channel_id=1, source_target_pairs={{0,1},{1,0},{2,3},{3,2},{4,5},{5,4},{6,7},{7,6},{8,9},{9,8},{10,11... | collective-permute-start | bytes 442376 | tf_op jit(solution)/shard_map/ppermute | solution.py:273
  26.2 1.4 %collective-permute-start.13 = (bf16[48,1536]{1,0:T(8,128)(2,1)S(1)}, bf16[48,1536]{1,0:T(8,128)(2,1)S(1)}, u32[]{:S(2)}, u32[]{:S(2)}) collective-permute-start(bf16[48,1536]{1,0:T(8,128)(2,1)S(1)} %collective-permute-done.10.refs_10_), channel_id=1, source_target_pairs={{0,1},{1,0},{2,3},{3,2},{4,5},{5,4},{6,7},{7,6},{8,9},{9,8},{10,11... | collective-permute-start | bytes 442376 | tf_op jit(solution)/shard_map/ppermute | solution.py:273
  27.6 2.6 %copy-start.2 = (bf16[672,3072]{1,0:T(8,128)(2,1)S(1)}, bf16[672,3072]{1,0:T(8,128)(2,1)}, u32[]{:S(2)}) copy-start(bf16[672,3072]{1,0:T(8,128)(2,1)} %refs_21_.1) | copy-start | bytes 12386308
  30.2 17.6 %copy-start.5 = (f32[48,64]{1,0:T(8,128)S(1)}, f32[48,64]{1,0:T(8,128)}, u32[]{:S(2)}) copy-start(f32[48,64]{1,0:T(8,128)} %get-tuple-element.35.weight_ref) | copy-start | bytes 36868
  30.2 21.3 %copy-start.4 = (f32[48,64]{1,0:T(8,128)S(1)}, f32[48,64]{1,0:T(8,128)}, u32[]{:S(2)}) copy-start(f32[48,64]{1,0:T(8,128)} %get-tuple-element.34.place_ref) | copy-start | bytes 36868
  30.2 21.3 %copy-start.6 = (s32[4,64]{1,0:T(4,128)S(1)}, s32[4,64]{1,0:T(4,128)}, u32[]{:S(2)}) copy-start(s32[4,64]{1,0:T(4,128)} %get-tuple-element.33.ids_ref) | copy-start | bytes 3076
  34.3 2.1 %collective-permute-start.15 = (bf16[192,1664]{1,0:T(8,128)(2,1)S(1)}, bf16[192,1664]{1,0:T(8,128)(2,1)S(1)}, u32[]{:S(2)}, u32[]{:S(2)}) collective-permute-start(bf16[192,1664]{1,0:T(8,128)(2,1)S(1)} %get-tuple-element.53), channel_id=1, source_target_pairs={{0,1},{1,0},{2,3},{3,2},{4,5},{5,4},{6,7},{7,6},{8,9},{9,8},{10,11... | collective-permute-start | bytes 1916936 | tf_op jit(solution)/shard_map/ppermute | solution.py:273
  36.7 5.4 %collective-permute-start.16 = (bf16[24,1664]{1,0:T(8,128)(2,1)S(1)}, bf16[24,1664]{1,0:T(8,128)(2,1)S(1)}, u32[]{:S(2)}, u32[]{:S(2)}) collective-permute-start(bf16[24,1664]{1,0:T(8,128)(2,1)S(1)} %get-tuple-element.55), channel_id=1, source_target_pairs={{0,2},{1,3},{2,0},{3,1},{4,6},{5,7},{6,4},{7,5},{8,10},{9,11},{10,... | collective-permute-start | bytes 239624 | tf_op jit(solution)/shard_map/ppermute | solution.py:273
  38.2 5.6 %collective-permute-start.17 = (bf16[24,1664]{1,0:T(8,128)(2,1)S(1)}, bf16[24,1664]{1,0:T(8,128)(2,1)S(1)}, u32[]{:S(2)}, u32[]{:S(2)}) collective-permute-start(bf16[24,1664]{1,0:T(8,128)(2,1)S(1)} %get-tuple-element.56), channel_id=1, source_target_pairs={{0,4},{1,5},{2,6},{3,7},{4,0},{5,1},{6,2},{7,3},{8,12},{9,13},{10,... | collective-permute-start | bytes 239624 | tf_op jit(solution)/shard_map/ppermute | solution.py:273
  38.6 6.5 %collective-permute-start.18 = (bf16[24,1664]{1,0:T(8,128)(2,1)S(1)}, bf16[24,1664]{1,0:T(8,128)(2,1)S(1)}, u32[]{:S(2)}, u32[]{:S(2)}) collective-permute-start(bf16[24,1664]{1,0:T(8,128)(2,1)S(1)} %get-tuple-element.57), channel_id=1, source_target_pairs={{0,6},{1,7},{2,4},{3,5},{4,2},{5,3},{6,0},{7,1},{8,14},{9,15},{10,... | collective-permute-start | bytes 239624 | tf_op jit(solution)/shard_map/ppermute | solution.py:273
  40.3 7.6 %collective-permute-start.20 = (bf16[24,1664]{1,0:T(8,128)(2,1)S(1)}, bf16[24,1664]{1,0:T(8,128)(2,1)S(1)}, u32[]{:S(2)}, u32[]{:S(2)}) collective-permute-start(bf16[24,1664]{1,0:T(8,128)(2,1)S(1)} %get-tuple-element.59), channel_id=1, source_target_pairs={{0,2},{1,3},{2,0},{3,1},{4,6},{5,7},{6,4},{7,5},{8,10},{9,11},{10,... | collective-permute-start | bytes 239624 | tf_op jit(solution)/shard_map/ppermute | solution.py:273
  41.7 6.2 %collective-permute-start.21 = (bf16[24,1664]{1,0:T(8,128)(2,1)S(1)}, bf16[24,1664]{1,0:T(8,128)(2,1)S(1)}, u32[]{:S(2)}, u32[]{:S(2)}) collective-permute-start(bf16[24,1664]{1,0:T(8,128)(2,1)S(1)} %get-tuple-element.60), channel_id=1, source_target_pairs={{0,4},{1,5},{2,6},{3,7},{4,0},{5,1},{6,2},{7,3},{8,12},{9,13},{10,... | collective-permute-start | bytes 239624 | tf_op jit(solution)/shard_map/ppermute | solution.py:273
  42.1 5.8 %collective-permute-start.22 = (bf16[24,1664]{1,0:T(8,128)(2,1)S(1)}, bf16[24,1664]{1,0:T(8,128)(2,1)S(1)}, u32[]{:S(2)}, u32[]{:S(2)}) collective-permute-start(bf16[24,1664]{1,0:T(8,128)(2,1)S(1)} %get-tuple-element.61), channel_id=1, source_target_pairs={{0,6},{1,7},{2,4},{3,5},{4,2},{5,3},{6,0},{7,1},{8,14},{9,15},{10,... | collective-permute-start | bytes 239624 | tf_op jit(solution)/shard_map/ppermute | solution.py:273
  45.3 6.2 %collective-permute-start.19 = (bf16[24,1664]{1,0:T(8,128)(2,1)S(1)}, bf16[24,1664]{1,0:T(8,128)(2,1)S(1)}, u32[]{:S(2)}, u32[]{:S(2)}) collective-permute-start(bf16[24,1664]{1,0:T(8,128)(2,1)S(1)} %other.1), channel_id=1, source_target_pairs={{0,8},{1,9},{2,10},{3,11},{4,12},{5,13},{6,14},{7,15},{8,0},{9,1},... | collective-permute-start | bytes 239624 | tf_op jit(solution)/shard_map/ppermute | solution.py:273

commit v3 on v2

--- a/solution.py
+++ b/solution.py
@@ -92,17 +92,18 @@
     return high, x - high
 
 
-def layout_kernel(weight_ref, left_ref, right_ref):
+def layout_kernel(weight_ref, *out_refs):
     weight = weight_ref[...]
-    own_high, own_low = split_two(weight[:PAIR])
-    other_high, other_low = split_two(weight[PAIR:])
-    rest = jnp.zeros((LANES - 5 * PAIR, weight.shape[1]), F32)
-    table = jnp.concatenate([other_high, other_low, own_high, own_low, own_high, rest], axis=0)
-    row = lax.broadcasted_iota(jnp.int32, table.shape, 0)
-    block = sum((row >= PAIR * i).astype(jnp.int32) for i in range(1, 6))
-    first = row - PAIR * block < CAP
-    left_ref[...] = jnp.where(first, table, 0.0).T.astype(BF16)
-    right_ref[...] = jnp.where(first, 0.0, table).T.astype(BF16)
+    for i, (part, lows) in enumerate(((weight[:PAIR], 1), (weight[PAIR:], 0))):
+        high, low = split_two(part)
+        parts = [high, low] + [high] * lows
+        rest = jnp.zeros((LANES - PAIR * len(parts), weight.shape[1]), F32)
+        table = jnp.concatenate([*parts, rest], axis=0)
+        row = lax.broadcasted_iota(jnp.int32, table.shape, 0)
+        block = sum((row >= PAIR * j).astype(jnp.int32) for j in range(1, len(parts) + 1))
+        first = row - PAIR * block < CAP
+        out_refs[2 * i][...] = jnp.where(first, table, 0.0).T.astype(BF16)
+        out_refs[2 * i + 1][...] = jnp.where(first, 0.0, table).T.astype(BF16)
 
 
 def gate_kernel(*refs):
@@ -172,7 +173,7 @@
 def backward_kernel(blocks, *refs):
     own_refs, other_refs = refs[:blocks], refs[blocks : 2 * blocks]
     slope_ref, active_ref, hidden_ref, wg_ref, wu_ref, wd_ref = refs[2 * blocks : 2 * blocks + 6]
-    keep_ref, send_ref, left_ref, right_ref = refs[2 * blocks + 6 :]
+    out_refs, left_ref, right_ref = refs[2 * blocks + 6 : -2], *refs[-2:]
     half = left_ref.shape[1]
     halves(own_refs, slice(PAIR - ROWS, PAIR), other_refs, PAIR, left_ref, right_ref)
     split = ROWS * blocks
@@ -184,12 +185,9 @@
     grads = (dh * slope_ref[...], dh * active_ref[...])
 
     def put(to, left, right):
-        for i in range(2):
-            mine = slice(split * i, split * i + split // 2)
-            theirs = slice(split * i + split // 2, split * (i + 1))
-            rows = slice(PAIR * blocks // 2 * i, PAIR * blocks // 2 * (i + 1))
-            keep_ref[rows, to] = weave(left[mine], right[mine], blocks // 2).astype(BF16)
-            send_ref[rows, to] = weave(left[theirs], right[theirs], blocks // 2).astype(BF16)
+        for i, ref in enumerate(out_refs):
+            part = slice(split // 2 * i, split // 2 * (i + 1))
+            ref[:, to] = weave(left[part], right[part], blocks // 2).astype(BF16)
 
     def back(pair, cols):
         return jnp.dot(pair[0], wg_ref[:, cols], preferred_element_type=F32) + jnp.dot(
@@ -234,19 +232,30 @@
     refs[-1][...] = packed(total_of(refs[:-1]))
 
 
-def final_kernel(sources, mine_ref, ids_ref, place_ref, left_ref, right_ref, back_ref, *refs):
-    own = total_of(refs[:sources])
-    grad_ref, gate_ref = refs[sources:]
-    back = back_ref[...]
+def weighted(tables, parts):
+    rest = jnp.zeros((LANES - PAIR * len(parts), parts[0].shape[1]), F32)
+    rows = jnp.concatenate([*parts, rest], axis=0).astype(BF16)
+    return [jnp.dot(ref[...], rows, preferred_element_type=F32) for ref in tables]
+
+
+def own_kernel(left_ref, right_ref, *refs):
+    grad_ref, tail_ref = refs[-2:]
+    own = total_of(refs[:-2])
     half = own.shape[1] - LANES
-    own_high, own_low = split_two(own[:, :half])
-    other = back[:, :half].astype(F32)
-    rest = jnp.zeros((LANES - 5 * PAIR, half), F32)
-    table = jnp.concatenate([other, other, own_high, own_high, own_low, rest], axis=0).astype(BF16)
-    for i, ref in enumerate((left_ref, right_ref)):
-        out = jnp.dot(ref[...], table, preferred_element_type=F32)
-        grad_ref[:, half * i : half * (i + 1)] = out.astype(BF16)
-    tail = jnp.concatenate([own[:, half:], back[:, half:].astype(F32)], axis=0)
+    high, low = split_two(own[:, :half])
+    for i, out in enumerate(weighted((left_ref, right_ref), (high, high, low))):
+        grad_ref[:, half * i : half * (i + 1)] = out
+    tail_ref[...] = own[:, half:]
+
+
+def final_kernel(mine_ref, ids_ref, place_ref, left_ref, right_ref, own_ref, tail_ref, back_ref, grad_ref, gate_ref):
+    back = back_ref[...].astype(F32)
+    half = back.shape[1] - LANES
+    other = back[:, :half]
+    for i, out in enumerate(weighted((left_ref, right_ref), (other, other))):
+        cols = slice(half * i, half * (i + 1))
+        grad_ref[:, cols] = (own_ref[:, cols] + out).astype(BF16)
+    tail = jnp.concatenate([tail_ref[...], back[:, half:]], axis=0)
     score = (tail[:, 0:1] + tail[:, 1:2]) * place_ref[...]
     mine = mine_ref[0]
     ids = ids_ref[...]
@@ -260,7 +269,7 @@
 def per_device(tokens, cotangent, gate_weights, expert_ids, w_gate, w_up, w_down):
     devices = lax.axis_size("expert")
     split = devices // EXP_WIN
-    evens = range(2, split, 2)
+    evens = list(range(split - 2, 0, -2))
     width = tokens.shape[1]
     units = w_down.shape[0]
     count = tokens.shape[0]
@@ -288,10 +297,10 @@
         limit=PICK_LIMIT,
     )
     weights = (w_gate.T, w_up.T, w_down)
-    left, right = call(
+    *own_weight, left, right = call(
         layout_kernel,
         "layout",
-        [struct((count, LANES), BF16)] * 2,
+        [struct((count, LANES), BF16)] * 4,
         [VMEM],
         (weight,),
     )
@@ -315,7 +324,8 @@
     other, token = together((other, token))
     own = near(own)
     other = near(other)
-    own, other[-1] = together((own, other[-1]))
+    own, token = together((own, gate(token)))
+    other, token = together((other, token))
     own = both_cores(own)
     other = both_cores(other)
     states = call(
@@ -328,35 +338,44 @@
         flops=4 * rows * width * units,
         limit=24,
     )
-    keep, send = call(
+    own_keep, own_send, keep, send = call(
         functools.partial(backward_kernel, split),
         "backward",
-        [struct((PAIR * split, wide), BF16)] * 2,
+        [struct((PAIR * split // 2, wide), BF16)] * 4,
         [VMEM] * (2 * split + 6),
         (*own, *other, *states, *weights),
         stacked,
         flops=6 * rows * width * units,
         limit=24,
     )
-    got = swap(send, 1)
     kinds = [struct((PAIR, wide), F32)] + [struct((PAIR, wide), BF16)] * len(evens)
-    sums = call(chip_kernel, "chip", kinds * 2, [VMEM] * 2, (keep, got))
+
+    def chip_sums(keep, got):
+        return call(chip_kernel, "chip", kinds, [VMEM] * 2, (keep, got))
 
     def returned(sums):
-        return [sums[0]] + [swap(s, k) for s, k in zip(sums[1:], evens)]
-
-    cross_back = returned(sums[len(kinds) :])
-    own_back = returned(sums[: len(kinds)])
+        return [sums[0]] + [swap(x, k) for x, k in zip(sums[1:], evens)]
+
+    got, own_got = swap(send, 1), swap(own_send, 1)
+    cross_back = returned(chip_sums(keep, got))
+    own_back = returned(chip_sums(own_keep, own_got))
     (cross_total,) = call(
         other_kernel, "other", [struct((PAIR, wide), BF16)], [VMEM] * len(cross_back), tuple(cross_back)
     )
     back = swap(cross_total, split)
+    own_part = call(
+        own_kernel,
+        "own",
+        [struct((count, width), F32), struct((PAIR, LANES), F32)],
+        [VMEM] * (2 + len(own_back)),
+        (*own_weight, *own_back),
+    )
     grad, gate_grad = call(
-        functools.partial(final_kernel, len(own_back)),
+        final_kernel,
         "final",
         [struct((count, width), BF16), struct(ids.shape, F32)],
-        [SMEM] + [VMEM] * (5 + len(own_back)),
-        (mine, ids, place, left, right, back, *own_back),
+        [SMEM] + [VMEM] * 7,
+        (mine, ids, place, left, right, *own_part, back),
     )
     return (grad, gate_grad.T)
 

time: 52.7 us -> 50.1 us (0.951)
  waiting for transfers between devices: 18.8 us -> 16.1 us
    ppermute x23 -> x24, waiting for transfers between devices: 18.8 us -> 16.1 us  [swap(): return lax.ppermute(x, 'expert', [(i, i ^ offset) for i in range(devices)])]
    pallas_call x8 -> x11, Pallas kernels: 10.5 us -> 10.8 us  [call(): pl.pallas_call(kernel, name=name, out_shape=out_shape, in_specs=in_specs,...]
    ppermute x23 -> x24, starting transfers between devices: 22.5 us -> 22.2 us  [swap(): return lax.ppermute(x, 'expert', [(i, i ^ offset) for i in range(devices)])]
  transfers between devices with their start and end apart: 23 -> 24, of which waited for: 12 -> 15; matrix products, arithmetic and copies ran while one was open for 0% -> 0% of each run, Pallas kernels for 0% -> 2%
where the time goes in v3:
time: 50.1 us; the launch traced here: 49.9 us
  starting transfers between devices  22.2 us (44%)
  waiting for transfers between devices  16.1 us (32%)
  Pallas kernels  10.8 us (22%)
  between operations  0.78 us (2%)
    ppermute x24, starting transfers between devices, swap(): return lax.ppermute(x, 'expert', [(i, i ^ offset) for i in range(devices)])  22.2 us
    ppermute x24, waiting for transfers between devices, swap(): return lax.ppermute(x, 'expert', [(i, i ^ offset) for i in range(devices)])  16.1 us
    pallas_call x11, Pallas kernels, call(): pl.pallas_call(kernel, name=name, out_shape=out_shape, in_specs=in_specs,...  10.8 us
  transfers between devices with their start and end apart: 24, of which 15 were waited for; matrix products, arithmetic and copies ran while one was open for 0% of the time, Pallas kernels for 2%

profile of v3, /device:TPU:0, one launch (start us, length us, event | category | flops | bytes accessed | tf_op | source)
XLA Modules:
  0.0 49.9 jit_solution(13391680580586187127)
XLA Ops:
  0.6 2.2 %pick.1 = (bf16[24,3072]{1,0:T(8,128)(2,1)}, bf16[48,1536]{1,0:T(8,128)(2,1)}, s32[4,64]{1,0:T(4,128)}, f32[48,64]{1,0:T(8,128)}, f32[48,64]{1,0:T(8,128)}) custom-call(s32[1]{0:T(128)} %bitcast.mine_ref, s32[4,64]{1,0:T(4,128)} %bitcast.10, f32[4,64]{1,0:T(4,128)} %bitcast.11, bf16[64,3072]{1,0:T(8,128)(2,1)} %tok_hbm.1, bf16[64,3072]{1,0:T(8,128)(2,1)} %cot_hbm.1), custom_call_target="tpu_custom_call" | custom-call | flops 37748736 | bytes 1108996 | tf_op jit(solution)/shard_map/pick/pallas_call | solution.py:28
  2.9 0.0 copy-start.3
  2.9 4.1 %collective-permute-start.3 = (bf16[48,1536]{1,0:T(8,128)(2,1)}, bf16[48,1536]{1,0:T(8,128)(2,1)S(1)}, u32[]{:S(2)}, u32[]{:S(2)}) collective-permute-start(bf16[48,1536]{1,0:T(8,128)(2,1)} %get-tuple-element.53), channel_id=1, source_target_pairs={{0,8},{1,9},{2,10},{3,11},{4,12},{5,13},{6,14},{7,15},{8,0},{9,1},... | collective-permute-start | bytes 442376 | tf_op jit(solution)/shard_map/ppermute | solution.py:282
  7.0 2.6 %collective-permute-start = (bf16[24,3072]{1,0:T(8,128)(2,1)S(1)}, bf16[24,3072]{1,0:T(8,128)(2,1)S(1)}, u32[]{:S(2)}, u32[]{:S(2)}) collective-permute-start(bf16[24,3072]{1,0:T(8,128)(2,1)S(1)} %copy-done.3), channel_id=1, source_target_pairs={{0,6},{1,7},{2,4},{3,5},{4,2},{5,3},{6,0},{7,1},{8,14},{9,15},{10,... | collective-permute-start | bytes 442376 | tf_op jit(solution)/shard_map/ppermute | solution.py:282
  9.6 0.4 collective-permute-start.1
  10.0 0.5 %collective-permute-start.2 = (bf16[24,3072]{1,0:T(8,128)(2,1)S(1)}, bf16[24,3072]{1,0:T(8,128)(2,1)S(1)}, u32[]{:S(2)}, u32[]{:S(2)}) collective-permute-start(bf16[24,3072]{1,0:T(8,128)(2,1)S(1)} %copy-done.3), channel_id=1, source_target_pairs={{0,2},{1,3},{2,0},{3,1},{4,6},{5,7},{6,4},{7,5},{8,10},{9,11},{10,... | collective-permute-start | bytes 442376 | tf_op jit(solution)/shard_map/ppermute | solution.py:282
  10.5 3.7 %collective-permute-done.3.refs_8_ = bf16[48,1536]{1,0:T(8,128)(2,1)S(1)} collective-permute-done((bf16[48,1536]{1,0:T(8,128)(2,1)}, bf16[48,1536]{1,0:T(8,128)(2,1)S(1)}, u32[]{:S(2)}, u32[]{:S(2)}) %collective-permute-start.3) | collective-permute-done | bytes 147488 | tf_op jit(solution)/shard_map/ppermute | solution.py:282
  14.3 1.6 %collective-permute-start.10 = (bf16[48,1536]{1,0:T(8,128)(2,1)S(1)}, bf16[48,1536]{1,0:T(8,128)(2,1)S(1)}, u32[]{:S(2)}, u32[]{:S(2)}) collective-permute-start(bf16[48,1536]{1,0:T(8,128)(2,1)S(1)} %collective-permute-done.3.refs_8_), channel_id=1, source_target_pairs={{0,2},{1,3},{2,0},{3,1},{4,6},{5,7},{6,4},{7,5},{8,10},{9,11},{10,... | collective-permute-start | bytes 442376 | tf_op jit(solution)/shard_map/ppermute | solution.py:282
  15.9 0.7 %collective-permute-start.8 = (bf16[48,1536]{1,0:T(8,128)(2,1)S(1)}, bf16[48,1536]{1,0:T(8,128)(2,1)S(1)}, u32[]{:S(2)}, u32[]{:S(2)}) collective-permute-start(bf16[48,1536]{1,0:T(8,128)(2,1)S(1)} %collective-permute-done.3.refs_8_), channel_id=1, source_target_pairs={{0,6},{1,7},{2,4},{3,5},{4,2},{5,3},{6,0},{7,1},{8,14},{9,15},{10,... | collective-permute-start | bytes 442376 | tf_op jit(solution)/shard_map/ppermute | solution.py:282
  16.5 0.2 collective-permute-done.refs_1_
  16.8 1.3 %collective-permute-start.9 = (bf16[48,1536]{1,0:T(8,128)(2,1)S(1)}, bf16[48,1536]{1,0:T(8,128)(2,1)S(1)}, u32[]{:S(2)}, u32[]{:S(2)}) collective-permute-start(bf16[48,1536]{1,0:T(8,128)(2,1)S(1)} %collective-permute-done.3.refs_8_), channel_id=1, source_target_pairs={{0,4},{1,5},{2,6},{3,7},{4,0},{5,1},{6,2},{7,3},{8,12},{9,13},{10,... | collective-permute-start | bytes 442376 | tf_op jit(solution)/shard_map/ppermute | solution.py:282
  18.1 1.6 %collective-permute-done.1.refs_2_ = bf16[24,3072]{1,0:T(8,128)(2,1)S(1)} collective-permute-done((bf16[24,3072]{1,0:T(8,128)(2,1)S(1)}, bf16[24,3072]{1,0:T(8,128)(2,1)S(1)}, u32[]{:S(2)}, u32[]{:S(2)}) %collective-permute-start.1) | collective-permute-done | bytes 147488 | tf_op jit(solution)/shard_map/ppermute | solution.py:282
  19.6 0.0 collective-permute-done.2.refs_3_
  19.6 0.0 collective-permute-start.4
  19.6 0.5 %collective-permute-start.5 = (bf16[24,3072]{1,0:T(8,128)(2,1)S(1)}, bf16[24,3072]{1,0:T(8,128)(2,1)S(1)}, u32[]{:S(2)}, u32[]{:S(2)}) collective-permute-start(bf16[24,3072]{1,0:T(8,128)(2,1)S(1)} %collective-permute-done.refs_1_), channel_id=1, source_target_pairs={{0,1},{1,0},{2,3},{3,2},{4,5},{5,4},{6,7},{7,6},{8,9},{9,8},{10,11... | collective-permute-start | bytes 442376 | tf_op jit(solution)/shard_map/ppermute | solution.py:282
  20.1 1.8 %collective-permute-done.10.refs_11_ = bf16[48,1536]{1,0:T(8,128)(2,1)S(1)} collective-permute-done((bf16[48,1536]{1,0:T(8,128)(2,1)S(1)}, bf16[48,1536]{1,0:T(8,128)(2,1)S(1)}, u32[]{:S(2)}, u32[]{:S(2)}) %collective-permute-start.10) | collective-permute-done | bytes 147488 | tf_op jit(solution)/shard_map/ppermute | solution.py:282
  21.9 1.3 %collective-permute-done.8.refs_9_ = bf16[48,1536]{1,0:T(8,128)(2,1)S(1)} collective-permute-done((bf16[48,1536]{1,0:T(8,128)(2,1)S(1)}, bf16[48,1536]{1,0:T(8,128)(2,1)S(1)}, u32[]{:S(2)}, u32[]{:S(2)}) %collective-permute-start.8) | collective-permute-done | bytes 147488 | tf_op jit(solution)/shard_map/ppermute | solution.py:282
  23.3 1.5 %collective-permute-done.9.refs_10_ = bf16[48,1536]{1,0:T(8,128)(2,1)S(1)} collective-permute-done((bf16[48,1536]{1,0:T(8,128)(2,1)S(1)}, bf16[48,1536]{1,0:T(8,128)(2,1)S(1)}, u32[]{:S(2)}, u32[]{:S(2)}) %collective-permute-start.9) | collective-permute-done | bytes 147488 | tf_op jit(solution)/shard_map/ppermute | solution.py:282
  24.8 0.5 %collective-permute-start.12 = (bf16[48,1536]{1,0:T(8,128)(2,1)S(1)}, bf16[48,1536]{1,0:T(8,128)(2,1)S(1)}, u32[]{:S(2)}, u32[]{:S(2)}) collective-permute-start(bf16[48,1536]{1,0:T(8,128)(2,1)S(1)} %collective-permute-done.8.refs_9_), channel_id=1, source_target_pairs={{0,1},{1,0},{2,3},{3,2},{4,5},{5,4},{6,7},{7,6},{8,9},{9,8},{10,11... | collective-permute-start | bytes 442376 | tf_op jit(solution)/shard_map/ppermute | solution.py:282
  25.3 0.1 collective-permute-start.13
  25.4 0.4 collective-permute-start.14
  25.8 0.3 collective-permute-done.11.refs_12_
  26.2 0.2 collective-permute-done.12.refs_13_
  26.4 0.3 collective-permute-done.13.refs_14_
  26.7 0.2 collective-permute-done.14.refs_15_
  26.9 2.6 %forward.1 = (f32[672,256]{1,0:T(8,128)S(1)}, f32[672,256]{1,0:T(8,128)S(1)}, bf16[672,256]{1,0:T(8,128)(2,1)S(1)}) custom-call(bf16[24,3072]{1,0:T(8,128)(2,1)S(1)} %copy-done.3, bf16[24,3072]{1,0:T(8,128)(2,1)S(1)} %collective-permute-done.refs_1_, bf16[24,3072]{1,0:T(8,128)(2,1)S(1)} %collective-permute-done.1.refs_2_, ...), custom_call_target="tpu_custom_call" | custom-call | flops 2113929216 | bytes 12341248 | tf_op jit(solution)/shard_map/forward/pallas_call | solution.py:28
  29.6 0.0 copy-start.6
  29.6 4.1 %backward.1 = (bf16[96,1664]{1,0:T(8,128)(2,1)S(1)}, bf16[96,1664]{1,0:T(8,128)(2,1)S(1)}, bf16[96,1664]{1,0:T(8,128)(2,1)S(1)}, bf16[96,1664]{1,0:T(8,128)(2,1)S(1)}) custom-call(bf16[24,3072]{1,0:T(8,128)(2,1)S(1)} %copy-done.3, bf16[24,3072]{1,0:T(8,128)(2,1)S(1)} %collective-permute-done.refs_1_, bf16[24,3072]{1,0:T(8,128)(2,1)S(1)} %collective-permute-done.1.refs_2_, ...), custom_call_target="tpu_custom_call" | custom-call | flops 3170893824 | bytes 17743872 | tf_op jit(solution)/shard_map/backward/pallas_call | solution.py:28
  33.7 0.3 collective-permute-start.19
  34.1 0.2 collective-permute-start.15
  34.3 1.1 %collective-permute-done.19.got_ref = bf16[96,1664]{1,0:T(8,128)(2,1)S(1)} collective-permute-done((bf16[96,1664]{1,0:T(8,128)(2,1)S(1)}, bf16[96,1664]{1,0:T(8,128)(2,1)S(1)}, u32[]{:S(2)}, u32[]{:S(2)}) %collective-permute-start.19) | collective-permute-done | bytes 319520 | tf_op jit(solution)/shard_map/ppermute | solution.py:282
  35.4 0.2 chip.3
  35.6 1.7 %collective-permute-start.20 = (bf16[24,1664]{1,0:T(8,128)(2,1)S(1)}, bf16[24,1664]{1,0:T(8,128)(2,1)S(1)}, u32[]{:S(2)}, u32[]{:S(2)}) collective-permute-start(bf16[24,1664]{1,0:T(8,128)(2,1)S(1)} %get-tuple-element.81), channel_id=1, source_target_pairs={{0,6},{1,7},{2,4},{3,5},{4,2},{5,3},{6,0},{7,1},{8,14},{9,15},{10,... | collective-permute-start | bytes 239624 | tf_op jit(solution)/shard_map/ppermute | solution.py:282
  37.3 0.4 collective-permute-start.21
  37.7 1.4 %collective-permute-start.22 = (bf16[24,1664]{1,0:T(8,128)(2,1)S(1)}, bf16[24,1664]{1,0:T(8,128)(2,1)S(1)}, u32[]{:S(2)}, u32[]{:S(2)}) collective-permute-start(bf16[24,1664]{1,0:T(8,128)(2,1)S(1)} %get-tuple-element.83), channel_id=1, source_target_pairs={{0,2},{1,3},{2,0},{3,1},{4,6},{5,7},{6,4},{7,5},{8,10},{9,11},{10,... | collective-permute-start | bytes 239624 | tf_op jit(solution)/shard_map/ppermute | solution.py:282
  39.1 0.2 chip.2
  39.3 1.7 %collective-permute-start.16 = (bf16[24,1664]{1,0:T(8,128)(2,1)S(1)}, bf16[24,1664]{1,0:T(8,128)(2,1)S(1)}, u32[]{:S(2)}, u32[]{:S(2)}) collective-permute-start(bf16[24,1664]{1,0:T(8,128)(2,1)S(1)} %get-tuple-element.73), channel_id=1, source_target_pairs={{0,6},{1,7},{2,4},{3,5},{4,2},{5,3},{6,0},{7,1},{8,14},{9,15},{10,... | collective-permute-start | bytes 239624 | tf_op jit(solution)/shard_map/ppermute | solution.py:282
  41.0 0.4 collective-permute-start.17
  41.4 0.4 collective-permute-done.20.refs_1_
  41.8 1.1 %collective-permute-start.18 = (bf16[24,1664]{1,0:T(8,128)(2,1)S(1)}, bf16[24,1664]{1,0:T(8,128)(2,1)S(1)}, u32[]{:S(2)}, u32[]{:S(2)}) collective-permute-start(bf16[24,1664]{1,0:T(8,128)(2,1)S(1)} %get-tuple-element.75), channel_id=1, source_target_pairs={{0,2},{1,3},{2,0},{3,1},{4,6},{5,7},{6,4},{7,5},{8,10},{9,11},{10,... | collective-permute-start | bytes 239624 | tf_op jit(solution)/shard_map/ppermute | solution.py:282
  42.8 0.5 collective-permute-done.22.refs_3_
  43.3 0.2 other.1
  43.5 2.2 %collective-permute-start.23 = (bf16[24,1664]{1,0:T(8,128)(2,1)S(1)}, bf16[24,1664]{1,0:T(8,128)(2,1)S(1)}, u32[]{:S(2)}, u32[]{:S(2)}) collective-permute-start(bf16[24,1664]{1,0:T(8,128)(2,1)S(1)} %other.1), channel_id=1, source_target_pairs={{0,8},{1,9},{2,10},{3,11},{4,12},{5,13},{6,14},{7,15},{8,0},{9,1},... | collective-permute-start | bytes 239624 | tf_op jit(solution)/shard_map/ppermute | solution.py:282
  45.6 0.1 layout.1
  45.8 0.5 collective-permute-done.18.refs_3_
  46.2 0.3 own.1
  46.5 2.4 %collective-permute-done.23.back_ref = bf16[24,1664]{1,0:T(8,128)(2,1)S(1)} collective-permute-done((bf16[24,1664]{1,0:T(8,128)(2,1)S(1)}, bf16[24,1664]{1,0:T(8,128)(2,1)S(1)}, u32[]{:S(2)}, u32[]{:S(2)}) %collective-permute-start.23) | collective-permute-done | bytes 79904 | tf_op jit(solution)/shard_map/ppermute | solution.py:282
  48.9 1.0 %final.1 = (bf16[64,3072]{1,0:T(8,128)(2,1)}, f32[4,64]{1,0:T(4,128)}) custom-call(s32[1]{0:T(128)} %bitcast.mine_ref, s32[4,64]{1,0:T(4,128)S(1)} %copy-done.6, f32[48,64]{1,0:T(8,128)S(1)} %copy-done.5, bf16[64,128]{1,0:T(8,128)(2,1)S(1)} %get-tuple-element.47.left_ref, bf16[64,128]{1,0:T(8,128)(2,1)S(1)} %get-tuple-element.48.right_ref, ...), custom_call_target="tpu_custom_call" | custom-call | bytes 1318916 | tf_op jit(solution)/shard_map/final/pallas_call | solution.py:28
  (25 shorter events, 0.1 us)
Async XLA Ops:
  2.9 4.1 %copy-start.3 = (bf16[24,3072]{1,0:T(8,128)(2,1)S(1)}, bf16[24,3072]{1,0:T(8,128)(2,1)}, u32[]{:S(2)}) copy-start(bf16[24,3072]{1,0:T(8,128)(2,1)} %get-tuple-element.56.refs_0_) | copy-start | bytes 442372
  2.9 11.4 %collective-permute-start.3 = (bf16[48,1536]{1,0:T(8,128)(2,1)}, bf16[48,1536]{1,0:T(8,128)(2,1)S(1)}, u32[]{:S(2)}, u32[]{:S(2)}) collective-permute-start(bf16[48,1536]{1,0:T(8,128)(2,1)} %get-tuple-element.53), channel_id=1, source_target_pairs={{0,8},{1,9},{2,10},{3,11},{4,12},{5,13},{6,14},{7,15},{8,0},{9,1},... | collective-permute-start | bytes 442376 | tf_op jit(solution)/shard_map/ppermute | solution.py:282
  7.0 19.9 %copy-start = (bf16[3072,672]{0,1:T(8,128)(2,1)S(1)}, bf16[3072,672]{0,1:T(8,128)(2,1)}, u32[]{:S(2)}) copy-start(bf16[3072,672]{0,1:T(8,128)(2,1)} %param.11) | copy-start | bytes 12386308
  7.0 19.9 %copy-start.1 = (bf16[3072,672]{0,1:T(8,128)(2,1)S(1)}, bf16[3072,672]{0,1:T(8,128)(2,1)}, u32[]{:S(2)}) copy-start(bf16[3072,672]{0,1:T(8,128)(2,1)} %param.12) | copy-start | bytes 12386308
  7.0 9.8 %collective-permute-start = (bf16[24,3072]{1,0:T(8,128)(2,1)S(1)}, bf16[24,3072]{1,0:T(8,128)(2,1)S(1)}, u32[]{:S(2)}, u32[]{:S(2)}) collective-permute-start(bf16[24,3072]{1,0:T(8,128)(2,1)S(1)} %copy-done.3), channel_id=1, source_target_pairs={{0,6},{1,7},{2,4},{3,5},{4,2},{5,3},{6,0},{7,1},{8,14},{9,15},{10,... | collective-permute-start | bytes 442376 | tf_op jit(solution)/shard_map/ppermute | solution.py:282
  9.6 10.0 %collective-permute-start.1 = (bf16[24,3072]{1,0:T(8,128)(2,1)S(1)}, bf16[24,3072]{1,0:T(8,128)(2,1)S(1)}, u32[]{:S(2)}, u32[]{:S(2)}) collective-permute-start(bf16[24,3072]{1,0:T(8,128)(2,1)S(1)} %copy-done.3), channel_id=1, source_target_pairs={{0,4},{1,5},{2,6},{3,7},{4,0},{5,1},{6,2},{7,3},{8,12},{9,13},{10,... | collective-permute-start | bytes 442376 | tf_op jit(solution)/shard_map/ppermute | solution.py:282
  10.0 9.6 %collective-permute-start.2 = (bf16[24,3072]{1,0:T(8,128)(2,1)S(1)}, bf16[24,3072]{1,0:T(8,128)(2,1)S(1)}, u32[]{:S(2)}, u32[]{:S(2)}) collective-permute-start(bf16[24,3072]{1,0:T(8,128)(2,1)S(1)} %copy-done.3), channel_id=1, source_target_pairs={{0,2},{1,3},{2,0},{3,1},{4,6},{5,7},{6,4},{7,5},{8,10},{9,11},{10,... | collective-permute-start | bytes 442376 | tf_op jit(solution)/shard_map/ppermute | solution.py:282
  14.3 7.6 %collective-permute-start.10 = (bf16[48,1536]{1,0:T(8,128)(2,1)S(1)}, bf16[48,1536]{1,0:T(8,128)(2,1)S(1)}, u32[]{:S(2)}, u32[]{:S(2)}) collective-permute-start(bf16[48,1536]{1,0:T(8,128)(2,1)S(1)} %collective-permute-done.3.refs_8_), channel_id=1, source_target_pairs={{0,2},{1,3},{2,0},{3,1},{4,6},{5,7},{6,4},{7,5},{8,10},{9,11},{10,... | collective-permute-start | bytes 442376 | tf_op jit(solution)/shard_map/ppermute | solution.py:282
  15.9 7.4 %collective-permute-start.8 = (bf16[48,1536]{1,0:T(8,128)(2,1)S(1)}, bf16[48,1536]{1,0:T(8,128)(2,1)S(1)}, u32[]{:S(2)}, u32[]{:S(2)}) collective-permute-start(bf16[48,1536]{1,0:T(8,128)(2,1)S(1)} %collective-permute-done.3.refs_8_), channel_id=1, source_target_pairs={{0,6},{1,7},{2,4},{3,5},{4,2},{5,3},{6,0},{7,1},{8,14},{9,15},{10,... | collective-permute-start | bytes 442376 | tf_op jit(solution)/shard_map/ppermute | solution.py:282
  16.8 8.0 %collective-permute-start.9 = (bf16[48,1536]{1,0:T(8,128)(2,1)S(1)}, bf16[48,1536]{1,0:T(8,128)(2,1)S(1)}, u32[]{:S(2)}, u32[]{:S(2)}) collective-permute-start(bf16[48,1536]{1,0:T(8,128)(2,1)S(1)} %collective-permute-done.3.refs_8_), channel_id=1, source_target_pairs={{0,4},{1,5},{2,6},{3,7},{4,0},{5,1},{6,2},{7,3},{8,12},{9,13},{10,... | collective-permute-start | bytes 442376 | tf_op jit(solution)/shard_map/ppermute | solution.py:282
  19.6 5.2 %collective-permute-start.4 = (bf16[24,3072]{1,0:T(8,128)(2,1)S(1)}, bf16[24,3072]{1,0:T(8,128)(2,1)S(1)}, u32[]{:S(2)}, u32[]{:S(2)}) collective-permute-start(bf16[24,3072]{1,0:T(8,128)(2,1)S(1)} %copy-done.3), channel_id=1, source_target_pairs={{0,1},{1,0},{2,3},{3,2},{4,5},{5,4},{6,7},{7,6},{8,9},{9,8},{10,11... | collective-permute-start | bytes 442376 | tf_op jit(solution)/shard_map/ppermute | solution.py:282
  19.6 5.7 %collective-permute-start.5 = (bf16[24,3072]{1,0:T(8,128)(2,1)S(1)}, bf16[24,3072]{1,0:T(8,128)(2,1)S(1)}, u32[]{:S(2)}, u32[]{:S(2)}) collective-permute-start(bf16[24,3072]{1,0:T(8,128)(2,1)S(1)} %collective-permute-done.refs_1_), channel_id=1, source_target_pairs={{0,1},{1,0},{2,3},{3,2},{4,5},{5,4},{6,7},{7,6},{8,9},{9,8},{10,11... | collective-permute-start | bytes 442376 | tf_op jit(solution)/shard_map/ppermute | solution.py:282
  21.9 3.5 %collective-permute-start.6 = (bf16[24,3072]{1,0:T(8,128)(2,1)S(1)}, bf16[24,3072]{1,0:T(8,128)(2,1)S(1)}, u32[]{:S(2)}, u32[]{:S(2)}) collective-permute-start(bf16[24,3072]{1,0:T(8,128)(2,1)S(1)} %collective-permute-done.1.refs_2_), channel_id=1, source_target_pairs={{0,1},{1,0},{2,3},{3,2},{4,5},{5,4},{6,7},{7,6},{8,9},{9,8},{10,11... | collective-permute-start | bytes 442376 | tf_op jit(solution)/shard_map/ppermute | solution.py:282
  23.2 2.6 %collective-permute-start.7 = (bf16[24,3072]{1,0:T(8,128)(2,1)S(1)}, bf16[24,3072]{1,0:T(8,128)(2,1)S(1)}, u32[]{:S(2)}, u32[]{:S(2)}) collective-permute-start(bf16[24,3072]{1,0:T(8,128)(2,1)S(1)} %collective-permute-done.2.refs_3_), channel_id=1, source_target_pairs={{0,1},{1,0},{2,3},{3,2},{4,5},{5,4},{6,7},{7,6},{8,9},{9,8},{10,11... | collective-permute-start | bytes 442376 | tf_op jit(solution)/shard_map/ppermute | solution.py:282
  24.8 1.4 %collective-permute-start.11 = (bf16[48,1536]{1,0:T(8,128)(2,1)S(1)}, bf16[48,1536]{1,0:T(8,128)(2,1)S(1)}, u32[]{:S(2)}, u32[]{:S(2)}) collective-permute-start(bf16[48,1536]{1,0:T(8,128)(2,1)S(1)} %collective-permute-done.3.refs_8_), channel_id=1, source_target_pairs={{0,1},{1,0},{2,3},{3,2},{4,5},{5,4},{6,7},{7,6},{8,9},{9,8},{10,11... | collective-permute-start | bytes 442376 | tf_op jit(solution)/shard_map/ppermute | solution.py:282
  24.8 1.6 %collective-permute-start.12 = (bf16[48,1536]{1,0:T(8,128)(2,1)S(1)}, bf16[48,1536]{1,0:T(8,128)(2,1)S(1)}, u32[]{:S(2)}, u32[]{:S(2)}) collective-permute-start(bf16[48,1536]{1,0:T(8,128)(2,1)S(1)} %collective-permute-done.8.refs_9_), channel_id=1, source_target_pairs={{0,1},{1,0},{2,3},{3,2},{4,5},{5,4},{6,7},{7,6},{8,9},{9,8},{10,11... | collective-permute-start | bytes 442376 | tf_op jit(solution)/shard_map/ppermute | solution.py:282
  25.3 1.4 %collective-permute-start.13 = (bf16[48,1536]{1,0:T(8,128)(2,1)S(1)}, bf16[48,1536]{1,0:T(8,128)(2,1)S(1)}, u32[]{:S(2)}, u32[]{:S(2)}) collective-permute-start(bf16[48,1536]{1,0:T(8,128)(2,1)S(1)} %collective-permute-done.9.refs_10_), channel_id=1, source_target_pairs={{0,1},{1,0},{2,3},{3,2},{4,5},{5,4},{6,7},{7,6},{8,9},{9,8},{10,11... | collective-permute-start | bytes 442376 | tf_op jit(solution)/shard_map/ppermute | solution.py:282
  25.4 1.5 %collective-permute-start.14 = (bf16[48,1536]{1,0:T(8,128)(2,1)S(1)}, bf16[48,1536]{1,0:T(8,128)(2,1)S(1)}, u32[]{:S(2)}, u32[]{:S(2)}) collective-permute-start(bf16[48,1536]{1,0:T(8,128)(2,1)S(1)} %collective-permute-done.10.refs_11_), channel_id=1, source_target_pairs={{0,1},{1,0},{2,3},{3,2},{4,5},{5,4},{6,7},{7,6},{8,9},{9,8},{10,11... | collective-permute-start | bytes 442376 | tf_op jit(solution)/shard_map/ppermute | solution.py:282
  26.9 2.6 %copy-start.2 = (bf16[672,3072]{1,0:T(8,128)(2,1)S(1)}, bf16[672,3072]{1,0:T(8,128)(2,1)}, u32[]{:S(2)}) copy-start(bf16[672,3072]{1,0:T(8,128)(2,1)} %refs_21_.1) | copy-start | bytes 12386308
  29.6 16.1 %copy-start.4 = (f32[48,64]{1,0:T(8,128)S(1)}, f32[48,64]{1,0:T(8,128)}, u32[]{:S(2)}) copy-start(f32[48,64]{1,0:T(8,128)} %get-tuple-element.46.weight_ref) | copy-start | bytes 36868
  29.6 19.3 %copy-start.5 = (f32[48,64]{1,0:T(8,128)S(1)}, f32[48,64]{1,0:T(8,128)}, u32[]{:S(2)}) copy-start(f32[48,64]{1,0:T(8,128)} %get-tuple-element.45.place_ref) | copy-start | bytes 36868
  29.6 19.3 %copy-start.6 = (s32[4,64]{1,0:T(4,128)S(1)}, s32[4,64]{1,0:T(4,128)}, u32[]{:S(2)}) copy-start(s32[4,64]{1,0:T(4,128)} %get-tuple-element.44.ids_ref) | copy-start | bytes 3076
  33.7 1.7 %collective-permute-start.19 = (bf16[96,1664]{1,0:T(8,128)(2,1)S(1)}, bf16[96,1664]{1,0:T(8,128)(2,1)S(1)}, u32[]{:S(2)}, u32[]{:S(2)}) collective-permute-start(bf16[96,1664]{1,0:T(8,128)(2,1)S(1)} %get-tuple-element.79), channel_id=1, source_target_pairs={{0,1},{1,0},{2,3},{3,2},{4,5},{5,4},{6,7},{7,6},{8,9},{9,8},{10,11... | collective-permute-start | bytes 958472 | tf_op jit(solution)/shard_map/ppermute | solution.py:282
  34.1 5.1 %collective-permute-start.15 = (bf16[96,1664]{1,0:T(8,128)(2,1)S(1)}, bf16[96,1664]{1,0:T(8,128)(2,1)S(1)}, u32[]{:S(2)}, u32[]{:S(2)}) collective-permute-start(bf16[96,1664]{1,0:T(8,128)(2,1)S(1)} %get-tuple-element.71), channel_id=1, source_target_pairs={{0,1},{1,0},{2,3},{3,2},{4,5},{5,4},{6,7},{7,6},{8,9},{9,8},{10,11... | collective-permute-start | bytes 958472 | tf_op jit(solution)/shard_map/ppermute | solution.py:282
  35.6 6.2 %collective-permute-start.20 = (bf16[24,1664]{1,0:T(8,128)(2,1)S(1)}, bf16[24,1664]{1,0:T(8,128)(2,1)S(1)}, u32[]{:S(2)}, u32[]{:S(2)}) collective-permute-start(bf16[24,1664]{1,0:T(8,128)(2,1)S(1)} %get-tuple-element.81), channel_id=1, source_target_pairs={{0,6},{1,7},{2,4},{3,5},{4,2},{5,3},{6,0},{7,1},{8,14},{9,15},{10,... | collective-permute-start | bytes 239624 | tf_op jit(solution)/shard_map/ppermute | solution.py:282
  37.3 5.6 %collective-permute-start.21 = (bf16[24,1664]{1,0:T(8,128)(2,1)S(1)}, bf16[24,1664]{1,0:T(8,128)(2,1)S(1)}, u32[]{:S(2)}, u32[]{:S(2)}) collective-permute-start(bf16[24,1664]{1,0:T(8,128)(2,1)S(1)} %get-tuple-element.82), channel_id=1, source_target_pairs={{0,4},{1,5},{2,6},{3,7},{4,0},{5,1},{6,2},{7,3},{8,12},{9,13},{10,... | collective-permute-start | bytes 239624 | tf_op jit(solution)/shard_map/ppermute | solution.py:282
  37.7 5.6 %collective-permute-start.22 = (bf16[24,1664]{1,0:T(8,128)(2,1)S(1)}, bf16[24,1664]{1,0:T(8,128)(2,1)S(1)}, u32[]{:S(2)}, u32[]{:S(2)}) collective-permute-start(bf16[24,1664]{1,0:T(8,128)(2,1)S(1)} %get-tuple-element.83), channel_id=1, source_target_pairs={{0,2},{1,3},{2,0},{3,1},{4,6},{5,7},{6,4},{7,5},{8,10},{9,11},{10,... | collective-permute-start | bytes 239624 | tf_op jit(solution)/shard_map/ppermute | solution.py:282
  39.3 6.5 %collective-permute-start.16 = (bf16[24,1664]{1,0:T(8,128)(2,1)S(1)}, bf16[24,1664]{1,0:T(8,128)(2,1)S(1)}, u32[]{:S(2)}, u32[]{:S(2)}) collective-permute-start(bf16[24,1664]{1,0:T(8,128)(2,1)S(1)} %get-tuple-element.73), channel_id=1, source_target_pairs={{0,6},{1,7},{2,4},{3,5},{4,2},{5,3},{6,0},{7,1},{8,14},{9,15},{10,... | collective-permute-start | bytes 239624 | tf_op jit(solution)/shard_map/ppermute | solution.py:282
  41.0 4.8 %collective-permute-start.17 = (bf16[24,1664]{1,0:T(8,128)(2,1)S(1)}, bf16[24,1664]{1,0:T(8,128)(2,1)S(1)}, u32[]{:S(2)}, u32[]{:S(2)}) collective-permute-start(bf16[24,1664]{1,0:T(8,128)(2,1)S(1)} %get-tuple-element.74), channel_id=1, source_target_pairs={{0,4},{1,5},{2,6},{3,7},{4,0},{5,1},{6,2},{7,3},{8,12},{9,13},{10,... | collective-permute-start | bytes 239624 | tf_op jit(solution)/shard_map/ppermute | solution.py:282
  41.8 4.5 %collective-permute-start.18 = (bf16[24,1664]{1,0:T(8,128)(2,1)S(1)}, bf16[24,1664]{1,0:T(8,128)(2,1)S(1)}, u32[]{:S(2)}, u32[]{:S(2)}) collective-permute-start(bf16[24,1664]{1,0:T(8,128)(2,1)S(1)} %get-tuple-element.75), channel_id=1, source_target_pairs={{0,2},{1,3},{2,0},{3,1},{4,6},{5,7},{6,4},{7,5},{8,10},{9,11},{10,... | collective-permute-start | bytes 239624 | tf_op jit(solution)/shard_map/ppermute | solution.py:282
  43.5 5.4 %collective-permute-start.23 = (bf16[24,1664]{1,0:T(8,128)(2,1)S(1)}, bf16[24,1664]{1,0:T(8,128)(2,1)S(1)}, u32[]{:S(2)}, u32[]{:S(2)}) collective-permute-start(bf16[24,1664]{1,0:T(8,128)(2,1)S(1)} %other.1), channel_id=1, source_target_pairs={{0,8},{1,9},{2,10},{3,11},{4,12},{5,13},{6,14},{7,15},{8,0},{9,1},... | collective-permute-start | bytes 239624 | tf_op jit(solution)/shard_map/ppermute | solution.py:282

commit v4 on v3

--- a/solution.py
+++ b/solution.py
@@ -323,9 +323,10 @@
     own, token = together((own, gate()))
     other, token = together((other, token))
     own = near(own)
-    other = near(other)
+    far = [swap(other, k) for k in evens]
     own, token = together((own, gate(token)))
-    other, token = together((other, token))
+    far, token = together((far[::-1], token))
+    other = [other] + far[::-1]
     own = both_cores(own)
     other = both_cores(other)
     states = call(

time: 50.1 us -> 50 us (level)
  no operation moved by 1% of the time
where the time goes in v4:
time: 50 us; the launch traced here: 49.8 us
  starting transfers between devices  22.4 us (45%)
  waiting for transfers between devices  15.8 us (32%)
  Pallas kernels  10.8 us (22%)
  between operations  0.78 us (2%)
    ppermute x24, starting transfers between devices, swap(): return lax.ppermute(x, 'expert', [(i, i ^ offset) for i in range(devices)])  22.4 us
    ppermute x24, waiting for transfers between devices, swap(): return lax.ppermute(x, 'expert', [(i, i ^ offset) for i in range(devices)])  15.8 us
    pallas_call x11, Pallas kernels, call(): pl.pallas_call(kernel, name=name, out_shape=out_shape, in_specs=in_specs,...  10.8 us
  transfers between devices with their start and end apart: 24, of which 15 were waited for; matrix products, arithmetic and copies ran while one was open for 0% of the time, Pallas kernels for 2%

profile of v4, /device:TPU:0, one launch (start us, length us, event | category | flops | bytes accessed | tf_op | source)
XLA Modules:
  0.0 49.8 jit_solution(16598949327628093509)
XLA Ops:
  0.6 2.2 %pick.1 = (bf16[24,3072]{1,0:T(8,128)(2,1)}, bf16[48,1536]{1,0:T(8,128)(2,1)}, s32[4,64]{1,0:T(4,128)}, f32[48,64]{1,0:T(8,128)}, f32[48,64]{1,0:T(8,128)}) custom-call(s32[1]{0:T(128)} %bitcast.mine_ref, s32[4,64]{1,0:T(4,128)} %bitcast.10, f32[4,64]{1,0:T(4,128)} %bitcast.11, bf16[64,3072]{1,0:T(8,128)(2,1)} %tok_hbm.1, bf16[64,3072]{1,0:T(8,128)(2,1)} %cot_hbm.1), custom_call_target="tpu_custom_call" | custom-call | flops 37748736 | bytes 1108996 | tf_op jit(solution)/shard_map/pick/pallas_call | solution.py:28
  2.9 0.0 copy-start.3
  2.9 4.1 %collective-permute-start.3 = (bf16[48,1536]{1,0:T(8,128)(2,1)}, bf16[48,1536]{1,0:T(8,128)(2,1)S(1)}, u32[]{:S(2)}, u32[]{:S(2)}) collective-permute-start(bf16[48,1536]{1,0:T(8,128)(2,1)} %get-tuple-element.52), channel_id=1, source_target_pairs={{0,8},{1,9},{2,10},{3,11},{4,12},{5,13},{6,14},{7,15},{8,0},{9,1},... | collective-permute-start | bytes 442376 | tf_op jit(solution)/shard_map/ppermute | solution.py:282
  7.0 2.6 %collective-permute-start = (bf16[24,3072]{1,0:T(8,128)(2,1)S(1)}, bf16[24,3072]{1,0:T(8,128)(2,1)S(1)}, u32[]{:S(2)}, u32[]{:S(2)}) collective-permute-start(bf16[24,3072]{1,0:T(8,128)(2,1)S(1)} %copy-done.3), channel_id=1, source_target_pairs={{0,6},{1,7},{2,4},{3,5},{4,2},{5,3},{6,0},{7,1},{8,14},{9,15},{10,... | collective-permute-start | bytes 442376 | tf_op jit(solution)/shard_map/ppermute | solution.py:282
  9.6 0.4 collective-permute-start.1
  10.0 0.5 %collective-permute-start.2 = (bf16[24,3072]{1,0:T(8,128)(2,1)S(1)}, bf16[24,3072]{1,0:T(8,128)(2,1)S(1)}, u32[]{:S(2)}, u32[]{:S(2)}) collective-permute-start(bf16[24,3072]{1,0:T(8,128)(2,1)S(1)} %copy-done.3), channel_id=1, source_target_pairs={{0,2},{1,3},{2,0},{3,1},{4,6},{5,7},{6,4},{7,5},{8,10},{9,11},{10,... | collective-permute-start | bytes 442376 | tf_op jit(solution)/shard_map/ppermute | solution.py:282
  10.5 3.7 %collective-permute-done.3.refs_8_ = bf16[48,1536]{1,0:T(8,128)(2,1)S(1)} collective-permute-done((bf16[48,1536]{1,0:T(8,128)(2,1)}, bf16[48,1536]{1,0:T(8,128)(2,1)S(1)}, u32[]{:S(2)}, u32[]{:S(2)}) %collective-permute-start.3) | collective-permute-done | bytes 147488 | tf_op jit(solution)/shard_map/ppermute | solution.py:282
  14.3 1.7 %collective-permute-start.10 = (bf16[48,1536]{1,0:T(8,128)(2,1)S(1)}, bf16[48,1536]{1,0:T(8,128)(2,1)S(1)}, u32[]{:S(2)}, u32[]{:S(2)}) collective-permute-start(bf16[48,1536]{1,0:T(8,128)(2,1)S(1)} %collective-permute-done.3.refs_8_), channel_id=1, source_target_pairs={{0,6},{1,7},{2,4},{3,5},{4,2},{5,3},{6,0},{7,1},{8,14},{9,15},{10,... | collective-permute-start | bytes 442376 | tf_op jit(solution)/shard_map/ppermute | solution.py:282
  16.0 0.5 %collective-permute-start.8 = (bf16[48,1536]{1,0:T(8,128)(2,1)S(1)}, bf16[48,1536]{1,0:T(8,128)(2,1)S(1)}, u32[]{:S(2)}, u32[]{:S(2)}) collective-permute-start(bf16[48,1536]{1,0:T(8,128)(2,1)S(1)} %collective-permute-done.3.refs_8_), channel_id=1, source_target_pairs={{0,2},{1,3},{2,0},{3,1},{4,6},{5,7},{6,4},{7,5},{8,10},{9,11},{10,... | collective-permute-start | bytes 442376 | tf_op jit(solution)/shard_map/ppermute | solution.py:282
  16.5 0.2 collective-permute-done.refs_1_
  16.8 1.3 %collective-permute-start.9 = (bf16[48,1536]{1,0:T(8,128)(2,1)S(1)}, bf16[48,1536]{1,0:T(8,128)(2,1)S(1)}, u32[]{:S(2)}, u32[]{:S(2)}) collective-permute-start(bf16[48,1536]{1,0:T(8,128)(2,1)S(1)} %collective-permute-done.3.refs_8_), channel_id=1, source_target_pairs={{0,4},{1,5},{2,6},{3,7},{4,0},{5,1},{6,2},{7,3},{8,12},{9,13},{10,... | collective-permute-start | bytes 442376 | tf_op jit(solution)/shard_map/ppermute | solution.py:282
  18.1 1.6 %collective-permute-done.1.refs_2_ = bf16[24,3072]{1,0:T(8,128)(2,1)S(1)} collective-permute-done((bf16[24,3072]{1,0:T(8,128)(2,1)S(1)}, bf16[24,3072]{1,0:T(8,128)(2,1)S(1)}, u32[]{:S(2)}, u32[]{:S(2)}) %collective-permute-start.1) | collective-permute-done | bytes 147488 | tf_op jit(solution)/shard_map/ppermute | solution.py:282
  19.7 0.0 collective-permute-done.2.refs_3_
  19.7 0.5 %collective-permute-start.5 = (bf16[24,3072]{1,0:T(8,128)(2,1)S(1)}, bf16[24,3072]{1,0:T(8,128)(2,1)S(1)}, u32[]{:S(2)}, u32[]{:S(2)}) collective-permute-start(bf16[24,3072]{1,0:T(8,128)(2,1)S(1)} %collective-permute-done.refs_1_), channel_id=1, source_target_pairs={{0,1},{1,0},{2,3},{3,2},{4,5},{5,4},{6,7},{7,6},{8,9},{9,8},{10,11... | collective-permute-start | bytes 442376 | tf_op jit(solution)/shard_map/ppermute | solution.py:282
  20.2 2.9 %collective-permute-done.10.refs_9_ = bf16[48,1536]{1,0:T(8,128)(2,1)S(1)} collective-permute-done((bf16[48,1536]{1,0:T(8,128)(2,1)S(1)}, bf16[48,1536]{1,0:T(8,128)(2,1)S(1)}, u32[]{:S(2)}, u32[]{:S(2)}) %collective-permute-start.10) | collective-permute-done | bytes 147488 | tf_op jit(solution)/shard_map/ppermute | solution.py:282
  23.1 0.0 collective-permute-start.6
  23.1 0.9 %collective-permute-done.8.refs_11_ = bf16[48,1536]{1,0:T(8,128)(2,1)S(1)} collective-permute-done((bf16[48,1536]{1,0:T(8,128)(2,1)S(1)}, bf16[48,1536]{1,0:T(8,128)(2,1)S(1)}, u32[]{:S(2)}, u32[]{:S(2)}) %collective-permute-start.8) | collective-permute-done | bytes 147488 | tf_op jit(solution)/shard_map/ppermute | solution.py:282
  24.0 0.8 %collective-permute-done.9.refs_10_ = bf16[48,1536]{1,0:T(8,128)(2,1)S(1)} collective-permute-done((bf16[48,1536]{1,0:T(8,128)(2,1)S(1)}, bf16[48,1536]{1,0:T(8,128)(2,1)S(1)}, u32[]{:S(2)}, u32[]{:S(2)}) %collective-permute-start.9) | collective-permute-done | bytes 147488 | tf_op jit(solution)/shard_map/ppermute | solution.py:282
  24.8 0.5 %collective-permute-start.12 = (bf16[48,1536]{1,0:T(8,128)(2,1)S(1)}, bf16[48,1536]{1,0:T(8,128)(2,1)S(1)}, u32[]{:S(2)}, u32[]{:S(2)}) collective-permute-start(bf16[48,1536]{1,0:T(8,128)(2,1)S(1)} %collective-permute-done.10.refs_9_), channel_id=1, source_target_pairs={{0,1},{1,0},{2,3},{3,2},{4,5},{5,4},{6,7},{7,6},{8,9},{9,8},{10,11... | collective-permute-start | bytes 442376 | tf_op jit(solution)/shard_map/ppermute | solution.py:282
  25.3 0.1 collective-permute-start.13
  25.4 0.4 collective-permute-start.14
  25.8 0.3 collective-permute-done.7.refs_7_
  26.2 0.2 collective-permute-done.12.refs_13_
  26.4 0.3 collective-permute-done.13.refs_14_
  26.7 0.2 collective-permute-done.14.refs_15_
  26.9 2.6 %forward.1 = (f32[672,256]{1,0:T(8,128)S(1)}, f32[672,256]{1,0:T(8,128)S(1)}, bf16[672,256]{1,0:T(8,128)(2,1)S(1)}) custom-call(bf16[24,3072]{1,0:T(8,128)(2,1)S(1)} %copy-done.3, bf16[24,3072]{1,0:T(8,128)(2,1)S(1)} %collective-permute-done.refs_1_, bf16[24,3072]{1,0:T(8,128)(2,1)S(1)} %collective-permute-done.1.refs_2_, ...), custom_call_target="tpu_custom_call" | custom-call | flops 2113929216 | bytes 12341248 | tf_op jit(solution)/shard_map/forward/pallas_call | solution.py:28
  29.6 0.0 copy-start.6
  29.6 4.1 %backward.1 = (bf16[96,1664]{1,0:T(8,128)(2,1)S(1)}, bf16[96,1664]{1,0:T(8,128)(2,1)S(1)}, bf16[96,1664]{1,0:T(8,128)(2,1)S(1)}, bf16[96,1664]{1,0:T(8,128)(2,1)S(1)}) custom-call(bf16[24,3072]{1,0:T(8,128)(2,1)S(1)} %copy-done.3, bf16[24,3072]{1,0:T(8,128)(2,1)S(1)} %collective-permute-done.refs_1_, bf16[24,3072]{1,0:T(8,128)(2,1)S(1)} %collective-permute-done.1.refs_2_, ...), custom_call_target="tpu_custom_call" | custom-call | flops 3170893824 | bytes 17743872 | tf_op jit(solution)/shard_map/backward/pallas_call | solution.py:28
  33.7 0.3 collective-permute-start.19
  34.1 0.2 collective-permute-start.15
  34.3 1.1 %collective-permute-done.19.got_ref = bf16[96,1664]{1,0:T(8,128)(2,1)S(1)} collective-permute-done((bf16[96,1664]{1,0:T(8,128)(2,1)S(1)}, bf16[96,1664]{1,0:T(8,128)(2,1)S(1)}, u32[]{:S(2)}, u32[]{:S(2)}) %collective-permute-start.19) | collective-permute-done | bytes 319520 | tf_op jit(solution)/shard_map/ppermute | solution.py:282
  35.4 0.2 chip.3
  35.6 1.7 %collective-permute-start.20 = (bf16[24,1664]{1,0:T(8,128)(2,1)S(1)}, bf16[24,1664]{1,0:T(8,128)(2,1)S(1)}, u32[]{:S(2)}, u32[]{:S(2)}) collective-permute-start(bf16[24,1664]{1,0:T(8,128)(2,1)S(1)} %get-tuple-element.79), channel_id=1, source_target_pairs={{0,6},{1,7},{2,4},{3,5},{4,2},{5,3},{6,0},{7,1},{8,14},{9,15},{10,... | collective-permute-start | bytes 239624 | tf_op jit(solution)/shard_map/ppermute | solution.py:282
  37.2 0.5 collective-permute-start.21
  37.7 1.4 %collective-permute-start.22 = (bf16[24,1664]{1,0:T(8,128)(2,1)S(1)}, bf16[24,1664]{1,0:T(8,128)(2,1)S(1)}, u32[]{:S(2)}, u32[]{:S(2)}) collective-permute-start(bf16[24,1664]{1,0:T(8,128)(2,1)S(1)} %get-tuple-element.81), channel_id=1, source_target_pairs={{0,2},{1,3},{2,0},{3,1},{4,6},{5,7},{6,4},{7,5},{8,10},{9,11},{10,... | collective-permute-start | bytes 239624 | tf_op jit(solution)/shard_map/ppermute | solution.py:282
  39.1 0.2 chip.2
  39.3 1.7 %collective-permute-start.16 = (bf16[24,1664]{1,0:T(8,128)(2,1)S(1)}, bf16[24,1664]{1,0:T(8,128)(2,1)S(1)}, u32[]{:S(2)}, u32[]{:S(2)}) collective-permute-start(bf16[24,1664]{1,0:T(8,128)(2,1)S(1)} %get-tuple-element.71), channel_id=1, source_target_pairs={{0,6},{1,7},{2,4},{3,5},{4,2},{5,3},{6,0},{7,1},{8,14},{9,15},{10,... | collective-permute-start | bytes 239624 | tf_op jit(solution)/shard_map/ppermute | solution.py:282
  40.9 0.5 collective-permute-start.17
  41.4 0.4 collective-permute-done.20.refs_1_
  41.8 1.1 %collective-permute-start.18 = (bf16[24,1664]{1,0:T(8,128)(2,1)S(1)}, bf16[24,1664]{1,0:T(8,128)(2,1)S(1)}, u32[]{:S(2)}, u32[]{:S(2)}) collective-permute-start(bf16[24,1664]{1,0:T(8,128)(2,1)S(1)} %get-tuple-element.73), channel_id=1, source_target_pairs={{0,2},{1,3},{2,0},{3,1},{4,6},{5,7},{6,4},{7,5},{8,10},{9,11},{10,... | collective-permute-start | bytes 239624 | tf_op jit(solution)/shard_map/ppermute | solution.py:282
  42.8 0.5 collective-permute-done.22.refs_3_
  43.3 0.2 other.1
  43.5 2.3 %collective-permute-start.23 = (bf16[24,1664]{1,0:T(8,128)(2,1)S(1)}, bf16[24,1664]{1,0:T(8,128)(2,1)S(1)}, u32[]{:S(2)}, u32[]{:S(2)}) collective-permute-start(bf16[24,1664]{1,0:T(8,128)(2,1)S(1)} %other.1), channel_id=1, source_target_pairs={{0,8},{1,9},{2,10},{3,11},{4,12},{5,13},{6,14},{7,15},{8,0},{9,1},... | collective-permute-start | bytes 239624 | tf_op jit(solution)/shard_map/ppermute | solution.py:282
  45.8 0.1 layout.1
  45.9 0.3 collective-permute-done.18.refs_3_
  46.2 0.3 own.1
  46.5 2.3 %collective-permute-done.23.back_ref = bf16[24,1664]{1,0:T(8,128)(2,1)S(1)} collective-permute-done((bf16[24,1664]{1,0:T(8,128)(2,1)S(1)}, bf16[24,1664]{1,0:T(8,128)(2,1)S(1)}, u32[]{:S(2)}, u32[]{:S(2)}) %collective-permute-start.23) | collective-permute-done | bytes 79904 | tf_op jit(solution)/shard_map/ppermute | solution.py:282
  48.8 1.0 %final.1 = (bf16[64,3072]{1,0:T(8,128)(2,1)}, f32[4,64]{1,0:T(4,128)}) custom-call(s32[1]{0:T(128)} %bitcast.mine_ref, s32[4,64]{1,0:T(4,128)S(1)} %copy-done.6, f32[48,64]{1,0:T(8,128)S(1)} %copy-done.5, bf16[64,128]{1,0:T(8,128)(2,1)S(1)} %get-tuple-element.46.left_ref, bf16[64,128]{1,0:T(8,128)(2,1)S(1)} %get-tuple-element.47.right_ref, ...), custom_call_target="tpu_custom_call" | custom-call | bytes 1318916 | tf_op jit(solution)/shard_map/final/pallas_call | solution.py:28
  (25 shorter events, 0.1 us)
Async XLA Ops:
  2.9 4.1 %copy-start.3 = (bf16[24,3072]{1,0:T(8,128)(2,1)S(1)}, bf16[24,3072]{1,0:T(8,128)(2,1)}, u32[]{:S(2)}) copy-start(bf16[24,3072]{1,0:T(8,128)(2,1)} %get-tuple-element.55.refs_0_) | copy-start | bytes 442372
  2.9 11.4 %collective-permute-start.3 = (bf16[48,1536]{1,0:T(8,128)(2,1)}, bf16[48,1536]{1,0:T(8,128)(2,1)S(1)}, u32[]{:S(2)}, u32[]{:S(2)}) collective-permute-start(bf16[48,1536]{1,0:T(8,128)(2,1)} %get-tuple-element.52), channel_id=1, source_target_pairs={{0,8},{1,9},{2,10},{3,11},{4,12},{5,13},{6,14},{7,15},{8,0},{9,1},... | collective-permute-start | bytes 442376 | tf_op jit(solution)/shard_map/ppermute | solution.py:282
  7.0 19.9 %copy-start = (bf16[3072,672]{0,1:T(8,128)(2,1)S(1)}, bf16[3072,672]{0,1:T(8,128)(2,1)}, u32[]{:S(2)}) copy-start(bf16[3072,672]{0,1:T(8,128)(2,1)} %param.11) | copy-start | bytes 12386308
  7.0 19.9 %copy-start.1 = (bf16[3072,672]{0,1:T(8,128)(2,1)S(1)}, bf16[3072,672]{0,1:T(8,128)(2,1)}, u32[]{:S(2)}) copy-start(bf16[3072,672]{0,1:T(8,128)(2,1)} %param.12) | copy-start | bytes 12386308
  7.0 9.8 %collective-permute-start = (bf16[24,3072]{1,0:T(8,128)(2,1)S(1)}, bf16[24,3072]{1,0:T(8,128)(2,1)S(1)}, u32[]{:S(2)}, u32[]{:S(2)}) collective-permute-start(bf16[24,3072]{1,0:T(8,128)(2,1)S(1)} %copy-done.3), channel_id=1, source_target_pairs={{0,6},{1,7},{2,4},{3,5},{4,2},{5,3},{6,0},{7,1},{8,14},{9,15},{10,... | collective-permute-start | bytes 442376 | tf_op jit(solution)/shard_map/ppermute | solution.py:282
  9.6 10.1 %collective-permute-start.1 = (bf16[24,3072]{1,0:T(8,128)(2,1)S(1)}, bf16[24,3072]{1,0:T(8,128)(2,1)S(1)}, u32[]{:S(2)}, u32[]{:S(2)}) collective-permute-start(bf16[24,3072]{1,0:T(8,128)(2,1)S(1)} %copy-done.3), channel_id=1, source_target_pairs={{0,4},{1,5},{2,6},{3,7},{4,0},{5,1},{6,2},{7,3},{8,12},{9,13},{10,... | collective-permute-start | bytes 442376 | tf_op jit(solution)/shard_map/ppermute | solution.py:282
  10.0 9.7 %collective-permute-start.2 = (bf16[24,3072]{1,0:T(8,128)(2,1)S(1)}, bf16[24,3072]{1,0:T(8,128)(2,1)S(1)}, u32[]{:S(2)}, u32[]{:S(2)}) collective-permute-start(bf16[24,3072]{1,0:T(8,128)(2,1)S(1)} %copy-done.3), channel_id=1, source_target_pairs={{0,2},{1,3},{2,0},{3,1},{4,6},{5,7},{6,4},{7,5},{8,10},{9,11},{10,... | collective-permute-start | bytes 442376 | tf_op jit(solution)/shard_map/ppermute | solution.py:282
  14.3 8.8 %collective-permute-start.10 = (bf16[48,1536]{1,0:T(8,128)(2,1)S(1)}, bf16[48,1536]{1,0:T(8,128)(2,1)S(1)}, u32[]{:S(2)}, u32[]{:S(2)}) collective-permute-start(bf16[48,1536]{1,0:T(8,128)(2,1)S(1)} %collective-permute-done.3.refs_8_), channel_id=1, source_target_pairs={{0,6},{1,7},{2,4},{3,5},{4,2},{5,3},{6,0},{7,1},{8,14},{9,15},{10,... | collective-permute-start | bytes 442376 | tf_op jit(solution)/shard_map/ppermute | solution.py:282
  16.0 8.0 %collective-permute-start.8 = (bf16[48,1536]{1,0:T(8,128)(2,1)S(1)}, bf16[48,1536]{1,0:T(8,128)(2,1)S(1)}, u32[]{:S(2)}, u32[]{:S(2)}) collective-permute-start(bf16[48,1536]{1,0:T(8,128)(2,1)S(1)} %collective-permute-done.3.refs_8_), channel_id=1, source_target_pairs={{0,2},{1,3},{2,0},{3,1},{4,6},{5,7},{6,4},{7,5},{8,10},{9,11},{10,... | collective-permute-start | bytes 442376 | tf_op jit(solution)/shard_map/ppermute | solution.py:282
  16.8 8.0 %collective-permute-start.9 = (bf16[48,1536]{1,0:T(8,128)(2,1)S(1)}, bf16[48,1536]{1,0:T(8,128)(2,1)S(1)}, u32[]{:S(2)}, u32[]{:S(2)}) collective-permute-start(bf16[48,1536]{1,0:T(8,128)(2,1)S(1)} %collective-permute-done.3.refs_8_), channel_id=1, source_target_pairs={{0,4},{1,5},{2,6},{3,7},{4,0},{5,1},{6,2},{7,3},{8,12},{9,13},{10,... | collective-permute-start | bytes 442376 | tf_op jit(solution)/shard_map/ppermute | solution.py:282
  19.7 5.1 %collective-permute-start.4 = (bf16[24,3072]{1,0:T(8,128)(2,1)S(1)}, bf16[24,3072]{1,0:T(8,128)(2,1)S(1)}, u32[]{:S(2)}, u32[]{:S(2)}) collective-permute-start(bf16[24,3072]{1,0:T(8,128)(2,1)S(1)} %copy-done.3), channel_id=1, source_target_pairs={{0,1},{1,0},{2,3},{3,2},{4,5},{5,4},{6,7},{7,6},{8,9},{9,8},{10,11... | collective-permute-start | bytes 442376 | tf_op jit(solution)/shard_map/ppermute | solution.py:282
  19.7 5.6 %collective-permute-start.5 = (bf16[24,3072]{1,0:T(8,128)(2,1)S(1)}, bf16[24,3072]{1,0:T(8,128)(2,1)S(1)}, u32[]{:S(2)}, u32[]{:S(2)}) collective-permute-start(bf16[24,3072]{1,0:T(8,128)(2,1)S(1)} %collective-permute-done.refs_1_), channel_id=1, source_target_pairs={{0,1},{1,0},{2,3},{3,2},{4,5},{5,4},{6,7},{7,6},{8,9},{9,8},{10,11... | collective-permute-start | bytes 442376 | tf_op jit(solution)/shard_map/ppermute | solution.py:282
  23.1 2.3 %collective-permute-start.6 = (bf16[24,3072]{1,0:T(8,128)(2,1)S(1)}, bf16[24,3072]{1,0:T(8,128)(2,1)S(1)}, u32[]{:S(2)}, u32[]{:S(2)}) collective-permute-start(bf16[24,3072]{1,0:T(8,128)(2,1)S(1)} %collective-permute-done.1.refs_2_), channel_id=1, source_target_pairs={{0,1},{1,0},{2,3},{3,2},{4,5},{5,4},{6,7},{7,6},{8,9},{9,8},{10,11... | collective-permute-start | bytes 442376 | tf_op jit(solution)/shard_map/ppermute | solution.py:282
  24.0 2.2 %collective-permute-start.11 = (bf16[48,1536]{1,0:T(8,128)(2,1)S(1)}, bf16[48,1536]{1,0:T(8,128)(2,1)S(1)}, u32[]{:S(2)}, u32[]{:S(2)}) collective-permute-start(bf16[48,1536]{1,0:T(8,128)(2,1)S(1)} %collective-permute-done.3.refs_8_), channel_id=1, source_target_pairs={{0,1},{1,0},{2,3},{3,2},{4,5},{5,4},{6,7},{7,6},{8,9},{9,8},{10,11... | collective-permute-start | bytes 442376 | tf_op jit(solution)/shard_map/ppermute | solution.py:282
  24.8 1.4 %collective-permute-start.7 = (bf16[24,3072]{1,0:T(8,128)(2,1)S(1)}, bf16[24,3072]{1,0:T(8,128)(2,1)S(1)}, u32[]{:S(2)}, u32[]{:S(2)}) collective-permute-start(bf16[24,3072]{1,0:T(8,128)(2,1)S(1)} %collective-permute-done.2.refs_3_), channel_id=1, source_target_pairs={{0,1},{1,0},{2,3},{3,2},{4,5},{5,4},{6,7},{7,6},{8,9},{9,8},{10,11... | collective-permute-start | bytes 442376 | tf_op jit(solution)/shard_map/ppermute | solution.py:282
  24.8 1.6 %collective-permute-start.12 = (bf16[48,1536]{1,0:T(8,128)(2,1)S(1)}, bf16[48,1536]{1,0:T(8,128)(2,1)S(1)}, u32[]{:S(2)}, u32[]{:S(2)}) collective-permute-start(bf16[48,1536]{1,0:T(8,128)(2,1)S(1)} %collective-permute-done.10.refs_9_), channel_id=1, source_target_pairs={{0,1},{1,0},{2,3},{3,2},{4,5},{5,4},{6,7},{7,6},{8,9},{9,8},{10,11... | collective-permute-start | bytes 442376 | tf_op jit(solution)/shard_map/ppermute | solution.py:282
  25.3 1.4 %collective-permute-start.13 = (bf16[48,1536]{1,0:T(8,128)(2,1)S(1)}, bf16[48,1536]{1,0:T(8,128)(2,1)S(1)}, u32[]{:S(2)}, u32[]{:S(2)}) collective-permute-start(bf16[48,1536]{1,0:T(8,128)(2,1)S(1)} %collective-permute-done.9.refs_10_), channel_id=1, source_target_pairs={{0,1},{1,0},{2,3},{3,2},{4,5},{5,4},{6,7},{7,6},{8,9},{9,8},{10,11... | collective-permute-start | bytes 442376 | tf_op jit(solution)/shard_map/ppermute | solution.py:282
  25.4 1.5 %collective-permute-start.14 = (bf16[48,1536]{1,0:T(8,128)(2,1)S(1)}, bf16[48,1536]{1,0:T(8,128)(2,1)S(1)}, u32[]{:S(2)}, u32[]{:S(2)}) collective-permute-start(bf16[48,1536]{1,0:T(8,128)(2,1)S(1)} %collective-permute-done.8.refs_11_), channel_id=1, source_target_pairs={{0,1},{1,0},{2,3},{3,2},{4,5},{5,4},{6,7},{7,6},{8,9},{9,8},{10,11... | collective-permute-start | bytes 442376 | tf_op jit(solution)/shard_map/ppermute | solution.py:282
  26.9 2.6 %copy-start.2 = (bf16[672,3072]{1,0:T(8,128)(2,1)S(1)}, bf16[672,3072]{1,0:T(8,128)(2,1)}, u32[]{:S(2)}) copy-start(bf16[672,3072]{1,0:T(8,128)(2,1)} %refs_21_.1) | copy-start | bytes 12386308
  29.6 16.3 %copy-start.4 = (f32[48,64]{1,0:T(8,128)S(1)}, f32[48,64]{1,0:T(8,128)}, u32[]{:S(2)}) copy-start(f32[48,64]{1,0:T(8,128)} %get-tuple-element.45.weight_ref) | copy-start | bytes 36868
  29.6 19.2 %copy-start.5 = (f32[48,64]{1,0:T(8,128)S(1)}, f32[48,64]{1,0:T(8,128)}, u32[]{:S(2)}) copy-start(f32[48,64]{1,0:T(8,128)} %get-tuple-element.44.place_ref) | copy-start | bytes 36868
  29.6 19.2 %copy-start.6 = (s32[4,64]{1,0:T(4,128)S(1)}, s32[4,64]{1,0:T(4,128)}, u32[]{:S(2)}) copy-start(s32[4,64]{1,0:T(4,128)} %get-tuple-element.43.ids_ref) | copy-start | bytes 3076
  33.7 1.7 %collective-permute-start.19 = (bf16[96,1664]{1,0:T(8,128)(2,1)S(1)}, bf16[96,1664]{1,0:T(8,128)(2,1)S(1)}, u32[]{:S(2)}, u32[]{:S(2)}) collective-permute-start(bf16[96,1664]{1,0:T(8,128)(2,1)S(1)} %get-tuple-element.77), channel_id=1, source_target_pairs={{0,1},{1,0},{2,3},{3,2},{4,5},{5,4},{6,7},{7,6},{8,9},{9,8},{10,11... | collective-permute-start | bytes 958472 | tf_op jit(solution)/shard_map/ppermute | solution.py:282
  34.1 5.1 %collective-permute-start.15 = (bf16[96,1664]{1,0:T(8,128)(2,1)S(1)}, bf16[96,1664]{1,0:T(8,128)(2,1)S(1)}, u32[]{:S(2)}, u32[]{:S(2)}) collective-permute-start(bf16[96,1664]{1,0:T(8,128)(2,1)S(1)} %get-tuple-element.69), channel_id=1, source_target_pairs={{0,1},{1,0},{2,3},{3,2},{4,5},{5,4},{6,7},{7,6},{8,9},{9,8},{10,11... | collective-permute-start | bytes 958472 | tf_op jit(solution)/shard_map/ppermute | solution.py:282
  35.6 6.2 %collective-permute-start.20 = (bf16[24,1664]{1,0:T(8,128)(2,1)S(1)}, bf16[24,1664]{1,0:T(8,128)(2,1)S(1)}, u32[]{:S(2)}, u32[]{:S(2)}) collective-permute-start(bf16[24,1664]{1,0:T(8,128)(2,1)S(1)} %get-tuple-element.79), channel_id=1, source_target_pairs={{0,6},{1,7},{2,4},{3,5},{4,2},{5,3},{6,0},{7,1},{8,14},{9,15},{10,... | collective-permute-start | bytes 239624 | tf_op jit(solution)/shard_map/ppermute | solution.py:282
  37.2 5.6 %collective-permute-start.21 = (bf16[24,1664]{1,0:T(8,128)(2,1)S(1)}, bf16[24,1664]{1,0:T(8,128)(2,1)S(1)}, u32[]{:S(2)}, u32[]{:S(2)}) collective-permute-start(bf16[24,1664]{1,0:T(8,128)(2,1)S(1)} %get-tuple-element.80), channel_id=1, source_target_pairs={{0,4},{1,5},{2,6},{3,7},{4,0},{5,1},{6,2},{7,3},{8,12},{9,13},{10,... | collective-permute-start | bytes 239624 | tf_op jit(solution)/shard_map/ppermute | solution.py:282
  37.7 5.6 %collective-permute-start.22 = (bf16[24,1664]{1,0:T(8,128)(2,1)S(1)}, bf16[24,1664]{1,0:T(8,128)(2,1)S(1)}, u32[]{:S(2)}, u32[]{:S(2)}) collective-permute-start(bf16[24,1664]{1,0:T(8,128)(2,1)S(1)} %get-tuple-element.81), channel_id=1, source_target_pairs={{0,2},{1,3},{2,0},{3,1},{4,6},{5,7},{6,4},{7,5},{8,10},{9,11},{10,... | collective-permute-start | bytes 239624 | tf_op jit(solution)/shard_map/ppermute | solution.py:282
  39.3 6.6 %collective-permute-start.16 = (bf16[24,1664]{1,0:T(8,128)(2,1)S(1)}, bf16[24,1664]{1,0:T(8,128)(2,1)S(1)}, u32[]{:S(2)}, u32[]{:S(2)}) collective-permute-start(bf16[24,1664]{1,0:T(8,128)(2,1)S(1)} %get-tuple-element.71), channel_id=1, source_target_pairs={{0,6},{1,7},{2,4},{3,5},{4,2},{5,3},{6,0},{7,1},{8,14},{9,15},{10,... | collective-permute-start | bytes 239624 | tf_op jit(solution)/shard_map/ppermute | solution.py:282
  40.9 5.0 %collective-permute-start.17 = (bf16[24,1664]{1,0:T(8,128)(2,1)S(1)}, bf16[24,1664]{1,0:T(8,128)(2,1)S(1)}, u32[]{:S(2)}, u32[]{:S(2)}) collective-permute-start(bf16[24,1664]{1,0:T(8,128)(2,1)S(1)} %get-tuple-element.72), channel_id=1, source_target_pairs={{0,4},{1,5},{2,6},{3,7},{4,0},{5,1},{6,2},{7,3},{8,12},{9,13},{10,... | collective-permute-start | bytes 239624 | tf_op jit(solution)/shard_map/ppermute | solution.py:282
  41.8 4.5 %collective-permute-start.18 = (bf16[24,1664]{1,0:T(8,128)(2,1)S(1)}, bf16[24,1664]{1,0:T(8,128)(2,1)S(1)}, u32[]{:S(2)}, u32[]{:S(2)}) collective-permute-start(bf16[24,1664]{1,0:T(8,128)(2,1)S(1)} %get-tuple-element.73), channel_id=1, source_target_pairs={{0,2},{1,3},{2,0},{3,1},{4,6},{5,7},{6,4},{7,5},{8,10},{9,11},{10,... | collective-permute-start | bytes 239624 | tf_op jit(solution)/shard_map/ppermute | solution.py:282
  43.5 5.3 %collective-permute-start.23 = (bf16[24,1664]{1,0:T(8,128)(2,1)S(1)}, bf16[24,1664]{1,0:T(8,128)(2,1)S(1)}, u32[]{:S(2)}, u32[]{:S(2)}) collective-permute-start(bf16[24,1664]{1,0:T(8,128)(2,1)S(1)} %other.1), channel_id=1, source_target_pairs={{0,8},{1,9},{2,10},{3,11},{4,12},{5,13},{6,14},{7,15},{8,0},{9,1},... | collective-permute-start | bytes 239624 | tf_op jit(solution)/shard_map/ppermute | solution.py:282

commit v5 on v4

--- a/solution.py
+++ b/solution.py
@@ -41,15 +41,10 @@
     return jax.ShapeDtypeStruct(shape, dtype)
 
 
-def pick_kernel(mine_ref, ids_hbm, gates_hbm, tok_hbm, cot_hbm, own_ref, other_ref, ids_ref, place_ref, weight_ref, gates_ref, tok_ref, cot_ref, sems):
-    pairs = ((ids_hbm, ids_ref), (gates_hbm, gates_ref), (tok_hbm, tok_ref), (cot_hbm, cot_ref))
-    copies = [pltpu.make_async_copy(a, b, sems.at[i]) for i, (a, b) in enumerate(pairs)]
-    for copy in copies:
-        copy.start()
+def slots(mine, ids_ref, gates_ref=None):
     rows = 2 * PAIR
     count = ids_ref.shape[1]
     row = lax.broadcasted_iota(jnp.int32, (rows, count), 0)
-    mine = mine_ref[0]
     expert = jnp.where(row < PAIR, mine, EXP_WIN - 1 - mine)
     before = jnp.where(
         lax.broadcasted_iota(jnp.int32, (count, count), 0)
@@ -62,18 +57,25 @@
     first = (taken == 0) | (taken == 2)
     named = jnp.zeros((rows, count), F32)
     weight = jnp.zeros((rows, count), F32)
-    copies[0].wait()
-    copies[1].wait()
     for k in range(ids_ref.shape[0]):
         same = ids_ref[k : k + 1, :] == expert
         named = named + jnp.where(same, 1.0, 0.0)
-        weight = weight + jnp.where(same, gates_ref[k : k + 1, :], 0.0)
-    slot = jnp.dot(named, before, preferred_element_type=F32)
+        if gates_ref is not None:
+            weight = weight + jnp.where(same, gates_ref[k : k + 1, :], 0.0)
+    slot = jnp.dot(named.astype(BF16), before.astype(BF16), preferred_element_type=F32)
     place = jnp.where((slot == want) & (named > 0.5), 1.0, 0.0)
+    return first, place, weight
+
+
+def pick_kernel(mine_ref, ids_hbm, tok_hbm, cot_hbm, own_ref, other_ref, ids_ref, tok_ref, cot_ref, sems):
+    pairs = ((ids_hbm, ids_ref), (tok_hbm, tok_ref), (cot_hbm, cot_ref))
+    copies = [pltpu.make_async_copy(a, b, sems.at[i]) for i, (a, b) in enumerate(pairs)]
+    for copy in copies:
+        copy.start()
+    copies[0].wait()
+    first, place, _ = slots(mine_ref[0], ids_ref)
     upper = jnp.where(first, place, 0.0).astype(BF16)
     lower = jnp.where(first, 0.0, place).astype(BF16)
-    copies[2].wait()
-    copies[3].wait()
 
     def rows_of(part, a, b):
         picked = jnp.dot(upper[part], a, preferred_element_type=F32)
@@ -81,10 +83,9 @@
 
     half = tok_ref.shape[1] // 2
     for i, ref in enumerate((tok_ref, cot_ref)):
-        other_ref[PAIR * i : PAIR * (i + 1), :] = rows_of(slice(PAIR, rows), ref[:, :half], ref[:, half:])
+        copies[i + 1].wait()
+        other_ref[PAIR * i : PAIR * (i + 1), :] = rows_of(slice(PAIR, None), ref[:, :half], ref[:, half:])
     own_ref[...] = rows_of(slice(0, PAIR), tok_ref[...], cot_ref[...])
-    place_ref[...] = place
-    weight_ref[...] = place * weight
 
 
 def split_two(x):
@@ -92,8 +93,10 @@
     return high, x - high
 
 
-def layout_kernel(weight_ref, *out_refs):
-    weight = weight_ref[...]
+def layout_kernel(mine_ref, ids_ref, gates_ref, place_ref, *out_refs):
+    _, place, weight = slots(mine_ref[0], ids_ref, gates_ref)
+    place_ref[...] = place
+    weight = place * weight
     for i, (part, lows) in enumerate(((weight[:PAIR], 1), (weight[PAIR:], 0))):
         high, low = split_two(part)
         parts = [high, low] + [high] * lows
@@ -284,25 +287,23 @@
     def like(x):
         return pltpu.VMEM(x.shape, x.dtype)
 
-    own, other, ids, place, weight = call(
+    own, other = call(
         pick_kernel,
         "pick",
-        [struct((PAIR, width), BF16), struct((2 * PAIR, width // 2), BF16)]
-        + [struct(ids.shape, ids.dtype)]
-        + [struct((2 * PAIR, count), F32)] * 2,
-        [SMEM] + [HBM] * 4,
-        (mine, ids, gates, tokens, cotangent),
-        [like(gates), like(tokens), like(cotangent), pltpu.SemaphoreType.DMA((4,))],
+        [struct((PAIR, width), BF16), struct((2 * PAIR, width // 2), BF16)],
+        [SMEM] + [HBM] * 3,
+        (mine, ids, tokens, cotangent),
+        [like(ids), like(tokens), like(cotangent), pltpu.SemaphoreType.DMA((3,))],
         flops=4 * 2 * PAIR * count * width,
         limit=PICK_LIMIT,
     )
     weights = (w_gate.T, w_up.T, w_down)
-    *own_weight, left, right = call(
+    place, *own_weight, left, right = call(
         layout_kernel,
         "layout",
-        [struct((count, LANES), BF16)] * 4,
-        [VMEM],
-        (weight,),
+        [struct((2 * PAIR, count), F32)] + [struct((count, LANES), BF16)] * 4,
+        [SMEM] + [VMEM] * 2,
+        (mine, ids, gates),
     )
 
     def near(block):

time: 50 us -> 49.9 us (level)
  no operation moved by 1% of the time
where the time goes in v5:
time: 49.9 us; the launch traced here: 49.8 us
  starting transfers between devices  22.5 us (45%)
  waiting for transfers between devices  15.6 us (31%)
  Pallas kernels  10.9 us (22%)
  between operations  0.78 us (2%)
    ppermute x24, starting transfers between devices, swap(): return lax.ppermute(x, 'expert', [(i, i ^ offset) for i in range(devices)])  22.5 us
    ppermute x24, waiting for transfers between devices, swap(): return lax.ppermute(x, 'expert', [(i, i ^ offset) for i in range(devices)])  15.6 us
    pallas_call x11, Pallas kernels, call(): pl.pallas_call(kernel, name=name, out_shape=out_shape, in_specs=in_specs,...  10.9 us
  transfers between devices with their start and end apart: 24, of which 15 were waited for; matrix products, arithmetic and copies ran while one was open for 0% of the time, Pallas kernels for 2%

profile of v5, /device:TPU:0, one launch (start us, length us, event | category | flops | bytes accessed | tf_op | source)
XLA Modules:
  0.0 49.8 jit_solution(11663807395169992599)
XLA Ops:
  0.6 2.2 %pick.1 = (bf16[24,3072]{1,0:T(8,128)(2,1)}, bf16[48,1536]{1,0:T(8,128)(2,1)}) custom-call(s32[1]{0:T(128)} %bitcast.mine_ref, s32[4,64]{1,0:T(4,128)} %bitcast.10, bf16[64,3072]{1,0:T(8,128)(2,1)} %tok_hbm.1, bf16[64,3072]{1,0:T(8,128)(2,1)} %cot_hbm.1), custom_call_target="tpu_custom_call" | custom-call | flops 37748736 | bytes 1082372 | tf_op jit(solution)/shard_map/pick/pallas_call | solution.py:28
  2.9 0.0 copy-start.3
  2.9 4.1 %collective-permute-start.3 = (bf16[48,1536]{1,0:T(8,128)(2,1)}, bf16[48,1536]{1,0:T(8,128)(2,1)S(1)}, u32[]{:S(2)}, u32[]{:S(2)}) collective-permute-start(bf16[48,1536]{1,0:T(8,128)(2,1)} %get-tuple-element.48), channel_id=1, source_target_pairs={{0,8},{1,9},{2,10},{3,11},{4,12},{5,13},{6,14},{7,15},{8,0},{9,1},... | collective-permute-start | bytes 442376 | tf_op jit(solution)/shard_map/ppermute | solution.py:285
  7.0 2.6 %collective-permute-start = (bf16[24,3072]{1,0:T(8,128)(2,1)S(1)}, bf16[24,3072]{1,0:T(8,128)(2,1)S(1)}, u32[]{:S(2)}, u32[]{:S(2)}) collective-permute-start(bf16[24,3072]{1,0:T(8,128)(2,1)S(1)} %copy-done.3), channel_id=1, source_target_pairs={{0,6},{1,7},{2,4},{3,5},{4,2},{5,3},{6,0},{7,1},{8,14},{9,15},{10,... | collective-permute-start | bytes 442376 | tf_op jit(solution)/shard_map/ppermute | solution.py:285
  9.6 0.4 collective-permute-start.1
  10.0 0.5 %collective-permute-start.2 = (bf16[24,3072]{1,0:T(8,128)(2,1)S(1)}, bf16[24,3072]{1,0:T(8,128)(2,1)S(1)}, u32[]{:S(2)}, u32[]{:S(2)}) collective-permute-start(bf16[24,3072]{1,0:T(8,128)(2,1)S(1)} %copy-done.3), channel_id=1, source_target_pairs={{0,2},{1,3},{2,0},{3,1},{4,6},{5,7},{6,4},{7,5},{8,10},{9,11},{10,... | collective-permute-start | bytes 442376 | tf_op jit(solution)/shard_map/ppermute | solution.py:285
  10.5 3.7 %collective-permute-done.3.refs_8_ = bf16[48,1536]{1,0:T(8,128)(2,1)S(1)} collective-permute-done((bf16[48,1536]{1,0:T(8,128)(2,1)}, bf16[48,1536]{1,0:T(8,128)(2,1)S(1)}, u32[]{:S(2)}, u32[]{:S(2)}) %collective-permute-start.3) | collective-permute-done | bytes 147488 | tf_op jit(solution)/shard_map/ppermute | solution.py:285
  14.3 1.7 %collective-permute-start.10 = (bf16[48,1536]{1,0:T(8,128)(2,1)S(1)}, bf16[48,1536]{1,0:T(8,128)(2,1)S(1)}, u32[]{:S(2)}, u32[]{:S(2)}) collective-permute-start(bf16[48,1536]{1,0:T(8,128)(2,1)S(1)} %collective-permute-done.3.refs_8_), channel_id=1, source_target_pairs={{0,6},{1,7},{2,4},{3,5},{4,2},{5,3},{6,0},{7,1},{8,14},{9,15},{10,... | collective-permute-start | bytes 442376 | tf_op jit(solution)/shard_map/ppermute | solution.py:285
  16.0 0.5 %collective-permute-start.8 = (bf16[48,1536]{1,0:T(8,128)(2,1)S(1)}, bf16[48,1536]{1,0:T(8,128)(2,1)S(1)}, u32[]{:S(2)}, u32[]{:S(2)}) collective-permute-start(bf16[48,1536]{1,0:T(8,128)(2,1)S(1)} %collective-permute-done.3.refs_8_), channel_id=1, source_target_pairs={{0,2},{1,3},{2,0},{3,1},{4,6},{5,7},{6,4},{7,5},{8,10},{9,11},{10,... | collective-permute-start | bytes 442376 | tf_op jit(solution)/shard_map/ppermute | solution.py:285
  16.5 0.2 collective-permute-done.refs_1_
  16.8 1.3 %collective-permute-start.9 = (bf16[48,1536]{1,0:T(8,128)(2,1)S(1)}, bf16[48,1536]{1,0:T(8,128)(2,1)S(1)}, u32[]{:S(2)}, u32[]{:S(2)}) collective-permute-start(bf16[48,1536]{1,0:T(8,128)(2,1)S(1)} %collective-permute-done.3.refs_8_), channel_id=1, source_target_pairs={{0,4},{1,5},{2,6},{3,7},{4,0},{5,1},{6,2},{7,3},{8,12},{9,13},{10,... | collective-permute-start | bytes 442376 | tf_op jit(solution)/shard_map/ppermute | solution.py:285
  18.1 1.6 %collective-permute-done.1.refs_2_ = bf16[24,3072]{1,0:T(8,128)(2,1)S(1)} collective-permute-done((bf16[24,3072]{1,0:T(8,128)(2,1)S(1)}, bf16[24,3072]{1,0:T(8,128)(2,1)S(1)}, u32[]{:S(2)}, u32[]{:S(2)}) %collective-permute-start.1) | collective-permute-done | bytes 147488 | tf_op jit(solution)/shard_map/ppermute | solution.py:285
  19.7 0.0 collective-permute-done.2.refs_3_
  19.7 0.5 %collective-permute-start.5 = (bf16[24,3072]{1,0:T(8,128)(2,1)S(1)}, bf16[24,3072]{1,0:T(8,128)(2,1)S(1)}, u32[]{:S(2)}, u32[]{:S(2)}) collective-permute-start(bf16[24,3072]{1,0:T(8,128)(2,1)S(1)} %collective-permute-done.refs_1_), channel_id=1, source_target_pairs={{0,1},{1,0},{2,3},{3,2},{4,5},{5,4},{6,7},{7,6},{8,9},{9,8},{10,11... | collective-permute-start | bytes 442376 | tf_op jit(solution)/shard_map/ppermute | solution.py:285
  20.2 2.9 %collective-permute-done.10.refs_9_ = bf16[48,1536]{1,0:T(8,128)(2,1)S(1)} collective-permute-done((bf16[48,1536]{1,0:T(8,128)(2,1)S(1)}, bf16[48,1536]{1,0:T(8,128)(2,1)S(1)}, u32[]{:S(2)}, u32[]{:S(2)}) %collective-permute-start.10) | collective-permute-done | bytes 147488 | tf_op jit(solution)/shard_map/ppermute | solution.py:285
  23.1 0.9 %collective-permute-done.8.refs_11_ = bf16[48,1536]{1,0:T(8,128)(2,1)S(1)} collective-permute-done((bf16[48,1536]{1,0:T(8,128)(2,1)S(1)}, bf16[48,1536]{1,0:T(8,128)(2,1)S(1)}, u32[]{:S(2)}, u32[]{:S(2)}) %collective-permute-start.8) | collective-permute-done | bytes 147488 | tf_op jit(solution)/shard_map/ppermute | solution.py:285
  24.0 0.8 %collective-permute-done.9.refs_10_ = bf16[48,1536]{1,0:T(8,128)(2,1)S(1)} collective-permute-done((bf16[48,1536]{1,0:T(8,128)(2,1)S(1)}, bf16[48,1536]{1,0:T(8,128)(2,1)S(1)}, u32[]{:S(2)}, u32[]{:S(2)}) %collective-permute-start.9) | collective-permute-done | bytes 147488 | tf_op jit(solution)/shard_map/ppermute | solution.py:285
  24.8 0.5 %collective-permute-start.12 = (bf16[48,1536]{1,0:T(8,128)(2,1)S(1)}, bf16[48,1536]{1,0:T(8,128)(2,1)S(1)}, u32[]{:S(2)}, u32[]{:S(2)}) collective-permute-start(bf16[48,1536]{1,0:T(8,128)(2,1)S(1)} %collective-permute-done.10.refs_9_), channel_id=1, source_target_pairs={{0,1},{1,0},{2,3},{3,2},{4,5},{5,4},{6,7},{7,6},{8,9},{9,8},{10,11... | collective-permute-start | bytes 442376 | tf_op jit(solution)/shard_map/ppermute | solution.py:285
  25.3 0.1 collective-permute-start.13
  25.4 0.4 collective-permute-start.14
  25.8 0.3 collective-permute-done.7.refs_7_
  26.2 0.2 collective-permute-done.12.refs_13_
  26.4 0.3 collective-permute-done.13.refs_14_
  26.7 0.2 collective-permute-done.14.refs_15_
  26.9 2.6 %forward.1 = (f32[672,256]{1,0:T(8,128)S(1)}, f32[672,256]{1,0:T(8,128)S(1)}, bf16[672,256]{1,0:T(8,128)(2,1)S(1)}) custom-call(bf16[24,3072]{1,0:T(8,128)(2,1)S(1)} %copy-done.3, bf16[24,3072]{1,0:T(8,128)(2,1)S(1)} %collective-permute-done.refs_1_, bf16[24,3072]{1,0:T(8,128)(2,1)S(1)} %collective-permute-done.1.refs_2_, ...), custom_call_target="tpu_custom_call" | custom-call | flops 2113929216 | bytes 12341248 | tf_op jit(solution)/shard_map/forward/pallas_call | solution.py:28
  29.5 0.0 copy-start.4
  29.5 0.0 copy-start.5
  29.6 4.1 %backward.1 = (bf16[96,1664]{1,0:T(8,128)(2,1)S(1)}, bf16[96,1664]{1,0:T(8,128)(2,1)S(1)}, bf16[96,1664]{1,0:T(8,128)(2,1)S(1)}, bf16[96,1664]{1,0:T(8,128)(2,1)S(1)}) custom-call(bf16[24,3072]{1,0:T(8,128)(2,1)S(1)} %copy-done.3, bf16[24,3072]{1,0:T(8,128)(2,1)S(1)} %collective-permute-done.refs_1_, bf16[24,3072]{1,0:T(8,128)(2,1)S(1)} %collective-permute-done.1.refs_2_, ...), custom_call_target="tpu_custom_call" | custom-call | flops 3170893824 | bytes 17743872 | tf_op jit(solution)/shard_map/backward/pallas_call | solution.py:28
  33.7 0.4 collective-permute-start.19
  34.0 0.2 collective-permute-start.15
  34.3 1.1 %collective-permute-done.19.got_ref = bf16[96,1664]{1,0:T(8,128)(2,1)S(1)} collective-permute-done((bf16[96,1664]{1,0:T(8,128)(2,1)S(1)}, bf16[96,1664]{1,0:T(8,128)(2,1)S(1)}, u32[]{:S(2)}, u32[]{:S(2)}) %collective-permute-start.19) | collective-permute-done | bytes 319520 | tf_op jit(solution)/shard_map/ppermute | solution.py:285
  35.4 0.2 chip.3
  35.5 1.7 %collective-permute-start.20 = (bf16[24,1664]{1,0:T(8,128)(2,1)S(1)}, bf16[24,1664]{1,0:T(8,128)(2,1)S(1)}, u32[]{:S(2)}, u32[]{:S(2)}) collective-permute-start(bf16[24,1664]{1,0:T(8,128)(2,1)S(1)} %get-tuple-element.75), channel_id=1, source_target_pairs={{0,6},{1,7},{2,4},{3,5},{4,2},{5,3},{6,0},{7,1},{8,14},{9,15},{10,... | collective-permute-start | bytes 239624 | tf_op jit(solution)/shard_map/ppermute | solution.py:285
  37.2 0.5 collective-permute-start.21
  37.7 1.4 %collective-permute-start.22 = (bf16[24,1664]{1,0:T(8,128)(2,1)S(1)}, bf16[24,1664]{1,0:T(8,128)(2,1)S(1)}, u32[]{:S(2)}, u32[]{:S(2)}) collective-permute-start(bf16[24,1664]{1,0:T(8,128)(2,1)S(1)} %get-tuple-element.77), channel_id=1, source_target_pairs={{0,2},{1,3},{2,0},{3,1},{4,6},{5,7},{6,4},{7,5},{8,10},{9,11},{10,... | collective-permute-start | bytes 239624 | tf_op jit(solution)/shard_map/ppermute | solution.py:285
  39.1 0.2 chip.2
  39.2 1.7 %collective-permute-start.16 = (bf16[24,1664]{1,0:T(8,128)(2,1)S(1)}, bf16[24,1664]{1,0:T(8,128)(2,1)S(1)}, u32[]{:S(2)}, u32[]{:S(2)}) collective-permute-start(bf16[24,1664]{1,0:T(8,128)(2,1)S(1)} %get-tuple-element.67), channel_id=1, source_target_pairs={{0,6},{1,7},{2,4},{3,5},{4,2},{5,3},{6,0},{7,1},{8,14},{9,15},{10,... | collective-permute-start | bytes 239624 | tf_op jit(solution)/shard_map/ppermute | solution.py:285
  40.9 0.5 collective-permute-start.17
  41.4 0.3 collective-permute-done.20.refs_1_
  41.7 1.1 %collective-permute-start.18 = (bf16[24,1664]{1,0:T(8,128)(2,1)S(1)}, bf16[24,1664]{1,0:T(8,128)(2,1)S(1)}, u32[]{:S(2)}, u32[]{:S(2)}) collective-permute-start(bf16[24,1664]{1,0:T(8,128)(2,1)S(1)} %get-tuple-element.69), channel_id=1, source_target_pairs={{0,2},{1,3},{2,0},{3,1},{4,6},{5,7},{6,4},{7,5},{8,10},{9,11},{10,... | collective-permute-start | bytes 239624 | tf_op jit(solution)/shard_map/ppermute | solution.py:285
  42.8 0.5 collective-permute-done.22.refs_3_
  43.3 0.2 other.1
  43.4 2.4 %collective-permute-start.23 = (bf16[24,1664]{1,0:T(8,128)(2,1)S(1)}, bf16[24,1664]{1,0:T(8,128)(2,1)S(1)}, u32[]{:S(2)}, u32[]{:S(2)}) collective-permute-start(bf16[24,1664]{1,0:T(8,128)(2,1)S(1)} %other.1), channel_id=1, source_target_pairs={{0,8},{1,9},{2,10},{3,11},{4,12},{5,13},{6,14},{7,15},{8,0},{9,1},... | collective-permute-start | bytes 239624 | tf_op jit(solution)/shard_map/ppermute | solution.py:285
  45.8 0.2 layout.1
  46.1 0.1 collective-permute-done.18.refs_3_
  46.2 0.3 own.1
  46.5 2.3 %collective-permute-done.23.back_ref = bf16[24,1664]{1,0:T(8,128)(2,1)S(1)} collective-permute-done((bf16[24,1664]{1,0:T(8,128)(2,1)S(1)}, bf16[24,1664]{1,0:T(8,128)(2,1)S(1)}, u32[]{:S(2)}, u32[]{:S(2)}) %collective-permute-start.23) | collective-permute-done | bytes 79904 | tf_op jit(solution)/shard_map/ppermute | solution.py:285
  48.8 1.0 %final.1 = (bf16[64,3072]{1,0:T(8,128)(2,1)}, f32[4,64]{1,0:T(4,128)}) custom-call(s32[1]{0:T(128)} %bitcast.mine_ref, s32[4,64]{1,0:T(4,128)S(1)} %bitcast.12, f32[48,64]{1,0:T(8,128)S(1)} %get-tuple-element.41.place_ref, bf16[64,128]{1,0:T(8,128)(2,1)S(1)} %get-tuple-element.42.left_ref, bf16[64,128]{1,0:T(8,128)(2,1)S(1)} %get-tuple-element.43.right_ref, ...), custom_call_target="tpu_custom_call" | custom-call | bytes 1318916 | tf_op jit(solution)/shard_map/final/pallas_call | solution.py:28
  (23 shorter events, 0.1 us)
Async XLA Ops:
  2.9 4.1 %copy-start.3 = (bf16[24,3072]{1,0:T(8,128)(2,1)S(1)}, bf16[24,3072]{1,0:T(8,128)(2,1)}, u32[]{:S(2)}) copy-start(bf16[24,3072]{1,0:T(8,128)(2,1)} %get-tuple-element.51.refs_0_) | copy-start | bytes 442372
  2.9 11.4 %collective-permute-start.3 = (bf16[48,1536]{1,0:T(8,128)(2,1)}, bf16[48,1536]{1,0:T(8,128)(2,1)S(1)}, u32[]{:S(2)}, u32[]{:S(2)}) collective-permute-start(bf16[48,1536]{1,0:T(8,128)(2,1)} %get-tuple-element.48), channel_id=1, source_target_pairs={{0,8},{1,9},{2,10},{3,11},{4,12},{5,13},{6,14},{7,15},{8,0},{9,1},... | collective-permute-start | bytes 442376 | tf_op jit(solution)/shard_map/ppermute | solution.py:285
  7.0 19.9 %copy-start = (bf16[3072,672]{0,1:T(8,128)(2,1)S(1)}, bf16[3072,672]{0,1:T(8,128)(2,1)}, u32[]{:S(2)}) copy-start(bf16[3072,672]{0,1:T(8,128)(2,1)} %param.11) | copy-start | bytes 12386308
  7.0 19.9 %copy-start.1 = (bf16[3072,672]{0,1:T(8,128)(2,1)S(1)}, bf16[3072,672]{0,1:T(8,128)(2,1)}, u32[]{:S(2)}) copy-start(bf16[3072,672]{0,1:T(8,128)(2,1)} %param.12) | copy-start | bytes 12386308
  7.0 9.8 %collective-permute-start = (bf16[24,3072]{1,0:T(8,128)(2,1)S(1)}, bf16[24,3072]{1,0:T(8,128)(2,1)S(1)}, u32[]{:S(2)}, u32[]{:S(2)}) collective-permute-start(bf16[24,3072]{1,0:T(8,128)(2,1)S(1)} %copy-done.3), channel_id=1, source_target_pairs={{0,6},{1,7},{2,4},{3,5},{4,2},{5,3},{6,0},{7,1},{8,14},{9,15},{10,... | collective-permute-start | bytes 442376 | tf_op jit(solution)/shard_map/ppermute | solution.py:285
  9.6 10.1 %collective-permute-start.1 = (bf16[24,3072]{1,0:T(8,128)(2,1)S(1)}, bf16[24,3072]{1,0:T(8,128)(2,1)S(1)}, u32[]{:S(2)}, u32[]{:S(2)}) collective-permute-start(bf16[24,3072]{1,0:T(8,128)(2,1)S(1)} %copy-done.3), channel_id=1, source_target_pairs={{0,4},{1,5},{2,6},{3,7},{4,0},{5,1},{6,2},{7,3},{8,12},{9,13},{10,... | collective-permute-start | bytes 442376 | tf_op jit(solution)/shard_map/ppermute | solution.py:285
  10.0 9.7 %collective-permute-start.2 = (bf16[24,3072]{1,0:T(8,128)(2,1)S(1)}, bf16[24,3072]{1,0:T(8,128)(2,1)S(1)}, u32[]{:S(2)}, u32[]{:S(2)}) collective-permute-start(bf16[24,3072]{1,0:T(8,128)(2,1)S(1)} %copy-done.3), channel_id=1, source_target_pairs={{0,2},{1,3},{2,0},{3,1},{4,6},{5,7},{6,4},{7,5},{8,10},{9,11},{10,... | collective-permute-start | bytes 442376 | tf_op jit(solution)/shard_map/ppermute | solution.py:285
  14.3 8.8 %collective-permute-start.10 = (bf16[48,1536]{1,0:T(8,128)(2,1)S(1)}, bf16[48,1536]{1,0:T(8,128)(2,1)S(1)}, u32[]{:S(2)}, u32[]{:S(2)}) collective-permute-start(bf16[48,1536]{1,0:T(8,128)(2,1)S(1)} %collective-permute-done.3.refs_8_), channel_id=1, source_target_pairs={{0,6},{1,7},{2,4},{3,5},{4,2},{5,3},{6,0},{7,1},{8,14},{9,15},{10,... | collective-permute-start | bytes 442376 | tf_op jit(solution)/shard_map/ppermute | solution.py:285
  16.0 8.0 %collective-permute-start.8 = (bf16[48,1536]{1,0:T(8,128)(2,1)S(1)}, bf16[48,1536]{1,0:T(8,128)(2,1)S(1)}, u32[]{:S(2)}, u32[]{:S(2)}) collective-permute-start(bf16[48,1536]{1,0:T(8,128)(2,1)S(1)} %collective-permute-done.3.refs_8_), channel_id=1, source_target_pairs={{0,2},{1,3},{2,0},{3,1},{4,6},{5,7},{6,4},{7,5},{8,10},{9,11},{10,... | collective-permute-start | bytes 442376 | tf_op jit(solution)/shard_map/ppermute | solution.py:285
  16.8 8.0 %collective-permute-start.9 = (bf16[48,1536]{1,0:T(8,128)(2,1)S(1)}, bf16[48,1536]{1,0:T(8,128)(2,1)S(1)}, u32[]{:S(2)}, u32[]{:S(2)}) collective-permute-start(bf16[48,1536]{1,0:T(8,128)(2,1)S(1)} %collective-permute-done.3.refs_8_), channel_id=1, source_target_pairs={{0,4},{1,5},{2,6},{3,7},{4,0},{5,1},{6,2},{7,3},{8,12},{9,13},{10,... | collective-permute-start | bytes 442376 | tf_op jit(solution)/shard_map/ppermute | solution.py:285
  19.7 5.1 %collective-permute-start.4 = (bf16[24,3072]{1,0:T(8,128)(2,1)S(1)}, bf16[24,3072]{1,0:T(8,128)(2,1)S(1)}, u32[]{:S(2)}, u32[]{:S(2)}) collective-permute-start(bf16[24,3072]{1,0:T(8,128)(2,1)S(1)} %copy-done.3), channel_id=1, source_target_pairs={{0,1},{1,0},{2,3},{3,2},{4,5},{5,4},{6,7},{7,6},{8,9},{9,8},{10,11... | collective-permute-start | bytes 442376 | tf_op jit(solution)/shard_map/ppermute | solution.py:285
  19.7 5.6 %collective-permute-start.5 = (bf16[24,3072]{1,0:T(8,128)(2,1)S(1)}, bf16[24,3072]{1,0:T(8,128)(2,1)S(1)}, u32[]{:S(2)}, u32[]{:S(2)}) collective-permute-start(bf16[24,3072]{1,0:T(8,128)(2,1)S(1)} %collective-permute-done.refs_1_), channel_id=1, source_target_pairs={{0,1},{1,0},{2,3},{3,2},{4,5},{5,4},{6,7},{7,6},{8,9},{9,8},{10,11... | collective-permute-start | bytes 442376 | tf_op jit(solution)/shard_map/ppermute | solution.py:285
  23.1 2.3 %collective-permute-start.6 = (bf16[24,3072]{1,0:T(8,128)(2,1)S(1)}, bf16[24,3072]{1,0:T(8,128)(2,1)S(1)}, u32[]{:S(2)}, u32[]{:S(2)}) collective-permute-start(bf16[24,3072]{1,0:T(8,128)(2,1)S(1)} %collective-permute-done.1.refs_2_), channel_id=1, source_target_pairs={{0,1},{1,0},{2,3},{3,2},{4,5},{5,4},{6,7},{7,6},{8,9},{9,8},{10,11... | collective-permute-start | bytes 442376 | tf_op jit(solution)/shard_map/ppermute | solution.py:285
  24.0 2.2 %collective-permute-start.11 = (bf16[48,1536]{1,0:T(8,128)(2,1)S(1)}, bf16[48,1536]{1,0:T(8,128)(2,1)S(1)}, u32[]{:S(2)}, u32[]{:S(2)}) collective-permute-start(bf16[48,1536]{1,0:T(8,128)(2,1)S(1)} %collective-permute-done.3.refs_8_), channel_id=1, source_target_pairs={{0,1},{1,0},{2,3},{3,2},{4,5},{5,4},{6,7},{7,6},{8,9},{9,8},{10,11... | collective-permute-start | bytes 442376 | tf_op jit(solution)/shard_map/ppermute | solution.py:285
  24.8 1.4 %collective-permute-start.7 = (bf16[24,3072]{1,0:T(8,128)(2,1)S(1)}, bf16[24,3072]{1,0:T(8,128)(2,1)S(1)}, u32[]{:S(2)}, u32[]{:S(2)}) collective-permute-start(bf16[24,3072]{1,0:T(8,128)(2,1)S(1)} %collective-permute-done.2.refs_3_), channel_id=1, source_target_pairs={{0,1},{1,0},{2,3},{3,2},{4,5},{5,4},{6,7},{7,6},{8,9},{9,8},{10,11... | collective-permute-start | bytes 442376 | tf_op jit(solution)/shard_map/ppermute | solution.py:285
  24.8 1.6 %collective-permute-start.12 = (bf16[48,1536]{1,0:T(8,128)(2,1)S(1)}, bf16[48,1536]{1,0:T(8,128)(2,1)S(1)}, u32[]{:S(2)}, u32[]{:S(2)}) collective-permute-start(bf16[48,1536]{1,0:T(8,128)(2,1)S(1)} %collective-permute-done.10.refs_9_), channel_id=1, source_target_pairs={{0,1},{1,0},{2,3},{3,2},{4,5},{5,4},{6,7},{7,6},{8,9},{9,8},{10,11... | collective-permute-start | bytes 442376 | tf_op jit(solution)/shard_map/ppermute | solution.py:285
  25.3 1.4 %collective-permute-start.13 = (bf16[48,1536]{1,0:T(8,128)(2,1)S(1)}, bf16[48,1536]{1,0:T(8,128)(2,1)S(1)}, u32[]{:S(2)}, u32[]{:S(2)}) collective-permute-start(bf16[48,1536]{1,0:T(8,128)(2,1)S(1)} %collective-permute-done.9.refs_10_), channel_id=1, source_target_pairs={{0,1},{1,0},{2,3},{3,2},{4,5},{5,4},{6,7},{7,6},{8,9},{9,8},{10,11... | collective-permute-start | bytes 442376 | tf_op jit(solution)/shard_map/ppermute | solution.py:285
  25.4 1.5 %collective-permute-start.14 = (bf16[48,1536]{1,0:T(8,128)(2,1)S(1)}, bf16[48,1536]{1,0:T(8,128)(2,1)S(1)}, u32[]{:S(2)}, u32[]{:S(2)}) collective-permute-start(bf16[48,1536]{1,0:T(8,128)(2,1)S(1)} %collective-permute-done.8.refs_11_), channel_id=1, source_target_pairs={{0,1},{1,0},{2,3},{3,2},{4,5},{5,4},{6,7},{7,6},{8,9},{9,8},{10,11... | collective-permute-start | bytes 442376 | tf_op jit(solution)/shard_map/ppermute | solution.py:285
  26.9 2.6 %copy-start.2 = (bf16[672,3072]{1,0:T(8,128)(2,1)S(1)}, bf16[672,3072]{1,0:T(8,128)(2,1)}, u32[]{:S(2)}) copy-start(bf16[672,3072]{1,0:T(8,128)(2,1)} %refs_21_.1) | copy-start | bytes 12386308
  29.5 16.3 %copy-start.4 = (s32[64,4]{0,1:T(4,128)S(1)}, s32[64,4]{0,1:T(4,128)}, u32[]{:S(2)}) copy-start(s32[64,4]{0,1:T(4,128)} %param.10) | copy-start | bytes 3076
  29.5 16.3 %copy-start.5 = (f32[64,4]{0,1:T(4,128)S(1)}, f32[64,4]{0,1:T(4,128)}, u32[]{:S(2)}) copy-start(f32[64,4]{0,1:T(4,128)} %param.9) | copy-start | bytes 3076
  33.7 1.7 %collective-permute-start.19 = (bf16[96,1664]{1,0:T(8,128)(2,1)S(1)}, bf16[96,1664]{1,0:T(8,128)(2,1)S(1)}, u32[]{:S(2)}, u32[]{:S(2)}) collective-permute-start(bf16[96,1664]{1,0:T(8,128)(2,1)S(1)} %get-tuple-element.73), channel_id=1, source_target_pairs={{0,1},{1,0},{2,3},{3,2},{4,5},{5,4},{6,7},{7,6},{8,9},{9,8},{10,11... | collective-permute-start | bytes 958472 | tf_op jit(solution)/shard_map/ppermute | solution.py:285
  34.0 5.0 %collective-permute-start.15 = (bf16[96,1664]{1,0:T(8,128)(2,1)S(1)}, bf16[96,1664]{1,0:T(8,128)(2,1)S(1)}, u32[]{:S(2)}, u32[]{:S(2)}) collective-permute-start(bf16[96,1664]{1,0:T(8,128)(2,1)S(1)} %get-tuple-element.65), channel_id=1, source_target_pairs={{0,1},{1,0},{2,3},{3,2},{4,5},{5,4},{6,7},{7,6},{8,9},{9,8},{10,11... | collective-permute-start | bytes 958472 | tf_op jit(solution)/shard_map/ppermute | solution.py:285
  35.5 6.2 %collective-permute-start.20 = (bf16[24,1664]{1,0:T(8,128)(2,1)S(1)}, bf16[24,1664]{1,0:T(8,128)(2,1)S(1)}, u32[]{:S(2)}, u32[]{:S(2)}) collective-permute-start(bf16[24,1664]{1,0:T(8,128)(2,1)S(1)} %get-tuple-element.75), channel_id=1, source_target_pairs={{0,6},{1,7},{2,4},{3,5},{4,2},{5,3},{6,0},{7,1},{8,14},{9,15},{10,... | collective-permute-start | bytes 239624 | tf_op jit(solution)/shard_map/ppermute | solution.py:285
  37.2 5.6 %collective-permute-start.21 = (bf16[24,1664]{1,0:T(8,128)(2,1)S(1)}, bf16[24,1664]{1,0:T(8,128)(2,1)S(1)}, u32[]{:S(2)}, u32[]{:S(2)}) collective-permute-start(bf16[24,1664]{1,0:T(8,128)(2,1)S(1)} %get-tuple-element.76), channel_id=1, source_target_pairs={{0,4},{1,5},{2,6},{3,7},{4,0},{5,1},{6,2},{7,3},{8,12},{9,13},{10,... | collective-permute-start | bytes 239624 | tf_op jit(solution)/shard_map/ppermute | solution.py:285
  37.7 5.6 %collective-permute-start.22 = (bf16[24,1664]{1,0:T(8,128)(2,1)S(1)}, bf16[24,1664]{1,0:T(8,128)(2,1)S(1)}, u32[]{:S(2)}, u32[]{:S(2)}) collective-permute-start(bf16[24,1664]{1,0:T(8,128)(2,1)S(1)} %get-tuple-element.77), channel_id=1, source_target_pairs={{0,2},{1,3},{2,0},{3,1},{4,6},{5,7},{6,4},{7,5},{8,10},{9,11},{10,... | collective-permute-start | bytes 239624 | tf_op jit(solution)/shard_map/ppermute | solution.py:285
  39.2 6.8 %collective-permute-start.16 = (bf16[24,1664]{1,0:T(8,128)(2,1)S(1)}, bf16[24,1664]{1,0:T(8,128)(2,1)S(1)}, u32[]{:S(2)}, u32[]{:S(2)}) collective-permute-start(bf16[24,1664]{1,0:T(8,128)(2,1)S(1)} %get-tuple-element.67), channel_id=1, source_target_pairs={{0,6},{1,7},{2,4},{3,5},{4,2},{5,3},{6,0},{7,1},{8,14},{9,15},{10,... | collective-permute-start | bytes 239624 | tf_op jit(solution)/shard_map/ppermute | solution.py:285
  40.9 5.1 %collective-permute-start.17 = (bf16[24,1664]{1,0:T(8,128)(2,1)S(1)}, bf16[24,1664]{1,0:T(8,128)(2,1)S(1)}, u32[]{:S(2)}, u32[]{:S(2)}) collective-permute-start(bf16[24,1664]{1,0:T(8,128)(2,1)S(1)} %get-tuple-element.68), channel_id=1, source_target_pairs={{0,4},{1,5},{2,6},{3,7},{4,0},{5,1},{6,2},{7,3},{8,12},{9,13},{10,... | collective-permute-start | bytes 239624 | tf_op jit(solution)/shard_map/ppermute | solution.py:285
  41.7 4.5 %collective-permute-start.18 = (bf16[24,1664]{1,0:T(8,128)(2,1)S(1)}, bf16[24,1664]{1,0:T(8,128)(2,1)S(1)}, u32[]{:S(2)}, u32[]{:S(2)}) collective-permute-start(bf16[24,1664]{1,0:T(8,128)(2,1)S(1)} %get-tuple-element.69), channel_id=1, source_target_pairs={{0,2},{1,3},{2,0},{3,1},{4,6},{5,7},{6,4},{7,5},{8,10},{9,11},{10,... | collective-permute-start | bytes 239624 | tf_op jit(solution)/shard_map/ppermute | solution.py:285
  43.4 5.3 %collective-permute-start.23 = (bf16[24,1664]{1,0:T(8,128)(2,1)S(1)}, bf16[24,1664]{1,0:T(8,128)(2,1)S(1)}, u32[]{:S(2)}, u32[]{:S(2)}) collective-permute-start(bf16[24,1664]{1,0:T(8,128)(2,1)S(1)} %other.1), channel_id=1, source_target_pairs={{0,8},{1,9},{2,10},{3,11},{4,12},{5,13},{6,14},{7,15},{8,0},{9,1},... | collective-permute-start | bytes 239624 | tf_op jit(solution)/shard_map/ppermute | solution.py:285

commit v6 on v5

--- a/solution.py
+++ b/solution.py
@@ -269,6 +269,10 @@
     )
 
 
+def order_of(first, offsets):
+    return [i for i in first if i < len(offsets)] + list(range(len(first), len(offsets)))
+
+
 def per_device(tokens, cotangent, gate_weights, expert_ids, w_gate, w_up, w_down):
     devices = lax.axis_size("expert")
     split = devices // EXP_WIN
@@ -325,9 +329,11 @@
     other, token = together((other, token))
     own = near(own)
     far = [swap(other, k) for k in evens]
-    own, token = together((own, gate(token)))
-    far, token = together((far[::-1], token))
-    other = [other] + far[::-1]
+    own_order, far_order = order_of([0, 2, 1], evens), order_of([0, 1, 2], evens)
+    spread, token = together(([own[i + 1] for i in own_order], gate(token)))
+    own = [own[0]] + [spread[own_order.index(i)] for i in range(len(evens))]
+    spread, token = together(([far[i] for i in far_order], token))
+    other = [other] + [spread[far_order.index(i)] for i in range(len(evens))]
     own = both_cores(own)
     other = both_cores(other)
     states = call(

time: 49.9 us -> 50 us (level)
  waiting for transfers between devices: 15.6 us -> 16.2 us
  starting transfers between devices: 22.5 us -> 22 us
    ppermute x24, waiting for transfers between devices: 15.6 us -> 16.2 us  [swap(): return lax.ppermute(x, 'expert', [(i, i ^ offset) for i in range(devices)])]
    ppermute x24, starting transfers between devices: 22.5 us -> 22 us  [swap(): return lax.ppermute(x, 'expert', [(i, i ^ offset) for i in range(devices)])]
  transfers between devices with their start and end apart: 24 -> 24, of which waited for: 15 -> 14; matrix products, arithmetic and copies ran while one was open for 0% -> 0% of each run, Pallas kernels for 2% -> 2%
where the time goes in v6:
time: 50 us; the launch traced here: 49.8 us
  starting transfers between devices  22 us (44%)
  waiting for transfers between devices  16.2 us (32%)
  Pallas kernels  10.9 us (22%)
  between operations  0.78 us (2%)
    ppermute x24, starting transfers between devices, swap(): return lax.ppermute(x, 'expert', [(i, i ^ offset) for i in range(devices)])  22 us
    ppermute x24, waiting for transfers between devices, swap(): return lax.ppermute(x, 'expert', [(i, i ^ offset) for i in range(devices)])  16.2 us
    pallas_call x11, Pallas kernels, call(): pl.pallas_call(kernel, name=name, out_shape=out_shape, in_specs=in_specs,...  10.9 us
  transfers between devices with their start and end apart: 24, of which 14 were waited for; matrix products, arithmetic and copies ran while one was open for 0% of the time, Pallas kernels for 2%

profile of v6, /device:TPU:0, one launch (start us, length us, event | category | flops | bytes accessed | tf_op | source)
XLA Modules:
  0.0 49.8 jit_solution(12939306670644891650)
XLA Ops:
  0.6 2.2 %pick.1 = (bf16[24,3072]{1,0:T(8,128)(2,1)}, bf16[48,1536]{1,0:T(8,128)(2,1)}) custom-call(s32[1]{0:T(128)} %bitcast.mine_ref, s32[4,64]{1,0:T(4,128)} %bitcast.10, bf16[64,3072]{1,0:T(8,128)(2,1)} %tok_hbm.1, bf16[64,3072]{1,0:T(8,128)(2,1)} %cot_hbm.1), custom_call_target="tpu_custom_call" | custom-call | flops 37748736 | bytes 1082372 | tf_op jit(solution)/shard_map/pick/pallas_call | solution.py:28
  2.9 0.0 copy-start.3
  2.9 4.1 %collective-permute-start.3 = (bf16[48,1536]{1,0:T(8,128)(2,1)}, bf16[48,1536]{1,0:T(8,128)(2,1)S(1)}, u32[]{:S(2)}, u32[]{:S(2)}) collective-permute-start(bf16[48,1536]{1,0:T(8,128)(2,1)} %get-tuple-element.47), channel_id=1, source_target_pairs={{0,8},{1,9},{2,10},{3,11},{4,12},{5,13},{6,14},{7,15},{8,0},{9,1},... | collective-permute-start | bytes 442376 | tf_op jit(solution)/shard_map/ppermute | solution.py:289
  7.0 2.6 %collective-permute-start = (bf16[24,3072]{1,0:T(8,128)(2,1)S(1)}, bf16[24,3072]{1,0:T(8,128)(2,1)S(1)}, u32[]{:S(2)}, u32[]{:S(2)}) collective-permute-start(bf16[24,3072]{1,0:T(8,128)(2,1)S(1)} %copy-done.3), channel_id=1, source_target_pairs={{0,6},{1,7},{2,4},{3,5},{4,2},{5,3},{6,0},{7,1},{8,14},{9,15},{10,... | collective-permute-start | bytes 442376 | tf_op jit(solution)/shard_map/ppermute | solution.py:289
  9.6 0.5 %collective-permute-start.1 = (bf16[24,3072]{1,0:T(8,128)(2,1)S(1)}, bf16[24,3072]{1,0:T(8,128)(2,1)S(1)}, u32[]{:S(2)}, u32[]{:S(2)}) collective-permute-start(bf16[24,3072]{1,0:T(8,128)(2,1)S(1)} %copy-done.3), channel_id=1, source_target_pairs={{0,2},{1,3},{2,0},{3,1},{4,6},{5,7},{6,4},{7,5},{8,10},{9,11},{10,... | collective-permute-start | bytes 442376 | tf_op jit(solution)/shard_map/ppermute | solution.py:289
  10.1 0.4 collective-permute-start.2
  10.5 3.7 %collective-permute-done.3.refs_8_ = bf16[48,1536]{1,0:T(8,128)(2,1)S(1)} collective-permute-done((bf16[48,1536]{1,0:T(8,128)(2,1)}, bf16[48,1536]{1,0:T(8,128)(2,1)S(1)}, u32[]{:S(2)}, u32[]{:S(2)}) %collective-permute-start.3) | collective-permute-done | bytes 147488 | tf_op jit(solution)/shard_map/ppermute | solution.py:289
  14.3 1.6 %collective-permute-start.10 = (bf16[48,1536]{1,0:T(8,128)(2,1)S(1)}, bf16[48,1536]{1,0:T(8,128)(2,1)S(1)}, u32[]{:S(2)}, u32[]{:S(2)}) collective-permute-start(bf16[48,1536]{1,0:T(8,128)(2,1)S(1)} %collective-permute-done.3.refs_8_), channel_id=1, source_target_pairs={{0,2},{1,3},{2,0},{3,1},{4,6},{5,7},{6,4},{7,5},{8,10},{9,11},{10,... | collective-permute-start | bytes 442376 | tf_op jit(solution)/shard_map/ppermute | solution.py:289
  15.9 0.7 %collective-permute-start.8 = (bf16[48,1536]{1,0:T(8,128)(2,1)S(1)}, bf16[48,1536]{1,0:T(8,128)(2,1)S(1)}, u32[]{:S(2)}, u32[]{:S(2)}) collective-permute-start(bf16[48,1536]{1,0:T(8,128)(2,1)S(1)} %collective-permute-done.3.refs_8_), channel_id=1, source_target_pairs={{0,6},{1,7},{2,4},{3,5},{4,2},{5,3},{6,0},{7,1},{8,14},{9,15},{10,... | collective-permute-start | bytes 442376 | tf_op jit(solution)/shard_map/ppermute | solution.py:289
  16.5 0.0 collective-permute-done.refs_1_
  16.5 1.6 %collective-permute-start.9 = (bf16[48,1536]{1,0:T(8,128)(2,1)S(1)}, bf16[48,1536]{1,0:T(8,128)(2,1)S(1)}, u32[]{:S(2)}, u32[]{:S(2)}) collective-permute-start(bf16[48,1536]{1,0:T(8,128)(2,1)S(1)} %collective-permute-done.3.refs_8_), channel_id=1, source_target_pairs={{0,4},{1,5},{2,6},{3,7},{4,0},{5,1},{6,2},{7,3},{8,12},{9,13},{10,... | collective-permute-start | bytes 442376 | tf_op jit(solution)/shard_map/ppermute | solution.py:289
  18.1 0.0 collective-permute-done.1.refs_3_
  18.1 0.0 collective-permute-start.4
  18.1 1.5 %collective-permute-done.2.refs_2_ = bf16[24,3072]{1,0:T(8,128)(2,1)S(1)} collective-permute-done((bf16[24,3072]{1,0:T(8,128)(2,1)S(1)}, bf16[24,3072]{1,0:T(8,128)(2,1)S(1)}, u32[]{:S(2)}, u32[]{:S(2)}) %collective-permute-start.2) | collective-permute-done | bytes 147488 | tf_op jit(solution)/shard_map/ppermute | solution.py:289
  19.6 2.3 %collective-permute-done.10.refs_11_ = bf16[48,1536]{1,0:T(8,128)(2,1)S(1)} collective-permute-done((bf16[48,1536]{1,0:T(8,128)(2,1)S(1)}, bf16[48,1536]{1,0:T(8,128)(2,1)S(1)}, u32[]{:S(2)}, u32[]{:S(2)}) %collective-permute-start.10) | collective-permute-done | bytes 147488 | tf_op jit(solution)/shard_map/ppermute | solution.py:289
  21.9 1.3 %collective-permute-done.8.refs_9_ = bf16[48,1536]{1,0:T(8,128)(2,1)S(1)} collective-permute-done((bf16[48,1536]{1,0:T(8,128)(2,1)S(1)}, bf16[48,1536]{1,0:T(8,128)(2,1)S(1)}, u32[]{:S(2)}, u32[]{:S(2)}) %collective-permute-start.8) | collective-permute-done | bytes 147488 | tf_op jit(solution)/shard_map/ppermute | solution.py:289
  23.2 1.5 %collective-permute-done.9.refs_10_ = bf16[48,1536]{1,0:T(8,128)(2,1)S(1)} collective-permute-done((bf16[48,1536]{1,0:T(8,128)(2,1)S(1)}, bf16[48,1536]{1,0:T(8,128)(2,1)S(1)}, u32[]{:S(2)}, u32[]{:S(2)}) %collective-permute-start.9) | collective-permute-done | bytes 147488 | tf_op jit(solution)/shard_map/ppermute | solution.py:289
  24.8 0.5 %collective-permute-start.12 = (bf16[48,1536]{1,0:T(8,128)(2,1)S(1)}, bf16[48,1536]{1,0:T(8,128)(2,1)S(1)}, u32[]{:S(2)}, u32[]{:S(2)}) collective-permute-start(bf16[48,1536]{1,0:T(8,128)(2,1)S(1)} %collective-permute-done.8.refs_9_), channel_id=1, source_target_pairs={{0,1},{1,0},{2,3},{3,2},{4,5},{5,4},{6,7},{7,6},{8,9},{9,8},{10,11... | collective-permute-start | bytes 442376 | tf_op jit(solution)/shard_map/ppermute | solution.py:289
  25.3 0.1 collective-permute-start.13
  25.4 0.4 collective-permute-start.14
  25.8 0.3 collective-permute-done.7.refs_7_
  26.2 0.2 collective-permute-done.12.refs_13_
  26.4 0.3 collective-permute-done.13.refs_14_
  26.7 0.2 collective-permute-done.14.refs_15_
  26.9 2.6 %forward.1 = (f32[672,256]{1,0:T(8,128)S(1)}, f32[672,256]{1,0:T(8,128)S(1)}, bf16[672,256]{1,0:T(8,128)(2,1)S(1)}) custom-call(bf16[24,3072]{1,0:T(8,128)(2,1)S(1)} %copy-done.3, bf16[24,3072]{1,0:T(8,128)(2,1)S(1)} %collective-permute-done.refs_1_, bf16[24,3072]{1,0:T(8,128)(2,1)S(1)} %collective-permute-done.2.refs_2_, ...), custom_call_target="tpu_custom_call" | custom-call | flops 2113929216 | bytes 12341248 | tf_op jit(solution)/shard_map/forward/pallas_call | solution.py:28
  29.5 0.0 copy-start.4
  29.5 0.0 copy-start.5
  29.6 4.1 %backward.1 = (bf16[96,1664]{1,0:T(8,128)(2,1)S(1)}, bf16[96,1664]{1,0:T(8,128)(2,1)S(1)}, bf16[96,1664]{1,0:T(8,128)(2,1)S(1)}, bf16[96,1664]{1,0:T(8,128)(2,1)S(1)}) custom-call(bf16[24,3072]{1,0:T(8,128)(2,1)S(1)} %copy-done.3, bf16[24,3072]{1,0:T(8,128)(2,1)S(1)} %collective-permute-done.refs_1_, bf16[24,3072]{1,0:T(8,128)(2,1)S(1)} %collective-permute-done.2.refs_2_, ...), custom_call_target="tpu_custom_call" | custom-call | flops 3170893824 | bytes 17743872 | tf_op jit(solution)/shard_map/backward/pallas_call | solution.py:28
  33.7 0.4 collective-permute-start.19
  34.0 0.2 collective-permute-start.15
  34.3 1.1 %collective-permute-done.19.got_ref = bf16[96,1664]{1,0:T(8,128)(2,1)S(1)} collective-permute-done((bf16[96,1664]{1,0:T(8,128)(2,1)S(1)}, bf16[96,1664]{1,0:T(8,128)(2,1)S(1)}, u32[]{:S(2)}, u32[]{:S(2)}) %collective-permute-start.19) | collective-permute-done | bytes 319520 | tf_op jit(solution)/shard_map/ppermute | solution.py:289
  35.4 0.2 chip.3
  35.5 1.7 %collective-permute-start.20 = (bf16[24,1664]{1,0:T(8,128)(2,1)S(1)}, bf16[24,1664]{1,0:T(8,128)(2,1)S(1)}, u32[]{:S(2)}, u32[]{:S(2)}) collective-permute-start(bf16[24,1664]{1,0:T(8,128)(2,1)S(1)} %get-tuple-element.73), channel_id=1, source_target_pairs={{0,6},{1,7},{2,4},{3,5},{4,2},{5,3},{6,0},{7,1},{8,14},{9,15},{10,... | collective-permute-start | bytes 239624 | tf_op jit(solution)/shard_map/ppermute | solution.py:289
  37.3 0.4 collective-permute-start.21
  37.6 1.4 %collective-permute-start.22 = (bf16[24,1664]{1,0:T(8,128)(2,1)S(1)}, bf16[24,1664]{1,0:T(8,128)(2,1)S(1)}, u32[]{:S(2)}, u32[]{:S(2)}) collective-permute-start(bf16[24,1664]{1,0:T(8,128)(2,1)S(1)} %get-tuple-element.75), channel_id=1, source_target_pairs={{0,2},{1,3},{2,0},{3,1},{4,6},{5,7},{6,4},{7,5},{8,10},{9,11},{10,... | collective-permute-start | bytes 239624 | tf_op jit(solution)/shard_map/ppermute | solution.py:289
  39.1 0.2 chip.2
  39.2 1.7 %collective-permute-start.16 = (bf16[24,1664]{1,0:T(8,128)(2,1)S(1)}, bf16[24,1664]{1,0:T(8,128)(2,1)S(1)}, u32[]{:S(2)}, u32[]{:S(2)}) collective-permute-start(bf16[24,1664]{1,0:T(8,128)(2,1)S(1)} %get-tuple-element.65), channel_id=1, source_target_pairs={{0,6},{1,7},{2,4},{3,5},{4,2},{5,3},{6,0},{7,1},{8,14},{9,15},{10,... | collective-permute-start | bytes 239624 | tf_op jit(solution)/shard_map/ppermute | solution.py:289
  41.0 0.4 collective-permute-start.17
  41.4 0.3 collective-permute-done.20.refs_1_
  41.7 1.1 %collective-permute-start.18 = (bf16[24,1664]{1,0:T(8,128)(2,1)S(1)}, bf16[24,1664]{1,0:T(8,128)(2,1)S(1)}, u32[]{:S(2)}, u32[]{:S(2)}) collective-permute-start(bf16[24,1664]{1,0:T(8,128)(2,1)S(1)} %get-tuple-element.67), channel_id=1, source_target_pairs={{0,2},{1,3},{2,0},{3,1},{4,6},{5,7},{6,4},{7,5},{8,10},{9,11},{10,... | collective-permute-start | bytes 239624 | tf_op jit(solution)/shard_map/ppermute | solution.py:289
  42.8 0.5 collective-permute-done.22.refs_3_
  43.3 0.2 other.1
  43.4 2.1 %collective-permute-start.23 = (bf16[24,1664]{1,0:T(8,128)(2,1)S(1)}, bf16[24,1664]{1,0:T(8,128)(2,1)S(1)}, u32[]{:S(2)}, u32[]{:S(2)}) collective-permute-start(bf16[24,1664]{1,0:T(8,128)(2,1)S(1)} %other.1), channel_id=1, source_target_pairs={{0,8},{1,9},{2,10},{3,11},{4,12},{5,13},{6,14},{7,15},{8,0},{9,1},... | collective-permute-start | bytes 239624 | tf_op jit(solution)/shard_map/ppermute | solution.py:289
  45.6 0.2 layout.1
  45.8 0.4 collective-permute-done.18.refs_3_
  46.2 0.3 own.1
  46.5 2.4 %collective-permute-done.23.back_ref = bf16[24,1664]{1,0:T(8,128)(2,1)S(1)} collective-permute-done((bf16[24,1664]{1,0:T(8,128)(2,1)S(1)}, bf16[24,1664]{1,0:T(8,128)(2,1)S(1)}, u32[]{:S(2)}, u32[]{:S(2)}) %collective-permute-start.23) | collective-permute-done | bytes 79904 | tf_op jit(solution)/shard_map/ppermute | solution.py:289
  48.9 1.0 %final.1 = (bf16[64,3072]{1,0:T(8,128)(2,1)}, f32[4,64]{1,0:T(4,128)}) custom-call(s32[1]{0:T(128)} %bitcast.mine_ref, s32[4,64]{1,0:T(4,128)S(1)} %bitcast.12, f32[48,64]{1,0:T(8,128)S(1)} %get-tuple-element.40.place_ref, bf16[64,128]{1,0:T(8,128)(2,1)S(1)} %get-tuple-element.41.left_ref, bf16[64,128]{1,0:T(8,128)(2,1)S(1)} %get-tuple-element.42.right_ref, ...), custom_call_target="tpu_custom_call" | custom-call | bytes 1318916 | tf_op jit(solution)/shard_map/final/pallas_call | solution.py:28
  (23 shorter events, 0.1 us)
Async XLA Ops:
  2.9 4.1 %copy-start.3 = (bf16[24,3072]{1,0:T(8,128)(2,1)S(1)}, bf16[24,3072]{1,0:T(8,128)(2,1)}, u32[]{:S(2)}) copy-start(bf16[24,3072]{1,0:T(8,128)(2,1)} %get-tuple-element.46.refs_0_) | copy-start | bytes 442372
  2.9 11.4 %collective-permute-start.3 = (bf16[48,1536]{1,0:T(8,128)(2,1)}, bf16[48,1536]{1,0:T(8,128)(2,1)S(1)}, u32[]{:S(2)}, u32[]{:S(2)}) collective-permute-start(bf16[48,1536]{1,0:T(8,128)(2,1)} %get-tuple-element.47), channel_id=1, source_target_pairs={{0,8},{1,9},{2,10},{3,11},{4,12},{5,13},{6,14},{7,15},{8,0},{9,1},... | collective-permute-start | bytes 442376 | tf_op jit(solution)/shard_map/ppermute | solution.py:289
  7.0 19.9 %copy-start = (bf16[3072,672]{0,1:T(8,128)(2,1)S(1)}, bf16[3072,672]{0,1:T(8,128)(2,1)}, u32[]{:S(2)}) copy-start(bf16[3072,672]{0,1:T(8,128)(2,1)} %param.11) | copy-start | bytes 12386308
  7.0 19.9 %copy-start.1 = (bf16[3072,672]{0,1:T(8,128)(2,1)S(1)}, bf16[3072,672]{0,1:T(8,128)(2,1)}, u32[]{:S(2)}) copy-start(bf16[3072,672]{0,1:T(8,128)(2,1)} %param.12) | copy-start | bytes 12386308
  7.0 9.5 %collective-permute-start = (bf16[24,3072]{1,0:T(8,128)(2,1)S(1)}, bf16[24,3072]{1,0:T(8,128)(2,1)S(1)}, u32[]{:S(2)}, u32[]{:S(2)}) collective-permute-start(bf16[24,3072]{1,0:T(8,128)(2,1)S(1)} %copy-done.3), channel_id=1, source_target_pairs={{0,6},{1,7},{2,4},{3,5},{4,2},{5,3},{6,0},{7,1},{8,14},{9,15},{10,... | collective-permute-start | bytes 442376 | tf_op jit(solution)/shard_map/ppermute | solution.py:289
  9.6 8.5 %collective-permute-start.1 = (bf16[24,3072]{1,0:T(8,128)(2,1)S(1)}, bf16[24,3072]{1,0:T(8,128)(2,1)S(1)}, u32[]{:S(2)}, u32[]{:S(2)}) collective-permute-start(bf16[24,3072]{1,0:T(8,128)(2,1)S(1)} %copy-done.3), channel_id=1, source_target_pairs={{0,2},{1,3},{2,0},{3,1},{4,6},{5,7},{6,4},{7,5},{8,10},{9,11},{10,... | collective-permute-start | bytes 442376 | tf_op jit(solution)/shard_map/ppermute | solution.py:289
  10.1 9.5 %collective-permute-start.2 = (bf16[24,3072]{1,0:T(8,128)(2,1)S(1)}, bf16[24,3072]{1,0:T(8,128)(2,1)S(1)}, u32[]{:S(2)}, u32[]{:S(2)}) collective-permute-start(bf16[24,3072]{1,0:T(8,128)(2,1)S(1)} %copy-done.3), channel_id=1, source_target_pairs={{0,4},{1,5},{2,6},{3,7},{4,0},{5,1},{6,2},{7,3},{8,12},{9,13},{10,... | collective-permute-start | bytes 442376 | tf_op jit(solution)/shard_map/ppermute | solution.py:289
  14.3 7.6 %collective-permute-start.10 = (bf16[48,1536]{1,0:T(8,128)(2,1)S(1)}, bf16[48,1536]{1,0:T(8,128)(2,1)S(1)}, u32[]{:S(2)}, u32[]{:S(2)}) collective-permute-start(bf16[48,1536]{1,0:T(8,128)(2,1)S(1)} %collective-permute-done.3.refs_8_), channel_id=1, source_target_pairs={{0,2},{1,3},{2,0},{3,1},{4,6},{5,7},{6,4},{7,5},{8,10},{9,11},{10,... | collective-permute-start | bytes 442376 | tf_op jit(solution)/shard_map/ppermute | solution.py:289
  15.9 7.4 %collective-permute-start.8 = (bf16[48,1536]{1,0:T(8,128)(2,1)S(1)}, bf16[48,1536]{1,0:T(8,128)(2,1)S(1)}, u32[]{:S(2)}, u32[]{:S(2)}) collective-permute-start(bf16[48,1536]{1,0:T(8,128)(2,1)S(1)} %collective-permute-done.3.refs_8_), channel_id=1, source_target_pairs={{0,6},{1,7},{2,4},{3,5},{4,2},{5,3},{6,0},{7,1},{8,14},{9,15},{10,... | collective-permute-start | bytes 442376 | tf_op jit(solution)/shard_map/ppermute | solution.py:289
  16.5 8.3 %collective-permute-start.9 = (bf16[48,1536]{1,0:T(8,128)(2,1)S(1)}, bf16[48,1536]{1,0:T(8,128)(2,1)S(1)}, u32[]{:S(2)}, u32[]{:S(2)}) collective-permute-start(bf16[48,1536]{1,0:T(8,128)(2,1)S(1)} %collective-permute-done.3.refs_8_), channel_id=1, source_target_pairs={{0,4},{1,5},{2,6},{3,7},{4,0},{5,1},{6,2},{7,3},{8,12},{9,13},{10,... | collective-permute-start | bytes 442376 | tf_op jit(solution)/shard_map/ppermute | solution.py:289
  18.1 6.7 %collective-permute-start.4 = (bf16[24,3072]{1,0:T(8,128)(2,1)S(1)}, bf16[24,3072]{1,0:T(8,128)(2,1)S(1)}, u32[]{:S(2)}, u32[]{:S(2)}) collective-permute-start(bf16[24,3072]{1,0:T(8,128)(2,1)S(1)} %copy-done.3), channel_id=1, source_target_pairs={{0,1},{1,0},{2,3},{3,2},{4,5},{5,4},{6,7},{7,6},{8,9},{9,8},{10,11... | collective-permute-start | bytes 442376 | tf_op jit(solution)/shard_map/ppermute | solution.py:289
  19.6 5.7 %collective-permute-start.5 = (bf16[24,3072]{1,0:T(8,128)(2,1)S(1)}, bf16[24,3072]{1,0:T(8,128)(2,1)S(1)}, u32[]{:S(2)}, u32[]{:S(2)}) collective-permute-start(bf16[24,3072]{1,0:T(8,128)(2,1)S(1)} %collective-permute-done.refs_1_), channel_id=1, source_target_pairs={{0,1},{1,0},{2,3},{3,2},{4,5},{5,4},{6,7},{7,6},{8,9},{9,8},{10,11... | collective-permute-start | bytes 442376 | tf_op jit(solution)/shard_map/ppermute | solution.py:289
  21.9 3.5 %collective-permute-start.6 = (bf16[24,3072]{1,0:T(8,128)(2,1)S(1)}, bf16[24,3072]{1,0:T(8,128)(2,1)S(1)}, u32[]{:S(2)}, u32[]{:S(2)}) collective-permute-start(bf16[24,3072]{1,0:T(8,128)(2,1)S(1)} %collective-permute-done.2.refs_2_), channel_id=1, source_target_pairs={{0,1},{1,0},{2,3},{3,2},{4,5},{5,4},{6,7},{7,6},{8,9},{9,8},{10,11... | collective-permute-start | bytes 442376 | tf_op jit(solution)/shard_map/ppermute | solution.py:289
  23.2 2.9 %collective-permute-start.11 = (bf16[48,1536]{1,0:T(8,128)(2,1)S(1)}, bf16[48,1536]{1,0:T(8,128)(2,1)S(1)}, u32[]{:S(2)}, u32[]{:S(2)}) collective-permute-start(bf16[48,1536]{1,0:T(8,128)(2,1)S(1)} %collective-permute-done.3.refs_8_), channel_id=1, source_target_pairs={{0,1},{1,0},{2,3},{3,2},{4,5},{5,4},{6,7},{7,6},{8,9},{9,8},{10,11... | collective-permute-start | bytes 442376 | tf_op jit(solution)/shard_map/ppermute | solution.py:289
  24.8 1.4 %collective-permute-start.7 = (bf16[24,3072]{1,0:T(8,128)(2,1)S(1)}, bf16[24,3072]{1,0:T(8,128)(2,1)S(1)}, u32[]{:S(2)}, u32[]{:S(2)}) collective-permute-start(bf16[24,3072]{1,0:T(8,128)(2,1)S(1)} %collective-permute-done.1.refs_3_), channel_id=1, source_target_pairs={{0,1},{1,0},{2,3},{3,2},{4,5},{5,4},{6,7},{7,6},{8,9},{9,8},{10,11... | collective-permute-start | bytes 442376 | tf_op jit(solution)/shard_map/ppermute | solution.py:289
  24.8 1.6 %collective-permute-start.12 = (bf16[48,1536]{1,0:T(8,128)(2,1)S(1)}, bf16[48,1536]{1,0:T(8,128)(2,1)S(1)}, u32[]{:S(2)}, u32[]{:S(2)}) collective-permute-start(bf16[48,1536]{1,0:T(8,128)(2,1)S(1)} %collective-permute-done.8.refs_9_), channel_id=1, source_target_pairs={{0,1},{1,0},{2,3},{3,2},{4,5},{5,4},{6,7},{7,6},{8,9},{9,8},{10,11... | collective-permute-start | bytes 442376 | tf_op jit(solution)/shard_map/ppermute | solution.py:289
  25.3 1.4 %collective-permute-start.13 = (bf16[48,1536]{1,0:T(8,128)(2,1)S(1)}, bf16[48,1536]{1,0:T(8,128)(2,1)S(1)}, u32[]{:S(2)}, u32[]{:S(2)}) collective-permute-start(bf16[48,1536]{1,0:T(8,128)(2,1)S(1)} %collective-permute-done.9.refs_10_), channel_id=1, source_target_pairs={{0,1},{1,0},{2,3},{3,2},{4,5},{5,4},{6,7},{7,6},{8,9},{9,8},{10,11... | collective-permute-start | bytes 442376 | tf_op jit(solution)/shard_map/ppermute | solution.py:289
  25.4 1.5 %collective-permute-start.14 = (bf16[48,1536]{1,0:T(8,128)(2,1)S(1)}, bf16[48,1536]{1,0:T(8,128)(2,1)S(1)}, u32[]{:S(2)}, u32[]{:S(2)}) collective-permute-start(bf16[48,1536]{1,0:T(8,128)(2,1)S(1)} %collective-permute-done.10.refs_11_), channel_id=1, source_target_pairs={{0,1},{1,0},{2,3},{3,2},{4,5},{5,4},{6,7},{7,6},{8,9},{9,8},{10,11... | collective-permute-start | bytes 442376 | tf_op jit(solution)/shard_map/ppermute | solution.py:289
  26.9 2.6 %copy-start.2 = (bf16[672,3072]{1,0:T(8,128)(2,1)S(1)}, bf16[672,3072]{1,0:T(8,128)(2,1)}, u32[]{:S(2)}) copy-start(bf16[672,3072]{1,0:T(8,128)(2,1)} %refs_21_.1) | copy-start | bytes 12386308
  29.5 16.1 %copy-start.4 = (s32[64,4]{0,1:T(4,128)S(1)}, s32[64,4]{0,1:T(4,128)}, u32[]{:S(2)}) copy-start(s32[64,4]{0,1:T(4,128)} %param.10) | copy-start | bytes 3076
  29.5 16.0 %copy-start.5 = (f32[64,4]{0,1:T(4,128)S(1)}, f32[64,4]{0,1:T(4,128)}, u32[]{:S(2)}) copy-start(f32[64,4]{0,1:T(4,128)} %param.9) | copy-start | bytes 3076
  33.7 1.7 %collective-permute-start.19 = (bf16[96,1664]{1,0:T(8,128)(2,1)S(1)}, bf16[96,1664]{1,0:T(8,128)(2,1)S(1)}, u32[]{:S(2)}, u32[]{:S(2)}) collective-permute-start(bf16[96,1664]{1,0:T(8,128)(2,1)S(1)} %get-tuple-element.71), channel_id=1, source_target_pairs={{0,1},{1,0},{2,3},{3,2},{4,5},{5,4},{6,7},{7,6},{8,9},{9,8},{10,11... | collective-permute-start | bytes 958472 | tf_op jit(solution)/shard_map/ppermute | solution.py:289
  34.0 5.0 %collective-permute-start.15 = (bf16[96,1664]{1,0:T(8,128)(2,1)S(1)}, bf16[96,1664]{1,0:T(8,128)(2,1)S(1)}, u32[]{:S(2)}, u32[]{:S(2)}) collective-permute-start(bf16[96,1664]{1,0:T(8,128)(2,1)S(1)} %get-tuple-element.63), channel_id=1, source_target_pairs={{0,1},{1,0},{2,3},{3,2},{4,5},{5,4},{6,7},{7,6},{8,9},{9,8},{10,11... | collective-permute-start | bytes 958472 | tf_op jit(solution)/shard_map/ppermute | solution.py:289
  35.5 6.2 %collective-permute-start.20 = (bf16[24,1664]{1,0:T(8,128)(2,1)S(1)}, bf16[24,1664]{1,0:T(8,128)(2,1)S(1)}, u32[]{:S(2)}, u32[]{:S(2)}) collective-permute-start(bf16[24,1664]{1,0:T(8,128)(2,1)S(1)} %get-tuple-element.73), channel_id=1, source_target_pairs={{0,6},{1,7},{2,4},{3,5},{4,2},{5,3},{6,0},{7,1},{8,14},{9,15},{10,... | collective-permute-start | bytes 239624 | tf_op jit(solution)/shard_map/ppermute | solution.py:289
  37.3 5.6 %collective-permute-start.21 = (bf16[24,1664]{1,0:T(8,128)(2,1)S(1)}, bf16[24,1664]{1,0:T(8,128)(2,1)S(1)}, u32[]{:S(2)}, u32[]{:S(2)}) collective-permute-start(bf16[24,1664]{1,0:T(8,128)(2,1)S(1)} %get-tuple-element.74), channel_id=1, source_target_pairs={{0,4},{1,5},{2,6},{3,7},{4,0},{5,1},{6,2},{7,3},{8,12},{9,13},{10,... | collective-permute-start | bytes 239624 | tf_op jit(solution)/shard_map/ppermute | solution.py:289
  37.6 5.6 %collective-permute-start.22 = (bf16[24,1664]{1,0:T(8,128)(2,1)S(1)}, bf16[24,1664]{1,0:T(8,128)(2,1)S(1)}, u32[]{:S(2)}, u32[]{:S(2)}) collective-permute-start(bf16[24,1664]{1,0:T(8,128)(2,1)S(1)} %get-tuple-element.75), channel_id=1, source_target_pairs={{0,2},{1,3},{2,0},{3,1},{4,6},{5,7},{6,4},{7,5},{8,10},{9,11},{10,... | collective-permute-start | bytes 239624 | tf_op jit(solution)/shard_map/ppermute | solution.py:289
  39.2 6.6 %collective-permute-start.16 = (bf16[24,1664]{1,0:T(8,128)(2,1)S(1)}, bf16[24,1664]{1,0:T(8,128)(2,1)S(1)}, u32[]{:S(2)}, u32[]{:S(2)}) collective-permute-start(bf16[24,1664]{1,0:T(8,128)(2,1)S(1)} %get-tuple-element.65), channel_id=1, source_target_pairs={{0,6},{1,7},{2,4},{3,5},{4,2},{5,3},{6,0},{7,1},{8,14},{9,15},{10,... | collective-permute-start | bytes 239624 | tf_op jit(solution)/shard_map/ppermute | solution.py:289
  41.0 4.9 %collective-permute-start.17 = (bf16[24,1664]{1,0:T(8,128)(2,1)S(1)}, bf16[24,1664]{1,0:T(8,128)(2,1)S(1)}, u32[]{:S(2)}, u32[]{:S(2)}) collective-permute-start(bf16[24,1664]{1,0:T(8,128)(2,1)S(1)} %get-tuple-element.66), channel_id=1, source_target_pairs={{0,4},{1,5},{2,6},{3,7},{4,0},{5,1},{6,2},{7,3},{8,12},{9,13},{10,... | collective-permute-start | bytes 239624 | tf_op jit(solution)/shard_map/ppermute | solution.py:289
  41.7 4.5 %collective-permute-start.18 = (bf16[24,1664]{1,0:T(8,128)(2,1)S(1)}, bf16[24,1664]{1,0:T(8,128)(2,1)S(1)}, u32[]{:S(2)}, u32[]{:S(2)}) collective-permute-start(bf16[24,1664]{1,0:T(8,128)(2,1)S(1)} %get-tuple-element.67), channel_id=1, source_target_pairs={{0,2},{1,3},{2,0},{3,1},{4,6},{5,7},{6,4},{7,5},{8,10},{9,11},{10,... | collective-permute-start | bytes 239624 | tf_op jit(solution)/shard_map/ppermute | solution.py:289
  43.4 5.4 %collective-permute-start.23 = (bf16[24,1664]{1,0:T(8,128)(2,1)S(1)}, bf16[24,1664]{1,0:T(8,128)(2,1)S(1)}, u32[]{:S(2)}, u32[]{:S(2)}) collective-permute-start(bf16[24,1664]{1,0:T(8,128)(2,1)S(1)} %other.1), channel_id=1, source_target_pairs={{0,8},{1,9},{2,10},{3,11},{4,12},{5,13},{6,14},{7,15},{8,0},{9,1},... | collective-permute-start | bytes 239624 | tf_op jit(solution)/shard_map/ppermute | solution.py:289
